TPU v7x, 32 devices: a whole 2x2x4 slice. The times are simulated.
32 devices in a mesh: tm: 2 (over x), sy: 4 (over z), sx: 4 (over y, core).
Axes of the slice: x: 2, y: 2, z: 4, core: 2. Of those that a mesh axis runs over, the one named last changes fastest.
Arguments:
- latent_init: float32 [64, 96, 320], P('sy', 'sx'), may hold values from -80 to 80
- step_noise: bfloat16 [8, 64, 96, 320], P('tm', 'sy', 'sx'), may hold values from -6 to 6
- coef_state: float32 [8], P('tm'), may hold values from -0.06 to -0.01
- coef_drift: float32 [8], P('tm'), may hold values from -0.1 to 0.1
- coef_noise: float32 [8], P('tm'), may hold values from 0.05 to 0.2
- step_index: int32 [8], P('tm'), may hold values from 0 to 999
- time_table: float32 [1000, 320], replicated, may hold values from -1.5 to 1.5
- norm_gain: float32 [320], replicated, may hold values from 0.25 to 1.75
- conv_weight: bfloat16 [3, 3, 320, 320], replicated, may hold values from -0.109375 to 0.109375
- reward_grad: float32 [64, 96, 320], P('sy', 'sx'), may hold values from -0.18 to 0.18
Outputs:
- trajectory: float32 [8, 64, 96, 320], P('tm', 'sy', 'sx')
- grad_weight: float32 [3, 3, 320, 320], P(None, None, None, 'tm')
All inputs are finite; a program needn't handle non-finite values.
Results may differ from a plain program's by a relative error of at most 0.0009.
The roundings to bfloat16 on the way count: a program that leaves them out, or rounds other values in their place, can miss the bound.
Values may be sent and summed in bfloat16 or wider, within the bound.
No kernel may reach another device: no remote copies, remote signals or barrier semaphores. Data moves between devices by JAX's collectives and lax.ppermute only.
A program may use at most 128 MiB of HBM per device.

v0:
```python
import jax
import jax.numpy as jnp
from jax import lax
from jax.sharding import PartitionSpec as P

GROUPS = 32
ITERS = 2


EPSILON = 1e-05


def prefix(value, axis, join, neutral, backward):
    count, mine = (lax.axis_size(axis), lax.axis_index(axis))
    pieces = lax.all_gather(value, axis)
    if backward:
        pieces = pieces[::-1]
        mine = count - 1 - mine
    subtotal = jnp.full_like(value, 0) + jnp.asarray(neutral, value.dtype)

    def step(position, subtotal):
        longer = join(subtotal, pieces[position])
        return jnp.where(position < mine, longer, subtotal)

    return lax.fori_loop(0, count - 1, step, subtotal)


def with_halo(block, sides, width):
    for axis, dim in sides:
        count = lax.axis_size(axis)
        forward = [(i, i + 1) for i in range(count - 1)]
        backward = [(target, source) for source, target in forward]
        low = lax.ppermute(
            lax.slice_in_dim(block, block.shape[dim] - width, None, axis=dim), axis, forward
        )
        high = lax.ppermute(lax.slice_in_dim(block, 0, width, axis=dim), axis, backward)
        block = jnp.concatenate([low, block, high], axis=dim)
    return block


def add_terms(earlier, later):
    return earlier + later


def lower_total(block_total, reverse):
    return prefix(block_total, "tm", add_terms, jnp.zeros_like(block_total), reverse)


def group_count(tile_rows, tile_cols, channels):
    return tile_rows * lax.axis_size("sy") * tile_cols * lax.axis_size("sx") * (channels // GROUPS)


def group_stats(grouped, cell_count):
    totals = lax.psum(jnp.sum(grouped, axis=(1, 3)), ("sy", "sx"))
    center = totals / cell_count
    shifted = grouped - center[:, None, :, None]
    spread = lax.psum(jnp.sum(shifted * shifted, axis=(1, 3)), ("sy", "sx")) / cell_count
    return (shifted, spread)


def prepare(states, modulate):
    steps_here, tile_rows, tile_cols, channels = states.shape
    grouped = states.reshape(steps_here, tile_rows * tile_cols, GROUPS, channels // GROUPS)
    shifted, spread = group_stats(grouped, group_count(tile_rows, tile_cols, channels))
    inv_std = 1.0 / jnp.sqrt(spread + EPSILON)
    normal_field = (shifted * inv_std[:, None, :, None]).reshape(states.shape)
    pre_act = normal_field * modulate[:, None, None, :]
    activation = jax.nn.silu(pre_act).astype(jnp.bfloat16)
    act_pad = with_halo(activation, (("sy", 1), ("sx", 2)), 1)
    return (normal_field, inv_std, pre_act, act_pad)


def convolve(act_pad, conv_weight, tile_rows, tile_cols):
    result = jnp.zeros(
        act_pad.shape[:1] + (tile_rows, tile_cols, conv_weight.shape[3]), jnp.float32
    )
    for row_off in range(3):
        for col_off in range(3):
            window = act_pad[:, row_off : row_off + tile_rows, col_off : col_off + tile_cols, :]
            result = result + jnp.einsum(
                "bhwc,cd->bhwd",
                window,
                conv_weight[row_off, col_off],
                preferred_element_type=jnp.float32,
            )
    return result


def backprop(upstream, act_cache, modulate, conv_weight, need_state):
    normal_field, inv_std, pre_act, act_pad = act_cache
    steps_here, tile_rows, tile_cols, channels = upstream.shape
    up_half = upstream.astype(jnp.bfloat16)
    weight_rows = []
    for row_off in range(3):
        weight_cols = []
        for col_off in range(3):
            window = act_pad[:, row_off : row_off + tile_rows, col_off : col_off + tile_cols, :]
            weight_cols.append(
                jnp.einsum("bhwc,bhwd->cd", window, up_half, preferred_element_type=jnp.float32)
            )
        weight_rows.append(jnp.stack(weight_cols))
    grad_piece = jnp.stack(weight_rows)
    if not need_state:
        return (upstream, grad_piece)
    up_pad = with_halo(up_half, (("sy", 1), ("sx", 2)), 1)
    d_act = jnp.zeros(upstream.shape, jnp.float32)
    for row_off in range(3):
        for col_off in range(3):
            window = up_pad[
                :, 2 - row_off : 2 - row_off + tile_rows, 2 - col_off : 2 - col_off + tile_cols, :
            ]
            d_act = d_act + jnp.einsum(
                "bhwd,cd->bhwc",
                window,
                conv_weight[row_off, col_off],
                preferred_element_type=jnp.float32,
            )
    sig_value = jax.nn.sigmoid(pre_act)
    d_norm = d_act * sig_value * (1.0 + pre_act * (1.0 - sig_value)) * modulate[:, None, None, :]
    group_shape = (steps_here, tile_rows * tile_cols, GROUPS, channels // GROUPS)
    grouped_d = d_norm.reshape(group_shape)
    grouped_n = normal_field.reshape(group_shape)
    cell_count = group_count(tile_rows, tile_cols, channels)
    plain_sum, cross_sum = lax.psum(
        (jnp.sum(grouped_d, axis=(1, 3)), jnp.sum(grouped_d * grouped_n, axis=(1, 3))), ("sy", "sx")
    )
    plain_mean = plain_sum / cell_count
    cross_mean = cross_sum / cell_count
    d_group = (
        grouped_d - plain_mean[:, None, :, None] - grouped_n * cross_mean[:, None, :, None]
    ) * inv_std[:, None, :, None]
    return (upstream + d_group.reshape(upstream.shape), grad_piece)


def shards(
    latent_init,
    step_noise,
    coef_state,
    coef_drift,
    coef_noise,
    step_index,
    time_table,
    norm_gain,
    conv_weight,
    reward_grad,
):
    tile_rows, tile_cols = (step_noise.shape[1], step_noise.shape[2])
    table_ids = jnp.arange(time_table.shape[0], dtype=jnp.int32)
    one_hot = (step_index[:, None] == table_ids[None, :]).astype(jnp.float32)
    embedded = jnp.dot(one_hot, time_table, precision=lax.Precision.HIGHEST)
    modulate = norm_gain[None, :] * (1.0 + embedded)
    state_c = coef_state[:, None, None, None]
    drift_c = coef_drift[:, None, None, None]
    noise_c = coef_noise[:, None, None, None]
    states = jnp.broadcast_to(latent_init[None], step_noise.shape)
    saved_states = []
    caches = []
    trajectory = states
    for sweep_index in range(ITERS):
        saved_states.append(states)
        act_cache = prepare(states, modulate)
        caches.append(act_cache)
        drift_term = states + convolve(act_cache[3], conv_weight, tile_rows, tile_cols)
        increment = (
            state_c * states + drift_c * drift_term + noise_c * step_noise.astype(jnp.float32)
        )
        running = jnp.cumsum(increment, axis=0)
        offset = lower_total(running[-1], False)
        trajectory = latent_init[None] + (offset[None] + running)
        if sweep_index + 1 < ITERS:
            before = jnp.concatenate([jnp.zeros_like(running[:1]), running[:-1]], axis=0)
            states = latent_init[None] + (offset[None] + before)
    adjoint = jnp.broadcast_to(reward_grad[None], step_noise.shape)
    grad_total = jnp.zeros(conv_weight.shape, jnp.float32)
    for sweep_index in range(ITERS - 1, -1, -1):
        act_cache = prepare(saved_states[sweep_index], modulate)
        upstream = drift_c * adjoint
        d_state, grad_piece = backprop(upstream, act_cache, modulate, conv_weight, sweep_index > 0)
        grad_total = grad_total + grad_piece
        if sweep_index > 0:
            through = state_c * adjoint + d_state
            suffix = jnp.cumsum(through[::-1], axis=0)[::-1]
            higher = lower_total(suffix[0], True)
            after = jnp.concatenate([suffix[1:], jnp.zeros_like(suffix[:1])], axis=0)
            adjoint = higher[None] + after
    share = lax.psum_scatter(grad_total, "tm", scatter_dimension=3, tiled=True)
    grad_weight = lax.psum(share, ("sy", "sx"))
    return (trajectory, grad_weight)


def solution(mesh):
    placed = (
        P("sy", "sx", None),
        P("tm", "sy", "sx", None),
        P("tm"),
        P("tm"),
        P("tm"),
        P("tm"),
        P(),
        P(),
        P(),
        P("sy", "sx", None),
    )
    return jax.shard_map(
        shards,
        mesh=mesh,
        in_specs=placed,
        out_specs=(P("tm", "sy", "sx", None), P(None, None, None, "tm")),
        check_vma=False,
    )
```

profile of v0, /device:TPU:0, one launch (start us, length us, event | category | flops | bytes accessed | tf_op | source)
XLA Modules:
  0.0 535.1 jit_solution(11449198612127689566)
XLA Ops:
  8.7 34.9 %psum.46 = f32[4,32]{1,0:T(4,128)S(1)} all-reduce(f32[4,32]{1,0:T(4,128)S(1)} %reduce_sum.117), channel_id=1, replica_groups=mesh['tm'=2,'sy'=4,'sx'=4] {'sy','sx'}, use_global_device_ids=true, to_apply=%region_2.0 | all-reduce | flops 128 | bytes 1024 | tf_op jit(solution)/shard_map/psum | solution.py:54
  45.4 29.5 %psum.49 = f32[4,32]{1,0:T(4,128)S(1)} all-reduce(f32[4,32]{1,0:T(4,128)S(1)} %reduce_sum.120), channel_id=1, replica_groups=mesh['tm'=2,'sy'=4,'sx'=4] {'sy','sx'}, use_global_device_ids=true, to_apply=%region_5.6 | all-reduce | flops 128 | bytes 1024 | tf_op jit(solution)/shard_map/psum | solution.py:57
  83.3 5.2 collective-permute-start.8
  89.9 3.6 fusion.167
  103.5 4.3 collective-permute-start.11
  107.8 3.4 fusion.147
  138.2 7.3 %fusion.33 = f32[4,16,24,320]{3,2,1,0:T(8,128)S(1)} fusion(bf16[4,16,24,320]{3,2,1,0:T(8,128)(2,1)S(1)} %copy-done.23, f32[4,16,24,320]{3,2,1,0:T(8,128)} %fusion.128, f32[4,16,24,320]{3,2,1,0:T(8,128)S(1)} %copy-done.19, f32[4,16,24,320]{3,2,1,0:T(8,128)} %fusion.131, f32[4,16,24,320]{3,2,1,0:T(8,128)} %fusion.134, f32[4,16,24,320]{3,2,1,0:T(8,128)} %fusion.167, ...), kind=kOutput, calls=%fused_computation.46 | output fusion | flops 8847360 | bytes 21135408 | tf_op jit(solution)/shard_map/jit(cumsum)/reduce_window_sum | solution.py:167
  160.5 16.9 %all_gather.9 = f32[2,16,24,320]{3,2,1,0:T(8,128)S(1)} all-gather(f32[1,16,24,320]{3,2,1,0:T(8,128)S(1)} %slice-done), channel_id=1, replica_groups=mesh['tm'=2,'sy'=4,'sx'=4] {'tm'}, dimensions={0}, use_global_device_ids=true | all-gather | bytes 1474560 | tf_op jit(solution)/shard_map/all_gather | solution.py:15
  177.9 31.0 %psum.50 = f32[4,32]{1,0:T(4,128)S(1)} all-reduce(f32[4,32]{1,0:T(4,128)S(1)} %reduce_sum.123), channel_id=1, replica_groups=mesh['tm'=2,'sy'=4,'sx'=4] {'sy','sx'}, use_global_device_ids=true, to_apply=%region_9.10 | all-reduce | flops 128 | bytes 1024 | tf_op jit(solution)/shard_map/psum | solution.py:54
  209.8 29.5 %psum.51 = f32[4,32]{1,0:T(4,128)S(1)} all-reduce(f32[4,32]{1,0:T(4,128)S(1)} %reduce_sum.126), channel_id=1, replica_groups=mesh['tm'=2,'sy'=4,'sx'=4] {'sy','sx'}, use_global_device_ids=true, to_apply=%region_12.13 | all-reduce | flops 128 | bytes 1024 | tf_op jit(solution)/shard_map/psum | solution.py:57
  239.5 10.9 %fusion.222 = (f32[4,320]{1,0:T(4,128)S(1)}, f32[4,320]{1,0:T(4,128)S(1)}, f32[4,16,24,320]{3,2,1,0:T(8,128)}) fusion(f32[4,320]{1,0:T(4,128)S(1)} %mul.201, f32[4,320]{1,0:T(4,128)S(1)} %sub.66, f32[3,16,24,320]{3,2,1,0:T(8,128)S(1)} %slice.284, f32[16,24,320]{2,1,0:T(8,128)S(1)} %fusion.151, f32[16,24,320]{2,1,0:T(8,128)S(1)} %copy-done.2, ...), kind=kOutput, calls=%fused_computation.278 | convolution fusion | flops 326858240 | bytes 24749056 | tf_op jit(solution)/shard_map/bhwd,cd->bhwc/dot_general | solution.py:112
  250.8 29.5 %all-reduce.2 = (f32[4,32]{1,0:T(4,128)S(1)}, f32[4,32]{1,0:T(4,128)S(1)}) all-reduce(f32[4,32]{1,0:T(4,128)S(1)} %reduce_sum.132, f32[4,32]{1,0:T(4,128)S(1)} %reduce_sum.129), channel_id=1, replica_groups=mesh['tm'=2,'sy'=4,'sx'=4] {'sy','sx'}, use_global_device_ids=true, to_apply=%region_19.20 | all-reduce | flops 256 | bytes 2048 | tf_op jit(solution)/shard_map/psum | solution.py:124
  281.9 4.9 fusion.18
  296.8 16.1 %all_gather.11 = f32[2,16,24,320]{3,2,1,0:T(8,128)S(1)} all-gather(f32[1,16,24,320]{3,2,1,0:T(8,128)} %slice.302), channel_id=1, replica_groups=mesh['tm'=2,'sy'=4,'sx'=4] {'tm'}, dimensions={0}, use_global_device_ids=true | all-gather | bytes 1474560 | tf_op jit(solution)/shard_map/all_gather | solution.py:15
  342.4 8.4 %copy.42 = f32[3,3,320,320]{2,1,0,3:T(4,128)} copy(f32[3,3,320,320]{3,2,1,0:T(8,128)} %maximum_add_fusion) | data formatting | bytes 7372800
  350.8 7.6 %reshape.75 = f32[320,2880]{1,0:T(8,128)} reshape(f32[320,3,3,320]{3,2,1,0:T(4,128)} %bitcast.242) | data formatting | bytes 7372800
  358.8 3.5 fusion.165
  381.7 29.7 %reduce-scatter.4.cloned.1.call-done = f32[160,2880]{1,0:T(8,128)} async-done(((f32[320,2880]{1,0:T(8,128)}), f32[160,2880]{1,0:T(8,128)}) %reduce-scatter.4.cloned.1.call-update) | async-done | bytes 1843216
  411.4 4.5 reshape.76
  415.9 4.8 copy.43
  421.7 8.5 %fusion.19 = f32[4,16,24,320]{3,2,1,0:T(8,128)S(1)} fusion(f32[4,16,24,320]{3,2,1,0:T(8,128)} %fusion.110, f32[4,16,24,320]{3,2,1,0:T(8,128)} %fusion.145, f32[4,16,24,320]{3,2,1,0:T(8,128)} %fusion.113, f32[4,16,24,320]{3,2,1,0:T(8,128)} %fusion.116, f32[4,16,24,320]{3,2,1,0:T(8,128)} %fusion.165, f32[4,16,24,320]{3,2,1,0:T(8,128)} %fusion.119, ...), kind=kOutput, calls=%fused_computation.28 | output fusion | flops 9830400 | bytes 23101488 | tf_op jit(solution)/shard_map/jit(cumsum)/reduce_window_sum | solution.py:167
  430.3 15.7 %all_gather.10 = f32[2,16,24,320]{3,2,1,0:T(8,128)S(1)} all-gather(f32[1,16,24,320]{3,2,1,0:T(8,128)S(1)} %slice.293), channel_id=1, replica_groups=mesh['tm'=2,'sy'=4,'sx'=4] {'tm'}, dimensions={0}, use_global_device_ids=true | all-gather | bytes 1474560 | tf_op jit(solution)/shard_map/all_gather | solution.py:15
  447.8 75.6 %all-reduce.5.cloned.1.call-done = f32[3,3,320,160]{3,2,1,0:T(8,128)} async-done(((f32[3,3,320,160]{3,2,1,0:T(8,128)}), f32[3,3,320,160]{3,2,1,0:T(8,128)}) %all-reduce.5.cloned.1.call-update) | async-done | bytes 1843216 | tf_op jit(solution)/shard_map/psum | solution.py:187
  523.3 4.5 copy.14
  (216 shorter events, 130.2 us)
Async XLA Ops:
  7.2 68.0 %copy-start = (f32[1000,320]{0,1:T(8,128)S(1)}, f32[1000,320]{0,1:T(8,128)}, u32[]{:S(2)}) copy-start(f32[1000,320]{0,1:T(8,128)} %param.16) | copy-start | bytes 3840004
  7.2 69.3 %copy-start.2 = (f32[16,24,320]{2,1,0:T(8,128)S(1)}, f32[16,24,320]{2,1,0:T(8,128)}, u32[]{:S(2)}) copy-start(f32[16,24,320]{2,1,0:T(8,128)} %param.10) | copy-start | bytes 1474564
  7.2 404.2 %reduce-scatter.4.cloned.1.call-start = ((), (), s32[]{:S(2)}) async-start(), calls=%async_computation.2 | async-start | bytes 5652480
  43.7 37.5 %copy-start.33 = (f32[4]{0:T(128)S(1)}, f32[4]{0:T(128)}, u32[]{:S(2)}) copy-start(f32[4]{0:T(128)} %param.13) | copy-start | bytes 52
  43.9 46.0 %copy-start.29 = (f32[4,320]{1,0:T(4,128)}, f32[4,320]{1,0:T(4,128)S(1)}, u32[]{:S(2)}) copy-start(f32[4,320]{1,0:T(4,128)S(1)} %sub.62) | copy-start | bytes 15364
  77.3 43.6 %copy-start.3 = (bf16[4,16,24,320]{3,2,1,0:T(8,128)(2,1)}, bf16[4,16,24,320]{3,2,1,0:T(8,128)(2,1)S(1)}, u32[]{:S(2)}) copy-start(bf16[4,16,24,320]{3,2,1,0:T(8,128)(2,1)S(1)} %fusion.17) | copy-start | bytes 2949124
  78.0 18.8 %collective-permute-start = (bf16[4,1,24,320]{3,2,1,0:T(8,128)(2,1)}, bf16[4,1,24,320]{3,2,1,0:T(8,128)(2,1)}, u32[]{:S(2)}, u32[]{:S(2)}) collective-permute-start(bf16[4,1,24,320]{3,2,1,0:T(8,128)(2,1)} %get-tuple-element.75), channel_id=1, source_target_pairs={{0,4},{4,8},{8,12},{1,5},{5,9},{9,13},{2,6},{6,10},{10,14},{3,7},{... | collective-permute-start | bytes 184328 | tf_op jit(solution)/shard_map/ppermute | solution.py:33
  79.9 16.9 %collective-permute-start.1 = (bf16[4,1,24,320]{3,2,1,0:T(8,128)(2,1)}, bf16[4,1,24,320]{3,2,1,0:T(8,128)(2,1)}, u32[]{:S(2)}, u32[]{:S(2)}) collective-permute-start(bf16[4,1,24,320]{3,2,1,0:T(8,128)(2,1)} %get-tuple-element.76), channel_id=1, source_target_pairs={{4,0},{8,4},{12,8},{5,1},{9,5},{13,9},{6,2},{10,6},{14,10},{7,3},{... | collective-permute-start | bytes 184328 | tf_op jit(solution)/shard_map/ppermute | solution.py:36
  83.3 17.3 %collective-permute-start.8 = (bf16[4,1,24,320]{3,2,1,0:T(8,128)(2,1)}, bf16[4,1,24,320]{3,2,1,0:T(8,128)(2,1)}, u32[]{:S(2)}, u32[]{:S(2)}) collective-permute-start(bf16[4,1,24,320]{3,2,1,0:T(8,128)(2,1)} %get-tuple-element.72), channel_id=1, source_target_pairs={{0,4},{4,8},{8,12},{1,5},{5,9},{9,13},{2,6},{6,10},{10,14},{3,7},{... | collective-permute-start | bytes 184328 | tf_op jit(solution)/shard_map/ppermute | solution.py:33
  88.5 12.1 %collective-permute-start.9 = (bf16[4,1,24,320]{3,2,1,0:T(8,128)(2,1)}, bf16[4,1,24,320]{3,2,1,0:T(8,128)(2,1)}, u32[]{:S(2)}, u32[]{:S(2)}) collective-permute-start(bf16[4,1,24,320]{3,2,1,0:T(8,128)(2,1)} %get-tuple-element.71), channel_id=1, source_target_pairs={{4,0},{8,4},{12,8},{5,1},{9,5},{13,9},{6,2},{10,6},{14,10},{7,3},{... | collective-permute-start | bytes 184328 | tf_op jit(solution)/shard_map/ppermute | solution.py:36
  97.9 22.9 %collective-permute-start.2 = (bf16[4,18,1,320]{3,2,1,0:T(2,128)(2,1)S(1)}, bf16[4,18,1,320]{3,2,1,0:T(2,128)(2,1)S(1)}, u32[]{:S(2)}, u32[]{:S(2)}) collective-permute-start(bf16[4,18,1,320]{3,2,1,0:T(2,128)(2,1)S(1)} %get-tuple-element.69), channel_id=1, source_target_pairs={{0,1},{1,2},{2,3},{4,5},{5,6},{6,7},{8,9},{9,10},{10,11},{12,13},{... | collective-permute-start | bytes 138248 | tf_op jit(solution)/shard_map/ppermute | solution.py:33
  99.2 21.6 %collective-permute-start.3 = (bf16[4,18,1,320]{3,2,1,0:T(2,128)(2,1)S(1)}, bf16[4,18,1,320]{3,2,1,0:T(2,128)(2,1)S(1)}, u32[]{:S(2)}, u32[]{:S(2)}) collective-permute-start(bf16[4,18,1,320]{3,2,1,0:T(2,128)(2,1)S(1)} %get-tuple-element.70), channel_id=1, source_target_pairs={{1,0},{2,1},{3,2},{5,4},{6,5},{7,6},{9,8},{10,9},{11,10},{13,12},{... | collective-permute-start | bytes 138248 | tf_op jit(solution)/shard_map/ppermute | solution.py:36
  102.2 44.6 %collective-permute-start.10 = (bf16[4,18,1,320]{3,2,1,0:T(2,128)(2,1)}, bf16[4,18,1,320]{3,2,1,0:T(2,128)(2,1)}, u32[]{:S(2)}, u32[]{:S(2)}) collective-permute-start(bf16[4,18,1,320]{3,2,1,0:T(2,128)(2,1)} %get-tuple-element.62), channel_id=1, source_target_pairs={{1,0},{2,1},{3,2},{5,4},{6,5},{7,6},{9,8},{10,9},{11,10},{13,12},{... | collective-permute-start | bytes 138248 | tf_op jit(solution)/shard_map/ppermute | solution.py:36
  103.5 43.3 %collective-permute-start.11 = (bf16[4,18,1,320]{3,2,1,0:T(2,128)(2,1)}, bf16[4,18,1,320]{3,2,1,0:T(2,128)(2,1)}, u32[]{:S(2)}, u32[]{:S(2)}) collective-permute-start(bf16[4,18,1,320]{3,2,1,0:T(2,128)(2,1)} %get-tuple-element.61), channel_id=1, source_target_pairs={{0,1},{1,2},{2,3},{4,5},{5,6},{6,7},{8,9},{9,10},{10,11},{12,13},{... | collective-permute-start | bytes 138248 | tf_op jit(solution)/shard_map/ppermute | solution.py:33
  123.3 12.3 %copy-start.11 = (bf16[4,18,25,320]{3,2,1,0:T(8,128)(2,1)}, bf16[4,18,25,320]{3,2,1,0:T(8,128)(2,1)S(1)}, u32[]{:S(2)}) copy-start(bf16[4,18,25,320]{3,2,1,0:T(8,128)(2,1)S(1)} %get-tuple-element.67) | copy-start | bytes 3456004
  177.4 73.0 %copy-start.5 = (f32[16,24,320]{2,1,0:T(8,128)}, f32[16,24,320]{2,1,0:T(8,128)S(1)}, u32[]{:S(2)}) copy-start(f32[16,24,320]{2,1,0:T(8,128)S(1)} %fusion.151) | copy-start | bytes 1474564
  296.8 16.2 %copy-start.20 = (f32[3,16,24,320]{3,2,1,0:T(8,128)S(1)}, f32[3,16,24,320]{3,2,1,0:T(8,128)}, u32[]{:S(2)}) copy-start(f32[3,16,24,320]{3,2,1,0:T(8,128)} %slice.274) | copy-start | bytes 4423684
  296.8 16.2 %copy-start.36 = (f32[4]{0:T(128)S(1)}, f32[4]{0:T(128)}, u32[]{:S(2)}) copy-start(f32[4]{0:T(128)} %param.13) | copy-start | bytes 52
  321.6 6.3 %collective-permute-start.4 = (bf16[4,1,24,320]{3,2,1,0:T(8,128)(2,1)S(1)}, bf16[4,1,24,320]{3,2,1,0:T(8,128)(2,1)S(1)}, u32[]{:S(2)}, u32[]{:S(2)}) collective-permute-start(bf16[4,1,24,320]{3,2,1,0:T(8,128)(2,1)S(1)} %get-tuple-element.73), channel_id=1, source_target_pairs={{0,4},{4,8},{8,12},{1,5},{5,9},{9,13},{2,6},{6,10},{10,14},{3,7},{... | collective-permute-start | bytes 184328 | tf_op jit(solution)/shard_map/ppermute | solution.py:33
  323.0 6.2 %collective-permute-start.5 = (bf16[4,1,24,320]{3,2,1,0:T(8,128)(2,1)S(1)}, bf16[4,1,24,320]{3,2,1,0:T(8,128)(2,1)S(1)}, u32[]{:S(2)}, u32[]{:S(2)}) collective-permute-start(bf16[4,1,24,320]{3,2,1,0:T(8,128)(2,1)S(1)} %get-tuple-element.74), channel_id=1, source_target_pairs={{4,0},{8,4},{12,8},{5,1},{9,5},{13,9},{6,2},{10,6},{14,10},{7,3},{... | collective-permute-start | bytes 184328 | tf_op jit(solution)/shard_map/ppermute | solution.py:36
  329.4 4.2 collective-permute-start.6
  330.7 3.2 collective-permute-start.7
  358.4 164.9 %all-reduce.5.cloned.1.call-start = ((), (), s32[]{:S(2)}) async-start(), calls=%async_computation.1 | async-start | bytes 5898240 | tf_op jit(solution)/shard_map/psum | solution.py:187
  446.1 81.8 %copy-start.1 = (f32[1000,320]{0,1:T(8,128)S(1)}, f32[1000,320]{0,1:T(8,128)}, u32[]{:S(2)}) copy-start(f32[1000,320]{0,1:T(8,128)} %param.16) | copy-start | bytes 3840004
  (32 other events, 116.7 us)
Sparse Core Ops, SparseCore 0:
  358.6 52.7 reduce-scatter.3
  420.8 102.4 all-reduce.4
where the time goes:
time: 544 us; the launch traced here: 535 us
  blocking collectives  203 us (37%)
  waiting for transfers between devices  107 us (20%)
  matrix products  96.7 us (18%)
  local copies, waits for them, and re-layouts  47 us (9%)
  other arithmetic  42.4 us (8%)
  starting transfers between devices  23.7 us (4%)
  between operations  15.3 us (3%)
    psum x1, waiting for transfers between devices, shards(): grad_weight = lax.psum(share, ('sy', 'sx'))  75.6 us
    psum x2, blocking collectives, group_stats(): totals = lax.psum(jnp.sum(grouped, axis=(1, 3)), ('sy', 'sx'))  66 us
    psum x2, blocking collectives, group_stats(): lax.psum(jnp.sum(shifted * shifted, axis=(1, 3)), ('sy', 'sx')) / cell_count  59 us
    all_gather x3, blocking collectives, prefix(): pieces = lax.all_gather(value, axis)  48.7 us
    dot_general x18, matrix products, convolve(): jnp.einsum('bhwc,cd->bhwd', window, conv_weight[row_off, col_off], prefer...  47.9 us
    unnamed x87, local copies, waits for them, and re-layouts  34.2 us
    dot_general x9, matrix products, backprop(): jnp.einsum('bhwd,cd->bhwc', window, conv_weight[row_off, col_off], prefer...  32.1 us
    unnamed x3, waiting for transfers between devices  29.7 us
  transfers between devices with their start and end apart: 14, of which 4 were waited for; matrix products, arithmetic and copies ran while one was open for 16% of the time, Pallas kernels for 0%

commit v1 on v0

v1 whole, which is shorter than its diff:
```python
import functools

import jax
import jax.numpy as jnp
from jax import lax
from jax.experimental import pallas as pl
from jax.experimental.pallas import tpu as pltpu
from jax.sharding import PartitionSpec as P

GROUPS = 32
EPSILON = 1e-05
LANES = 128
F32 = jnp.float32
BF16 = jnp.bfloat16
VMEM_BYTES = 16 * 1024 * 1024
SMALL_BYTES = 4 * 1024 * 1024
WHOLE_BYTES = 61 * 10**6


def axis_bits(axes):
    bits = []
    for axis in axes:
        step = 1
        while step < lax.axis_size(axis):
            bits.append((axis, step))
            step *= 2
    return bits


def swap(value, axis, bit):
    pairs = [(i, i ^ bit) for i in range(lax.axis_size(axis))]
    return lax.ppermute(value, axis, pairs)


def half_of(tm_index, sy_index):
    last = lax.axis_size("tm") - 1
    return jnp.where(sy_index % 2 == 0, tm_index, last - tm_index)


def share(copies, axes):
    return lax.all_to_all(copies, axes, 0, 0)


def beside(value, axis, bit, work, needs):
    value, needs = lax.optimization_barrier((value, needs))
    other = swap(value, axis, bit)
    return lax.optimization_barrier((other, work(needs)))


def butterfly(value, axes, join, works):
    results = []
    for i, (axis, bit) in enumerate(axis_bits(axes)):
        if i < len(works):
            other, result = beside(value, axis, bit, *works[i](results))
            results.append(result)
        else:
            other = swap(value, axis, bit)
        value = join(value, other, 2**i)
    return value, results


def join_moments(count):
    def join(mine, other, size):
        gap = mine[0] - other[0]
        mean = 0.5 * (mine[0] + other[0])
        return jnp.stack([mean, mine[1] + other[1] + gap * gap * (0.5 * count * size)])

    return join


def join_sums(mine, other, size):
    return mine + other


def chain(axis):
    count = lax.axis_size(axis)
    forward = [(i, i + 1) for i in range(count - 1)]
    return forward, [(b, a) for a, b in forward]


def row_chain():
    slabs, tiles = lax.axis_size("tm"), lax.axis_size("sy")
    order = []
    for sy in range(tiles):
        for half in range(slabs):
            tm = half if sy % 2 == 0 else slabs - 1 - half
            order.append(tm * tiles + sy)
    forward = list(zip(order[:-1], order[1:]))
    return forward, [(b, a) for a, b in forward]


def group_matrix(rows, cols, group, channel_dim, slot):
    channel = lax.broadcasted_iota(jnp.int32, (rows, cols), channel_dim)
    place = lax.broadcasted_iota(jnp.int32, (rows, cols), 1 - channel_dim)
    scale = (1 << 16) // group + 1
    same = ((channel * scale) >> 16) + slot * GROUPS == place
    return (same & (channel < GROUPS * group)).astype(F32)


def exact_dot(left, right):
    return jnp.dot(left, right, precision=lax.Precision.HIGHEST, preferred_element_type=F32)


def gather_groups(values, group, slot):
    return exact_dot(values, group_matrix(values.shape[1], LANES, group, 0, slot))


def spread_groups(values, lanes, group):
    return exact_dot(values, group_matrix(LANES, lanes, group, 1, 0))


def lane_slot(values, slot):
    if slot:
        values = pltpu.roll(values, LANES - slot * GROUPS, 1)
    lane = lax.broadcasted_iota(jnp.int32, values.shape, 1)
    return jnp.where(lane < GROUPS, values, 0.0)


def merged_moments(parts, total_count, lanes, group):
    devices = parts.shape[0]
    total = jnp.sum(parts, axis=0)
    center = lane_slot(total, 0) * (1.0 / devices)
    gap = parts - center[None]
    between = lane_slot(jnp.sum(gap * gap, axis=0), 0) * (total_count / devices)
    spread = (between + lane_slot(total, 1)) * (1.0 / total_count)
    inv = lane_slot(1.0 / jnp.sqrt(spread + EPSILON), 0)
    return spread_groups(center, lanes, group), spread_groups(inv, lanes, group)


def final_moments(moments_ref, count, lanes, group):
    center = lane_slot(moments_ref[0], 0)
    inv = lane_slot(1.0 / jnp.sqrt(moments_ref[1] * (1.0 / count) + EPSILON), 0)
    return spread_groups(center, lanes, group), spread_groups(inv, lanes, group)


def start_copies(pairs, sem):
    copies = [pltpu.make_async_copy(a, b, sem.at[i]) for i, (a, b) in enumerate(pairs)]
    for copy in copies:
        copy.start()
    return copies


def wait_copies(copies):
    for copy in copies:
        copy.wait()


def widen(x, lanes):
    return jnp.concatenate([x, jnp.zeros((x.shape[0], lanes - x.shape[1]), x.dtype)], axis=1)


def framed_row(tile_ref, low_ref, high_ref, sides_ref, part, half, rows, row, lanes):
    tall = tile_ref.shape[0]
    place = half * rows + row - 1
    inner = tile_ref[jnp.clip(place, 0, tall - 1)]
    inner = jnp.where(place < 0, low_ref[part], jnp.where(place >= tall, high_ref[part], inner))
    left = sides_ref[0, part, pl.ds(place + 1, 1), :]
    right = sides_ref[1, part, pl.ds(place + 1, 1), :]
    return jnp.concatenate([left, widen(inner, lanes), right], axis=0)


def noise_of(own_ref, others_ref, place_ref, k, row, lanes):
    steps_here = own_ref.shape[0]
    slabs = others_ref.shape[0] + 1
    slab, step = divmod(k, steps_here)
    offset = lax.rem(place_ref[2] - slab + slabs, slabs)
    mine = own_ref[step, row].astype(F32)
    other = others_ref[jnp.maximum(offset - 1, 0), step, row].astype(F32)
    return widen(jnp.where(offset == 0, mine, other), lanes)


CORNERS = 8


def start_kernel(
    group, ready, index_ref, place_ref, state_ref, drift_ref, noise_coef_ref, lat_ref, reward_ref,
    time_ref, gain_ref, noise_hbm, part_ref, table_ref, low_ref, high_ref, first_ref, last_ref, sent_ref, sem,
):
    others, steps, rows = sent_ref.shape[:3]
    copies = start_copies(
        [
            (noise_hbm.at[:, pl.ds(place_ref[8 + i] * rows, rows)], sent_ref.at[i])
            for i in range(others)
        ],
        sem,
    )
    ready()
    tall, wide, channels = lat_ref.shape
    lanes = table_ref.shape[2]
    corners = []
    for part, ref in enumerate((lat_ref, reward_ref)):
        low_ref[part] = ref[tall - 1]
        high_ref[part] = ref[0]
        for row in range(tall):
            first_ref[part, row : row + 1] = ref[row, 0:1]
            last_ref[part, row : row + 1] = ref[row, wide - 1 : wide]
    for row in (0, tall - 1):
        for col in (0, wide - 1):
            for ref in (lat_ref, reward_ref):
                cell = widen(ref[row, col : col + 1], lanes)
                corners += [cell[:, at : at + LANES] for at in range(0, lanes, LANES)]
    entries = time_ref.shape[1]
    which = lax.broadcasted_iota(jnp.int32, (entries, LANES), 0)
    line = lax.broadcasted_iota(jnp.int32, (entries, LANES), 1)
    hit = jnp.zeros((entries, LANES), F32)
    for k in range(steps):
        hit = jnp.where((line == k) & (which == index_ref[k]), 1.0, hit)
    embedded = jnp.transpose(exact_dot(time_ref[...], hit))[:8]
    modulate = widen(gain_ref[...][None, :] * (1.0 + embedded), lanes)
    table_ref[0] = modulate[:steps]
    for k in range(steps):
        for i, ref in enumerate((state_ref, drift_ref, noise_coef_ref)):
            table_ref[i + 1, k : k + 1] = jnp.full((1, lanes), ref[k], F32)
    x = lat_ref[...].reshape(tall * wide, channels)
    sums = jnp.broadcast_to(jnp.sum(x, axis=0, keepdims=True), (8, channels))
    mean = gather_groups(sums, group, 0) * (1.0 / (tall * wide * group))
    gap = x - spread_groups(mean, channels, group)[0:1]
    square = jnp.broadcast_to(jnp.sum(gap * gap, axis=0, keepdims=True), (8, channels))
    part = jnp.concatenate([mean + gather_groups(square, group, 1)] + corners, axis=0)
    part_ref[...] = jnp.broadcast_to(part[None], part_ref.shape)
    wait_copies(copies)


def edge_kernel(ready, top_ref, bottom_ref, first_ref, last_ref, first_out, last_out):
    rows, steps, _ = first_ref.shape
    span = top_ref.shape[1]
    for out, ref, at in ((first_out, first_ref, 0), (last_out, last_ref, span - steps)):
        out[0] = top_ref[0, at : at + steps]
        out[1 : rows + 1] = ref[...]
        out[rows + 1] = bottom_ref[0, at : at + steps]


def table_kernel(ready, place_ref, own_ref, others_ref, out_ref):
    slabs = others_ref.shape[0] + 1
    kinds, steps, _ = own_ref.shape
    for offset in range(slabs):
        source = lax.rem(place_ref[2] - offset + slabs, slabs)
        for kind in range(kinds):
            rows = own_ref[kind] if offset == 0 else others_ref[offset - 1, kind]
            for k in range(steps):
                out_ref[kind, pl.ds(source * steps + k, 1), :] = rows[k : k + 1]


def packed_rows(taps, channels):
    whole = channels // LANES * LANES
    places = []
    for tap in range(taps):
        rest = taps * whole + tap // 2 * LANES + tap % 2 * (LANES // 2)
        places.append((tap * whole, rest))
    return whole, places


def pack_weight_kernel(ready, w_ref, out_ref, back_ref):
    taps, channels, _ = w_ref.shape
    lanes = out_ref.shape[1]
    whole, places = packed_rows(taps, channels)
    out_ref[...] = jnp.zeros(out_ref.shape, BF16)
    back_ref[...] = jnp.zeros(back_ref.shape, BF16)
    ready()
    for tap, (at, rest) in enumerate(places):
        for ref, value in ((out_ref, w_ref[tap]), (back_ref, jnp.transpose(w_ref[taps - 1 - tap]))):
            ref[at : at + whole, 0:channels] = value[:whole]
            ref[rest : rest + channels - whole, 0:channels] = value[whole:]


def half_turn(x):
    return pltpu.roll(x.astype(F32), LANES // 2, 1).astype(BF16)


def pair_rests(rests):
    pairs = []
    for i in range(0, len(rests), 2):
        pairs.append(rests[i] if i + 1 == len(rests) else rests[i] + half_turn(rests[i + 1]))
    return pairs


def convolve_rows(even_ref, odd_ref, w_ref, start, count, steps):
    span, lanes = odd_ref.shape[1:]
    parts = []
    for row_off in range(3):
        rows = pl.ds(start + row_off, count)
        parts.append(even_ref[rows, 0:span, :].reshape(count * span, lanes))
        parts.append(odd_ref[rows].reshape(count * span, lanes))
        parts.append(even_ref[rows, 2 * steps : 2 * steps + span, :].reshape(count * span, lanes))
    whole = lanes - LANES
    packed = [x[:, :whole] for x in parts] + pair_rests([x[:, whole:] for x in parts])
    return jnp.dot(jnp.concatenate(packed, axis=1), w_ref[...], preferred_element_type=F32)


def put_tiles(ref, value):
    for tile in range(ref.shape[0]):
        ref[tile] = value[:, tile * LANES : (tile + 1) * LANES]


def get_tiles(ref):
    return jnp.concatenate([ref[tile] for tile in range(ref.shape[0])], axis=1)


def get_step(ref, start, cols, steps):
    where = pl.ds(start, cols, stride=steps)
    return jnp.concatenate([ref[tile, where, :] for tile in range(ref.shape[0])], axis=1)


def put_step(ref, start, cols, steps, value):
    where = pl.ds(start, cols, stride=steps)
    for tile in range(ref.shape[0]):
        ref[tile, where, :] = value[:, tile * LANES : (tile + 1) * LANES]


def chunk_rows(rows, span):
    count = max(1, min(rows, 384 // span))
    while rows % count:
        count -= 1
    return count


def advance_row(row, at, half, rows, steps, lat_ref, noise, place_ref, coef_ref, y_ref, row_ref):
    lanes = row_ref.shape[0] * LANES
    cols = row_ref.shape[1] // steps
    own = widen(lat_ref[half * rows + row], lanes)
    run = jnp.zeros_like(own)
    for k in range(steps):
        put_step(row_ref, k, cols, steps, own + run)
        conv = get_step(y_ref, at + k, cols, steps)
        run = run + (
            coef_ref[1, k : k + 1] * own
            + coef_ref[2, k : k + 1] * (own + conv)
            + coef_ref[3, k : k + 1] * noise_of(*noise, place_ref, k, row, lanes)
        )
    return get_tiles(row_ref)


def edge_sweep_kernel(
    group, total_cells, ready, flag_ref, place_ref, low_ref, high_ref, left_ref, right_ref,
    parts_ref, coef_ref, lat_ref, others_ref, w_ref, noise_hbm,
    even_ref, odd_ref, sides_ref, first_row, last_row,
    noise_ref, y_ref, row_ref, sem,
):
    rows, span, lanes = odd_ref.shape
    rows = rows - 2
    steps = coef_ref.shape[1]
    cols = span // steps
    half = place_ref[0]
    tall = lat_ref.shape[0]
    own_noise = noise_hbm.at[:, pl.ds(half * rows, rows)]
    loads = start_copies([(own_noise, noise_ref)], sem)
    center, inv = merged_moments(parts_ref[:, :CORNERS], float(total_cells * group), lanes, group)
    center, inv = center[0:1], inv[0:1]
    pieces = lanes // LANES
    for side, ref in enumerate((left_ref, right_ref)):
        for part in range(2):
            sides_ref[side, part, 1 : tall + 1, :] = widen(ref[part], lanes)
            for end in range(2):
                at = CORNERS + ((3 - 2 * end - side) * 2 + part) * pieces
                device = place_ref[4 + 2 * end + side]
                cell = [parts_ref[device, at + i : at + i + 1, :] for i in range(pieces)]
                cell = jnp.concatenate(cell, axis=1) * flag_ref[4 + 2 * end + side]
                to = end * (tall + 1)
                sides_ref[side, part, to : to + 1, :] = cell
    ready()
    mod = coef_ref[0]

    def activate(row, _):
        field = framed_row(lat_ref, low_ref, high_ref, sides_ref, 0, half, rows, row, lanes)
        normal = (field - center) * inv
        pre = normal[:, None, :] * mod[None]
        act = pre / (1.0 + jnp.exp(-pre))
        keep = jnp.where(row == 0, flag_ref[0], jnp.where(row == rows + 1, flag_ref[1], 1.0))
        act = act * keep
        inner = act[1 : cols + 1]
        act = jnp.concatenate(
            [act[0:1] * flag_ref[2], inner, act[cols + 1 : cols + 2] * flag_ref[3]], axis=0
        )
        even_ref[row] = act.reshape((cols + 2) * steps, lanes).astype(BF16)
        odd_ref[row] = inner.reshape(span, lanes).astype(BF16)
        return 0

    lax.fori_loop(0, rows + 2, activate, 0)
    wait_copies(loads)
    for row, out in ((0, first_row), (rows - 1, last_row)):
        put_tiles(y_ref, convolve_rows(even_ref, odd_ref, w_ref, row, 1, steps))
        noise = (noise_ref, others_ref)
        out[0] = advance_row(row, 0, half, rows, steps, lat_ref, noise, place_ref, coef_ref, y_ref, row_ref)


def inner_sweep_kernel(
    group, ready, place_ref, first_row, last_row, even_ref, odd_ref, coef_ref, lat_ref, others_ref, w_ref,
    noise_hbm, states_ref, moment_ref, first_col, last_col, noise_ref, y_ref, row_ref, sem,
):
    rows, span, lanes = states_ref.shape
    steps = coef_ref.shape[1]
    cols = span // steps
    half = place_ref[0]
    own_noise = noise_hbm.at[:, pl.ds(half * rows, rows)]
    loads = start_copies([(own_noise, noise_ref)], sem)
    states_ref[0] = first_row[0]
    states_ref[rows - 1] = last_row[0]
    wait_copies(loads)
    count = chunk_rows(max(rows - 2, 1), span)

    def sweep(chunk, _):
        start = 1 + chunk * count
        put_tiles(y_ref, convolve_rows(even_ref, odd_ref, w_ref, start, count, steps))
        for inner in range(count):
            states_ref[start + inner] = advance_row(
                start + inner, inner * span, half, rows, steps, lat_ref, (noise_ref, others_ref),
                place_ref, coef_ref, y_ref, row_ref,
            )
        return 0

    lax.fori_loop(0, (rows - 2) // count, sweep, 0)
    zero = jnp.zeros((steps, lanes), F32)

    def add(row, total):
        return total + jnp.sum(states_ref[row].reshape(cols, steps, lanes), axis=0)

    mean = gather_groups(lax.fori_loop(0, rows, add, zero), group, 0) * (1.0 / (rows * cols * group))
    mean_here = spread_groups(mean, lanes, group)

    def squares(row, total):
        gap = states_ref[row].reshape(cols, steps, lanes) - mean_here[None]
        return total + jnp.sum(gap * gap, axis=0)

    moment_ref[0] = mean
    moment_ref[1] = gather_groups(lax.fori_loop(0, rows, squares, zero), group, 0)
    first_col[...] = states_ref[:, 0:steps]
    last_col[...] = states_ref[:, span - steps :]


def act_gradient_kernel(
    first, ready, place_ref, reward_ref, low_ref, high_ref, sides_ref, coef_ref, w_ref,
    out_ref, even_ref, odd_ref,
):
    rows, span, lanes = out_ref.shape
    steps = coef_ref.shape[1]
    cols = span // steps
    drift = coef_ref[2]

    def scale(row, _):
        field = framed_row(
            reward_ref, low_ref, high_ref, sides_ref, 1, place_ref[0], place_ref[3], row + first, lanes
        )
        up = field[:, None, :] * drift[None]
        even_ref[row] = up.reshape((cols + 2) * steps, lanes).astype(BF16)
        odd_ref[row] = up[1 : cols + 1].reshape(span, lanes).astype(BF16)
        return 0

    lax.fori_loop(0, rows + 2, scale, 0)
    count = chunk_rows(rows, span)

    def sweep(chunk, _):
        start = chunk * count
        out = convolve_rows(even_ref, odd_ref, w_ref, start, count, steps)
        out_ref[pl.ds(start, count)] = out.reshape(count, span, lanes)
        return 0

    lax.fori_loop(0, rows // count, sweep, 0)


def norm_gradient_kernel(
    group, total_cells, ready, flag_ref, place_ref, moments_ref, top_ref, bottom_ref, left_ref, right_ref,
    coef_ref, reward_ref, states_ref, *refs
):
    *d_act_refs, even_ref, odd_ref, d_norm_ref, sum_ref, norm_ref = refs
    rows, span, lanes = states_ref.shape
    steps = coef_ref.shape[1]
    cols = span // steps
    center, inv = final_moments(moments_ref, float(total_cells * group), lanes, group)
    norm_ref[0] = center
    norm_ref[1] = inv
    mod = coef_ref[0]

    def activate(at, inner, keep):
        field = jnp.concatenate(
            [left_ref[at][None], inner.reshape(cols, steps, lanes), right_ref[at][None]], axis=0
        )
        normal = (field - center[None]) * inv[None]
        pre = normal * mod[None]
        sig = 1.0 / (1.0 + jnp.exp(-pre))
        act = pre * sig
        if keep is not None:
            act = act * keep
        middle = act[1 : cols + 1]
        odd_ref[at] = middle.reshape(span, lanes).astype(BF16)
        act = jnp.concatenate(
            [act[0:1] * flag_ref[2], middle, act[cols + 1 : cols + 2] * flag_ref[3]], axis=0
        )
        even_ref[at] = act.reshape((cols + 2) * steps, lanes).astype(BF16)
        return [x[1 : cols + 1] for x in (normal, pre, sig)]

    activate(0, top_ref[0], flag_ref[0])
    activate(rows + 1, bottom_ref[0], flag_ref[1])

    def one(d_act_ref, first, index, sums):
        plain, cross, square = sums
        row = index + first
        normal, pre, sig = activate(row + 1, states_ref[row], None)
        slope = sig * (1.0 + pre * (1.0 - sig))
        d_norm = d_act_ref[index].reshape(cols, steps, lanes) * slope * mod[None]
        d_norm_ref[row] = d_norm.reshape(span, lanes)
        return (
            plain + jnp.sum(d_norm, axis=0),
            cross + jnp.sum(d_norm * normal, axis=0),
            square + jnp.sum(d_norm * d_norm, axis=0),
        )

    zero = jnp.zeros((steps, lanes), F32)
    sums = (zero, zero, zero)
    first = 0
    for d_act_ref in d_act_refs:
        count = d_act_ref.shape[0]
        sums = lax.fori_loop(0, count, functools.partial(one, d_act_ref, first), sums)
        first += count
    plain, cross, square = sums
    channels = reward_ref.shape[2]
    reward = reward_ref[pl.ds(place_ref[0] * rows, rows)].reshape(rows * cols, channels)
    reward = jnp.broadcast_to(jnp.sum(reward * reward, axis=0, keepdims=True), (steps, channels))
    sum_ref[...] = (
        gather_groups(plain, group, 0)
        + gather_groups(cross, group, 1)
        + gather_groups(square, group, 2)
        + gather_groups(reward, group, 3)
    )


def second_sweep_kernel(
    first, ready, place_ref, coef_ref, lat_ref, states_ref, others_ref, w_ref, even_ref, odd_ref, noise_hbm, *refs
):
    kept_hbm, sent_ref, noise_ref, y_ref, row_ref, out_ref, sem, out_sem = refs[-8:]
    all_rows, span, lanes = states_ref.shape
    slabs, steps_here, rows, cols, channels = out_ref.shape
    steps = slabs * steps_here
    half = place_ref[0]
    own_noise = noise_hbm.at[:, pl.ds(half * all_rows, all_rows)]
    wait_copies(start_copies([(own_noise, noise_ref)], sem))
    count = chunk_rows(rows, span)

    def sweep(chunk, _):
        start = chunk * count
        put_tiles(y_ref, convolve_rows(even_ref, odd_ref, w_ref, first + start, count, steps))
        for inner in range(count):
            row = first + start + inner
            own = widen(lat_ref[half * all_rows + row], lanes)
            put_tiles(row_ref, states_ref[row])
            run = jnp.zeros_like(own)
            for k in range(steps):
                conv = get_step(y_ref, inner * span + k, cols, steps)
                state = get_step(row_ref, k, cols, steps)
                run = run + (
                    coef_ref[1, k : k + 1] * state
                    + coef_ref[2, k : k + 1] * (state + conv)
                    + coef_ref[3, k : k + 1] * noise_of(noise_ref, others_ref, place_ref, k, row, lanes)
                )
                out_ref[k // steps_here, k % steps_here, start + inner] = run[:, :channels]
        return 0

    lax.fori_loop(0, rows // count, sweep, 0)
    for offset in range(1, slabs):
        sent_ref[offset - 1] = out_ref[lax.rem(place_ref[2] + offset, slabs)] * 0.125
    mine = place_ref[2]

    def complete(row, _):
        own = lat_ref[half * all_rows + first + row]
        for k in range(steps_here):
            out_ref[mine, k, row] = own + out_ref[mine, k, row]
        return 0

    lax.fori_loop(0, rows, complete, 0)
    pairs = [(out_ref.at[mine], kept_hbm.at[:, pl.ds(half * all_rows + first, rows)])]
    wait_copies(start_copies(pairs, out_sem))


def weight_terms(half, up_t, even_ref, odd_ref, steps, put):
    rows = odd_ref.shape[0] - 2
    span, lanes = odd_ref.shape[1:]
    whole = lanes - LANES

    def window(tap, first, last):
        row_off, col_off = divmod(tap, 3)
        if col_off == 1:
            part = odd_ref[row_off : row_off + rows, :, first:last]
        else:
            at = col_off * steps
            part = even_ref[row_off : row_off + rows, at : at + span, first:last]
        return part.reshape(rows * span, last - first)

    def emit(tile, part):
        term = jnp.dot(up_t, part, preferred_element_type=F32)
        for piece in range(part.shape[1] // LANES):
            put(tile + piece, term[:, piece * LANES : (piece + 1) * LANES])

    for i, tap in enumerate(range(6, 9) if half else range(0, 6)):
        emit(i * whole // LANES, window(tap, 0, whole))
    if half:
        rests = pair_rests([window(tap, whole, lanes) for tap in range(9)])
        emit(3 * whole // LANES, jnp.concatenate(rests, axis=1))
        put(3 * whole // LANES + 5, jnp.zeros((up_t.shape[0], LANES), F32))


def late_weight_kernel(half, ready, place_ref, reward_ref, coef_ref, even_ref, odd_ref, out_ref):
    rows, span, lanes = odd_ref.shape
    rows = rows - 2
    steps = coef_ref.shape[1]
    cols = span // steps
    channels = out_ref.shape[1]
    reward = reward_ref[pl.ds(place_ref[0] * rows, rows)].reshape(rows * cols, channels)
    up = widen(reward, lanes)[:, None, :] * coef_ref[2][None]
    up = up.reshape(rows * span, lanes).astype(BF16)

    def put(tile, value):
        out_ref[tile] = value

    weight_terms(half, jnp.transpose(up)[:channels], even_ref, odd_ref, steps, put)


def safe_scale(total, norm, mod, state_coef, drift_coef, cells, group):
    def whole(slot):
        return jnp.sqrt(jnp.sum(lane_slot(total, slot), axis=1, keepdims=True))

    gradient, reward = whole(2), whole(3)
    top_inv = jnp.max(norm, axis=1, keepdims=True)
    top_mod = jnp.max(jnp.abs(mod), axis=1, keepdims=True)
    state, drift = jnp.abs(state_coef[:, 0:1]), jnp.abs(drift_coef[:, 0:1])
    through = jnp.sum((state + drift) * reward + top_inv * gradient, axis=0, keepdims=True)
    field = top_mod * drift * (float(cells * group) ** 0.5)
    bound = jnp.sum(field * (reward + through), axis=0, keepdims=True) * 1.1
    power = jnp.clip(jnp.floor(jnp.log2(32768.0 / jnp.maximum(bound, 1e-30))), -60.0, 60.0)
    scale = jnp.ones_like(power)
    for bit in (32, 16, 8, 4, 2, 1):
        size = jnp.abs(power)
        has = jnp.floor(size / bit) - 2.0 * jnp.floor(size / (2 * bit)) > 0.5
        step = jnp.where(power > 0, 2.0**bit, 2.0**-bit)
        scale = jnp.where(has, scale * step, scale)
    return scale


def half_gradient(half, up_t, late_ref, scale, even_ref, odd_ref, steps, out_ref):
    slabs, _, share_rows, _ = out_ref.shape

    def put(tile, value):
        value = (value + late_ref[tile]) * scale
        for slab in range(slabs):
            out_ref[slab, tile] = value[slab * share_rows : (slab + 1) * share_rows]

    weight_terms(half, up_t, even_ref, odd_ref, steps, put)


def kept_weight_kernel(
    ready, place_ref, up_ref, coef_ref, scale_ref, even_ref, odd_ref, late_a_ref, late_b_ref, out_ref
):
    for half, late_ref in enumerate((late_a_ref, late_b_ref)):

        @pl.when(place_ref[1] == half)
        def _():
            scale, steps = scale_ref[0:1], coef_ref.shape[1]
            half_gradient(half, up_ref[...], late_ref, scale, even_ref, odd_ref, steps, out_ref)


def sent_weight_kernel(
    group, cells, ready, place_ref, states_ref, norm_ref, sums_ref, coef_ref,
    d_norm_ref, reward_ref, even_ref, odd_ref, late_a_ref, late_b_ref,
    out_ref, scale_ref, up_t_ref, d_ref, adj_ref, up_ref,
):
    rows, span, lanes = states_ref.shape
    steps = coef_ref.shape[1]
    cols = span // steps
    center, inv = norm_ref[0], norm_ref[1]
    total = sums_ref[...]
    count = 1.0 / (cells * group)
    plain = spread_groups(lane_slot(total, 0) * count, lanes, group)
    cross = spread_groups(lane_slot(total, 1) * count, lanes, group)
    scale = safe_scale(total, inv, coef_ref[0], coef_ref[1], coef_ref[2], cells, group)
    scale_ref[0:8] = jnp.broadcast_to(scale, (8, LANES))
    scale_ref[8:16] = jnp.broadcast_to(1.0 / scale, (8, LANES))

    def one(row, _):
        normal = (states_ref[row].reshape(cols, steps, lanes) - center[None]) * inv[None]
        d_norm = d_norm_ref[row].reshape(cols, steps, lanes)
        d_group = (d_norm - plain[None] - normal * cross[None]) * inv[None]
        put_tiles(d_ref, d_group.reshape(span, lanes))
        reward = widen(reward_ref[place_ref[0] * rows + row], lanes)
        run = jnp.zeros_like(reward)
        for k in range(steps - 1, -1, -1):
            drift = coef_ref[2, k : k + 1]
            put_step(adj_ref, k, cols, steps, drift * run)
            d_state = drift * reward + get_step(d_ref, k, cols, steps)
            run = run + (coef_ref[1, k : k + 1] * reward + d_state)
        up_ref[pl.ds(pl.multiple_of(row * span, 16), span), :] = get_tiles(adj_ref).astype(BF16)
        return 0

    lax.fori_loop(0, rows, one, 0)
    up_t_ref[...] = jnp.transpose(up_ref[...])[: up_t_ref.shape[0]]
    for half, late_ref in enumerate((late_a_ref, late_b_ref)):

        @pl.when(place_ref[1] != half)
        def _():
            half_gradient(half, up_t_ref[...], late_ref, scale, even_ref, odd_ref, steps, out_ref)


def unpack_kernel(ready, x_ref, scale_ref, out_ref):
    ready()
    whole = out_ref.shape[2] // LANES
    half = LANES // 2
    scale = scale_ref[8:9]
    for tap in range(9):
        for piece in range(whole):
            at = piece * LANES
            out_ref[tap, :, at : at + LANES] = x_ref[tap * whole + piece] * scale
        rest = x_ref[9 * whole + tap // 2] * scale
        if tap % 2:
            rest = pltpu.roll(rest, half, 1)
        out_ref[tap, :, whole * LANES :] = rest[:, :half]


def call(
    kernel, outs, scratch, flops, smem=(), vmem=(), load=(), hbm=(), grant=VMEM_BYTES, aliases=None, size=None
):
    args = [*smem, *vmem, *load, *hbm]
    counts = [len(smem) + len(vmem), len(load), len(hbm) + len(outs) + len(scratch)]
    specs = [pl.BlockSpec(memory_space=pltpu.SMEM)] * len(smem)
    specs += [pl.BlockSpec(memory_space=pltpu.VMEM)] * len(vmem)
    specs += [pl.BlockSpec(memory_space=pltpu.HBM)] * (len(load) + len(hbm))
    shapes = [jax.ShapeDtypeStruct(out[0], out[1]) for out in outs]
    out_specs = [pl.BlockSpec(memory_space=out[2] if len(out) > 2 else pltpu.VMEM) for out in outs]
    if size is None:
        size = sum(a.size * a.dtype.itemsize for a in [*args, *shapes])
    buffers = [s if not isinstance(s, tuple) else pltpu.VMEM(*s) for s in scratch]
    buffers += [pltpu.VMEM(x.shape, x.dtype) for x in load]
    buffers += [pltpu.SemaphoreType.DMA((len(load),))] if load else []

    def body(*refs):
        first, wanted, rest = counts[0], counts[1], counts[2]
        sources = refs[first : first + wanted]
        middle = refs[first + wanted : first + wanted + rest]
        held = refs[first + wanted + rest : first + wanted + rest + wanted]
        copies = start_copies(list(zip(sources, held)), refs[-1]) if wanted else []
        kernel(functools.partial(wait_copies, copies), *refs[:first], *held, *middle)

    return pl.pallas_call(
        body,
        out_shape=shapes,
        in_specs=specs,
        out_specs=out_specs,
        scratch_shapes=buffers,
        input_output_aliases=aliases or {},
        compiler_params=pltpu.CompilerParams(vmem_limit_bytes=grant),
        cost_estimate=pl.CostEstimate(flops=flops, bytes_accessed=size, transcendentals=0),
    )(*args)


F16 = jnp.float16


def bit_of(axis, bit):
    return (lax.axis_index(axis) // bit) % 2


def half_of_dim(value, which, dim):
    count = value.shape[dim] // 2
    return lax.dynamic_slice_in_dim(value, which * count, count, dim)


def half_sum(value, mine, send, dim):
    arrived = send(half_of_dim(value, 1 - mine, dim).astype(F16))
    return half_of_dim(value, mine, dim) + arrived.astype(value.dtype)


def both_halves(value, mine, send, dim):
    other = send(value)
    low = jnp.where(mine == 0, value, other)
    high = jnp.where(mine == 0, other, value)
    return jnp.concatenate([low, high], axis=dim)


def joint_sum(value, sides, dims, sends):
    def quarter(flips):
        part = value
        for side, dim, flip in zip(sides, dims, flips):
            part = half_of_dim(part, 1 - side if flip else side, dim)
        return part

    total = quarter((0, 0))
    arrived = [send(quarter(flips).astype(F16)) for flips, send in sends]
    for part in arrived:
        total = total + part.astype(value.dtype)
    return total


def joint_gather(value, sides, dims, sends):
    parts = {(0, 0): value}
    for flips, send in sends:
        parts[flips] = send(value)

    def order(first, second, side, dim):
        low = jnp.where(side == 0, first, second)
        high = jnp.where(side == 0, second, first)
        return jnp.concatenate([low, high], axis=dim)

    rows = [order(parts[(0, flip)], parts[(1, flip)], sides[0], dims[0]) for flip in (0, 1)]
    return order(rows[0], rows[1], sides[1], dims[1])


FLIPS = ((1, 0), (0, 1), (1, 1))


def reduce_weights(kept, arrived, ready):
    slabs, tiles, share_rows, lanes = kept.shape
    shape = (slabs, 2, tiles // 2, 2, 2, share_rows // 4, lanes)
    pieces = (kept.reshape(shape), arrived.reshape(shape))
    tall, wide = lax.axis_size("sy"), lax.axis_size("sx")
    even = bit_of("sx", 1) == 0

    def turned(sy, sx, turn):
        return (sy, sx ^ 2) if sx % 2 == turn else (sy ^ 1, sx)

    def send_tile(turn, flip_turn, flip_far):
        pairs = []
        for i in range(tall * wide):
            sy, sx = divmod(i, wide)
            to = turned(sy, sx, turn) if flip_turn else (sy, sx)
            to = (to[0] ^ 2, to[1]) if flip_far else to
            pairs.append((i, to[0] * wide + to[1]))
        return lambda value: lax.ppermute(value, ("sy", "sx"), pairs)

    def send_slab(bit, flip_slab, flip_far):
        pairs = []
        for i in range(slabs * tall):
            tm, sy = divmod(i, tall)
            pairs.append((i, (tm ^ (bit * flip_slab)) * tall + (sy ^ (2 * flip_far))))
        return lambda value: lax.ppermute(value, ("tm", "sy"), pairs)

    mine = [bit_of("sx", 2), bit_of("sy", 1)]
    first, second = (jnp.where(even, mine[turn], mine[1 - turn]) for turn in (0, 1))
    far = bit_of("sy", 2)

    def half(which):
        return sum(half_of_dim(x, which, 1) for x in pieces)

    other = send_tile(0, 1, 0)(half(1 - first).astype(F16))
    other, ready = lax.optimization_barrier((other, ready))
    value = half(first) + other.astype(F32)
    value = half_sum(value, second, send_tile(1, 1, 0), 3)
    bits = axis_bits(("tm",))[::-1]
    for axis, bit in bits[:-1]:
        value = half_sum(value, bit_of(axis, bit), lambda x, bit=bit: swap(x, "tm", bit), 0)
    if bits:
        sends = [(flips, send_slab(bits[-1][1], *flips)) for flips in FLIPS]
        value = joint_sum(value, (bit_of(*bits[-1]), far), (0, 4), sends)
    else:
        value = half_sum(value, far, lambda x: swap(x, "sy", 2), 4)
    value = value.astype(F16)
    sends = [(flips, send_tile(1, flips[1], flips[0])) for flips in FLIPS]
    value = joint_gather(value, (far, second), (4, 3), sends)
    value = both_halves(value, first, send_tile(0, 1, 0), 1)
    value = both_halves(value[None], bit_of("sx", 1), lambda x: swap(x, "sx", 1), 0)
    return value.astype(F32).reshape(2 * tiles, share_rows, lanes), ready


def shards(
    latent_init, step_noise, coef_state, coef_drift, coef_noise, step_index, time_table, norm_gain,
    conv_weight, reward_grad,
):
    tile_rows, cols, channels = latent_init.shape
    group = channels // GROUPS
    lanes = -(-channels // LANES) * LANES
    extra = lanes - channels
    slabs = lax.axis_size("tm")
    steps_here = step_noise.shape[0]
    steps = steps_here * slabs
    rows = tile_rows // slabs
    span = steps * cols
    tm, sy, sx = (lax.axis_index(axis) for axis in ("tm", "sy", "sx"))
    half = half_of(tm, sy)
    conv_flops = 2 * 9 * rows * span * channels * channels
    cells = tile_rows * lax.axis_size("sy") * cols * lax.axis_size("sx")
    targets = [half_of((tm + offset) % slabs, sy) for offset in range(1, slabs)]
    tall, wide = lax.axis_size("sy"), lax.axis_size("sx")
    diagonal = [(sy + dy, sx + dx) for dy in (-1, 1) for dx in (-1, 1)]
    corners = [jnp.clip(y, 0, tall - 1) * wide + jnp.clip(x, 0, wide - 1) for y, x in diagonal]
    place = [half, sx % 2, tm, jnp.int32(rows)] + corners + targets
    place = jnp.stack(place).astype(jnp.int32)
    flags = [(sy > 0) | (half > 0), (sy < tall - 1) | (half < slabs - 1), sx > 0, sx < wide - 1]
    flags += [(y >= 0) & (y < tall) & (x >= 0) & (x < wide) for y, x in diagonal]
    flags = jnp.stack(flags).astype(F32)

    def shifted(offset):
        return [(i, (i + offset) % slabs) for i in range(slabs)]

    tiles_axes = ("sy", "sx")
    tile_devices = lax.axis_size(tiles_axes)
    sent_shape = (slabs - 1, steps_here, rows, cols, channels)
    end_shape, col_shape = ((2, cols, channels), F32), ((2, tile_rows, channels), F32)
    part_rows = CORNERS + 8 * (lanes // LANES)
    moments, table, low_rows, high_rows, first_cols, last_cols, leaving = call(
        functools.partial(start_kernel, group),
        [((tile_devices, part_rows, LANES), F32), ((4, steps_here, lanes), F32)]
        + [end_shape, end_shape, col_shape, col_shape, (sent_shape, BF16)],
        [pltpu.SemaphoreType.DMA((slabs - 1,))],
        10**6,
        smem=[step_index, place, coef_state, coef_drift, coef_noise],
        load=[latent_init, reward_grad, time_table.T, norm_gain],
        hbm=[step_noise],
        grant=WHOLE_BYTES,
    )

    def to_slabs(pieces):
        if slabs == 2:
            return lax.ppermute(pieces, "tm", shifted(1))
        return jnp.stack([lax.ppermute(pieces[i], "tm", shifted(i + 1)) for i in range(slabs - 1)])

    down, up = chain("sy")
    right_way, left_way = chain("sx")
    low = lax.ppermute(low_rows, "sy", down)
    high = lax.ppermute(high_rows, "sy", up)
    left = lax.ppermute(last_cols, "sx", right_way)
    right = lax.ppermute(first_cols, "sx", left_way)
    other_tables = to_slabs(jnp.broadcast_to(table[None], (slabs - 1,) + table.shape))
    other_tables, leaving = lax.optimization_barrier((other_tables, leaving))
    others = to_slabs(leaving)
    parts1 = share(moments, tiles_axes)
    parts1, conv_weight = lax.optimization_barrier((parts1, conv_weight))
    (coefs,) = call(
        table_kernel, [((4, steps, lanes), F32)], [], 10**5, smem=[place], vmem=[table, other_tables],
        grant=SMALL_BYTES,
    )
    packed = ((9 * (lanes - LANES) + 5 * LANES, lanes), BF16)
    weight_out, weight_back = call(
        pack_weight_kernel, [packed, packed], [], 10**7, load=[conv_weight.reshape(9, channels, channels)],
    )

    even_shape = (rows + 2, (cols + 2) * steps, lanes)
    odd_shape = (rows + 2, span, lanes)
    field_shape = (rows, span, lanes)
    y_shape = (lanes // LANES, chunk_rows(rows, span) * span, LANES)
    row_shape = (lanes // LANES, span, LANES)
    noise_shape = (steps_here, rows, cols, channels)
    even_out, odd_out, field_out = (even_shape, BF16), (odd_shape, BF16), (field_shape, F32)
    edge_row, edge_col = ((1, span, lanes), F32), ((rows, steps, lanes), F32)
    noise_scratch = [(noise_shape, BF16)]
    even1, odd1, sides, first_row, last_row = call(
        functools.partial(edge_sweep_kernel, group, cells),
        [even_out, odd_out, ((2, 2, tile_rows + 2, lanes), F32), edge_row, edge_row],
        noise_scratch + [(row_shape, F32), (row_shape, F32), pltpu.SemaphoreType.DMA((1,))],
        conv_flops // 4,
        smem=[flags, place],
        vmem=[low, high, left, right, parts1, coefs, latent_init, others, weight_out],
        hbm=[step_noise],
    )
    down_rows, up_rows = row_chain()
    top = lax.ppermute(last_row, ("tm", "sy"), down_rows)
    bottom = lax.ppermute(first_row, ("tm", "sy"), up_rows)
    states, moments, first_col, last_col = call(
        functools.partial(inner_sweep_kernel, group),
        [field_out, ((2, steps, LANES), F32), edge_col, edge_col],
        noise_scratch + [(y_shape, F32), (row_shape, F32), pltpu.SemaphoreType.DMA((1,))],
        conv_flops,
        smem=[place],
        vmem=[first_row, last_row, even1, odd1, coefs, latent_init, others, weight_out],
        hbm=[step_noise],
    )

    def side_cols(args):
        top, bottom, first, last = args
        side_out = ((rows + 2, steps, lanes), F32)
        first, last = call(
            edge_kernel, [side_out, side_out], [], 10**5, vmem=[top, bottom, first, last], grant=SMALL_BYTES
        )
        return lax.ppermute(last, "sx", right_way), lax.ppermute(first, "sx", left_way)

    def act_gradient(first, count):
        def run(reward):
            (out,) = call(
                functools.partial(act_gradient_kernel, first),
                [((count, span, lanes), F32)],
                [((count + 2,) + even_shape[1:], BF16), ((count + 2,) + odd_shape[1:], BF16)],
                conv_flops // 4,
                smem=[place],
                vmem=[reward, low, high, sides, coefs, weight_back],
            )
            return out

        return run

    order = ("sx", "sy", "tm")
    cut = max(1, rows // 4)
    pieces = [(at, min(cut, rows - at)) for at in range(0, rows, cut)]

    def cols_and_first(args):
        return side_cols(args[1:]), act_gradient(*pieces[0])(args[0])

    def d_act_work(piece):
        return lambda done: (act_gradient(*piece), reward_grad)

    moments2, (((left2, right2), d_first), *d_rest) = butterfly(
        moments,
        order,
        join_moments(float(rows * cols * group)),
        [lambda done: (cols_and_first, (reward_grad, top, bottom, first_col, last_col))]
        + [d_act_work(piece) for piece in pieces[1:]],
    )
    even2, odd2, d_norm, sums, norm = call(
        functools.partial(norm_gradient_kernel, group, cells),
        [even_out, odd_out, field_out, ((steps, LANES), F32), ((2, steps, lanes), F32)],
        [],
        40 * rows * span * lanes,
        smem=[flags, place],
        vmem=[moments2, top, bottom, left2, right2, coefs, reward_grad, states, d_first, *d_rest],
    )

    share_rows = channels // slabs
    tiles = 9 * (channels // LANES) + 6

    def late_weight(half):
        def run(reward):
            (out,) = call(
                functools.partial(late_weight_kernel, half),
                [((tiles // 2, channels, LANES), F32)],
                [],
                conv_flops // 2,
                smem=[place],
                vmem=[reward, coefs, even2, odd2],
            )
            return out

        return lambda done: (run, reward_grad)

    def second_sweep(first, count):
        out_shape = (slabs, steps_here, count, cols, channels)

        def run(args):
            base = list(args[1:])
            return call(
                functools.partial(second_sweep_kernel, first),
                [(step_noise.shape, F32, pltpu.HBM), ((slabs - 1,) + out_shape[1:], F32)],
                [(noise_shape, BF16), (y_shape, F32), (row_shape, F32), (out_shape, F32)]
                + [pltpu.SemaphoreType.DMA((1,)), pltpu.SemaphoreType.DMA((1,))],
                conv_flops // 2,
                smem=[place],
                vmem=[coefs, args[0], states, others, weight_out, even2, odd2],
                hbm=[step_noise] + base,
                aliases={9: 0} if base else None,
            )

        return run

    sums, (late_a, late_b, (base, sent_a), (trajectory, sent_b)) = butterfly(
        sums,
        ("tm", "sx", "sy"),
        join_sums,
        [
            late_weight(0),
            late_weight(1),
            lambda done: (second_sweep(0, rows // 2), (latent_init,)),
            lambda done: (second_sweep(rows // 2, rows - rows // 2), (latent_init, done[2][0])),
        ],
    )
    landing = [to_slabs(sent_a.astype(F16)), to_slabs(sent_b.astype(F16))]

    payload = ((slabs, tiles // 2, share_rows, LANES), F32)
    up_shape = ((channels, rows * span), BF16)
    sent, scales, up_t = call(
        functools.partial(sent_weight_kernel, group, cells),
        [payload, ((16, LANES), F32), up_shape],
        [(row_shape, F32), (row_shape, F32), ((rows * span, lanes), BF16)],
        conv_flops // 2,
        smem=[place],
        vmem=[states, norm, sums, coefs, d_norm, reward_grad, even1, odd1, late_a, late_b],
        size=10**6,
    )

    def kept_weight(args):
        (kept,) = call(
            kept_weight_kernel,
            [payload],
            [],
            conv_flops // 2,
            smem=[place],
            vmem=[args[0], coefs, scales, even1, odd1, late_a, late_b],
        )
        return kept

    sent, landing = lax.optimization_barrier((sent, landing))
    arrived, kept = beside(sent, "sx", 1, kept_weight, (up_t,))

    cut = rows // 2
    for offset in range(1, slabs):
        source = half_of((tm - offset) % slabs, sy) * rows
        for part, at, count in zip(landing, (0, cut), (cut, rows - cut)):
            own = lax.dynamic_slice_in_dim(latent_init, source + at, count, 0)
            part = own[None] + 8.0 * part[offset - 1].astype(F32)
            trajectory = lax.dynamic_update_slice_in_dim(trajectory, part, source + at, 1)

    summed, trajectory = reduce_weights(kept, arrived, trajectory)
    (grad,) = call(
        unpack_kernel, [((9, share_rows, channels), F32)], [], 10**6, vmem=[summed, scales],
        grant=SMALL_BYTES,
    )
    return trajectory, grad.transpose(0, 2, 1).reshape(3, 3, channels, share_rows)


def solution(mesh):
    placed = (
        P("sy", "sx", None),
        P("tm", "sy", "sx", None),
        P("tm"),
        P("tm"),
        P("tm"),
        P("tm"),
        P(),
        P(),
        P(),
        P("sy", "sx", None),
    )
    return jax.shard_map(
        shards,
        mesh=mesh,
        in_specs=placed,
        out_specs=(P("tm", "sy", "sx", None), P(None, None, None, "tm")),
        check_vma=False,
    )
```

time: 544 us -> 168 us (0.31); the launches traced: 535 us -> 167 us
  blocking collectives: 203 us -> 0 us
  matrix products: 96.7 us -> 0 us
  waiting for transfers between devices: 107 us -> 41.4 us
  Pallas kernels: 0 us -> 54.7 us
  local copies, waits for them, and re-layouts: 47 us -> 10.2 us
  other arithmetic: 42.4 us -> 6.12 us
  starting transfers between devices: 23.7 us -> 52.8 us
  between operations: 15.3 us -> 1.47 us
    psum x5 -> x0, blocking collectives: 154 us -> none  [the longest x2 66 us: group_stats(): totals = lax.psum(jnp.sum(grouped, axis=(1, 3)), ('sy', 'sx'))]
    dot_general x46 -> x0, matrix products: 96.7 us -> none  [the longest x18 47.9 us: convolve(): jnp.einsum('bhwc,cd->bhwd', window, conv_weight[row_off, col_off], prefer...]
    psum x1 -> x0, waiting for transfers between devices: 75.6 us -> none  [shards(): grad_weight = lax.psum(share, ('sy', 'sx'))]
    pallas_call x0 -> x18, Pallas kernels: none -> 54.7 us  [call(): pl.pallas_call(body, out_shape=shapes, in_specs=specs, out_specs=out_spec...]
    all_gather x3 -> x0, blocking collectives: 48.7 us -> none  [prefix(): pieces = lax.all_gather(value, axis)]
    ppermute x12 -> x33, waiting for transfers between devices: 1.57 us -> 41.4 us  [the longest x6 20.9 us: send_tile(): return lambda value: lax.ppermute(value, ('sy', 'sx'), pairs)]
    unnamed x3 -> x0, waiting for transfers between devices: 29.7 us -> none
    unnamed x87 -> x40, local copies, waits for them, and re-layouts: 34.2 us -> 9.51 us
  transfers between devices with their start and end apart: 14 -> 34, of which waited for: 4 -> 14; matrix products, arithmetic and copies ran while one was open for 16% -> 1% of each run, Pallas kernels for 0% -> 24%
where the time goes in v1:
time: 168 us; the launch traced here: 167 us
  Pallas kernels  54.7 us (33%)
  starting transfers between devices  52.8 us (31%)
  waiting for transfers between devices  41.4 us (25%)
  local copies, waits for them, and re-layouts  10.2 us (6%)
  other arithmetic  6.12 us (4%)
    pallas_call x18, Pallas kernels, call(): pl.pallas_call(body, out_shape=shapes, in_specs=specs, out_specs=out_spec...  54.7 us
    ppermute x6, waiting for transfers between devices, send_tile(): return lambda value: lax.ppermute(value, ('sy', 'sx'), pairs)  20.9 us
    ppermute x12, starting transfers between devices, swap(): return lax.ppermute(value, axis, pairs)  14.3 us
    unnamed x40, local copies, waits for them, and re-layouts  9.51 us
    ppermute x12, waiting for transfers between devices, swap(): return lax.ppermute(value, axis, pairs)  8.69 us
    ppermute x6, starting transfers between devices, send_tile(): return lambda value: lax.ppermute(value, ('sy', 'sx'), pairs)  6.14 us
    all_to_all x1, starting transfers between devices, share(): return lax.all_to_all(copies, axes, 0, 0)  5.94 us
    ppermute x3, waiting for transfers between devices, send_slab(): return lambda value: lax.ppermute(value, ('tm', 'sy'), pairs)  5.86 us
  transfers between devices with their start and end apart: 34, of which 14 were waited for; matrix products, arithmetic and copies ran while one was open for 1% of the time, Pallas kernels for 24%

profile of v1, /device:TPU:0, one launch (start us, length us, event | category | flops | bytes accessed | tf_op | source)
XLA Modules:
  0.0 166.8 jit_solution(13604898346247815818)
XLA Ops:
  1.3 5.3 %shard_map.113 = (f32[16,32,128]{2,1,0:T(8,128)}, f32[4,4,384]{2,1,0:T(4,128)}, f32[2,24,320]{2,1,0:T(8,128)}, f32[2,24,320]{2,1,0:T(8,128)}, f32[2,16,320]{2,1,...) custom-call(s32[4]{0:T(128)} %refs_0_.1, s32[9]{0:T(128)} %stack.87.refs_1_.refs_0_, f32[4]{0:T(128)} %refs_2_.1, ...), custom_call_target="tpu_custom_call" | custom-call | flops 1000000 | bytes 4230500 | tf_op jit(solution)/shard_map/pallas_call | solution.py:739
  6.7 3.0 %collective-permute-start.4 = (f32[1,4,4,384]{3,2,1,0:T(4,128)}, f32[1,4,4,384]{3,2,1,0:T(4,128)S(1)}, u32[]{:S(2)}, u32[]{:S(2)}) collective-permute-start(f32[1,4,4,384]{3,2,1,0:T(4,128)} %bitcast.43), channel_id=1, source_target_pairs={{0,16},{16,0},{1,17},{17,1},{2,18},{18,2},{3,19},{19,3},{4,20},{20... | collective-permute-start | bytes 73736 | tf_op jit(solution)/shard_map/ppermute | solution.py:908
  9.7 5.9 %all-to-all-start = ((f32[16,32,128]{2,1,0:T(8,128)}), f32[16,32,128]{2,1,0:T(8,128)S(1)}, u32[]{:S(2)}, u32[]{:S(2)}) async-start(f32[16,32,128]{2,1,0:T(8,128)} %get-tuple-element.92), calls=%async_computation | async-start | bytes 524288 | tf_op jit(solution)/shard_map/all_to_all | solution.py:41
  16.2 3.8 %collective-permute-start = (f32[2,24,320]{2,1,0:T(8,128)}, f32[2,24,320]{2,1,0:T(8,128)S(1)}, u32[]{:S(2)}, u32[]{:S(2)}) collective-permute-start(f32[2,24,320]{2,1,0:T(8,128)} %get-tuple-element.88), channel_id=1, source_target_pairs={{0,4},{4,8},{8,12},{1,5},{5,9},{9,13},{2,6},{6,10},{10,14},{3,7},{... | collective-permute-start | bytes 184328 | tf_op jit(solution)/shard_map/ppermute | solution.py:913
  28.9 2.7 %collective-permute-done.5.refs_9_.refs_7_.refs_4_ = bf16[1,4,8,24,320]{4,3,2,1,0:T(8,128)(2,1)S(1)} collective-permute-done((bf16[1,4,8,24,320]{4,3,2,1,0:T(8,128)(2,1)}, bf16[1,4,8,24,320]{4,3,2,1,0:T(8,128)(2,1)S(1)}, u32[]{:S(2)}, u32[]{:S(2)}) %collective-permute-start.5) | collective-permute-done | bytes 491552 | tf_op jit(solution)/shard_map/ppermute | solution.py:908
  31.6 4.0 %shard_map.116 = (bf16[10,208,384]{2,1,0:T(8,128)(2,1)S(1)}, bf16[10,192,384]{2,1,0:T(8,128)(2,1)S(1)}, f32[2,2,18,384]{3,2,1,0:T(8,128)S(1)}, f32[1,192,384]{2,1,0:T(8,128)S(1)}, f32[1,192,384]{2,1,0:T(8,128)S(1)}) custom-call(f32[8]{0:T(128)S(1)} %convert_element_type.59.refs_0_, s32[9]{0:T(128)S(1)} %copy-done.16, ...), custom_call_target="tpu_custom_call" | custom-call | flops 707788800 | bytes 8515652 | tf_op jit(solution)/shard_map/pallas_call | solution.py:739
  35.7 2.5 %collective-permute-start.6 = (f32[1,192,384]{2,1,0:T(8,128)S(1)}, f32[1,192,384]{2,1,0:T(8,128)S(1)}, u32[]{:S(2)}, u32[]{:S(2)}) collective-permute-start(f32[1,192,384]{2,1,0:T(8,128)S(1)} %get-tuple-element.101.refs_2_), channel_id=1, source_target_pairs={{0,16},{16,20},{20,4},{4,8},{8,24},{24,28},{28,12},{1,17},{17,21},... | collective-permute-start | bytes 884744 | tf_op jit(solution)/shard_map/ppermute | solution.py:950
  39.4 6.7 %shard_map.117 = (f32[8,192,384]{2,1,0:T(8,128)S(1)}, f32[2,8,128]{2,1,0:T(8,128)S(1)}, f32[8,8,384]{2,1,0:T(8,128)S(1)}, f32[8,8,384]{2,1,0:T(8,128)S(1)}) custom-call(s32[9]{0:T(128)S(1)} %copy-done.16, f32[1,192,384]{2,1,0:T(8,128)S(1)} %get-tuple-element.100.refs_1_, f32[1,192,384]{2,1,0:T(8,128)S(1)} %get-tuple-element.101.refs_2_, ...), custom_call_target="tpu_custom_call" | custom-call | flops 2831155200 | bytes 10502180 | tf_op jit(solution)/shard_map/pallas_call | solution.py:739
  46.2 3.2 %collective-permute-done.7.refs_1_.refs_4_ = f32[1,192,384]{2,1,0:T(8,128)S(1)} collective-permute-done((f32[1,192,384]{2,1,0:T(8,128)S(1)}, f32[1,192,384]{2,1,0:T(8,128)S(1)}, u32[]{:S(2)}, u32[]{:S(2)}) %collective-permute-start.7) | collective-permute-done | bytes 294944 | tf_op jit(solution)/shard_map/ppermute | solution.py:951
  50.7 3.2 %collective-permute-start.9 = (f32[10,8,384]{2,1,0:T(8,128)S(1)}, f32[10,8,384]{2,1,0:T(8,128)S(1)}, u32[]{:S(2)}, u32[]{:S(2)}) collective-permute-start(f32[10,8,384]{2,1,0:T(8,128)S(1)} %get-tuple-element.113), channel_id=1, source_target_pairs={{0,1},{1,2},{2,3},{4,5},{5,6},{6,7},{8,9},{9,10},{10,11},{12,13},{... | collective-permute-start | bytes 368648 | tf_op jit(solution)/shard_map/ppermute | solution.py:968
  61.7 2.4 %collective-permute-start.12 = (f32[2,8,128]{2,1,0:T(8,128)S(1)}, f32[2,8,128]{2,1,0:T(8,128)S(1)}, u32[]{:S(2)}, u32[]{:S(2)}) collective-permute-start(f32[2,8,128]{2,1,0:T(8,128)S(1)} %pad_maximum_fusion.5), channel_id=1, source_target_pairs={{0,4},{4,0},{8,12},{12,8},{1,5},{5,1},{9,13},{13,9},{2,6},{6,2},{1... | collective-permute-start | bytes 24584 | tf_op jit(solution)/shard_map/ppermute | solution.py:32
  71.8 2.8 %collective-permute-done.14 = f32[2,8,128]{2,1,0:T(8,128)S(1)} collective-permute-done((f32[2,8,128]{2,1,0:T(8,128)S(1)}, f32[2,8,128]{2,1,0:T(8,128)S(1)}, u32[]{:S(2)}, u32[]{:S(2)}) %collective-permute-start.14) | collective-permute-done | bytes 8224 | tf_op jit(solution)/shard_map/ppermute | solution.py:32
  74.6 3.4 %shard_map.123 = (bf16[10,208,384]{2,1,0:T(8,128)(2,1)S(1)}, bf16[10,192,384]{2,1,0:T(8,128)(2,1)S(1)}, f32[8,192,384]{2,1,0:T(8,128)S(1)}, f32[8,128]{1,0:T(8,128)S(1)}, f32[2,8,384]{2,1,0:T(8,128)S(1)}) custom-call(f32[8]{0:T(128)S(1)} %convert_element_type.59.refs_0_, s32[9]{0:T(128)S(1)} %copy-done.16, f32[2,8,128]{2,1,0:T(8,128)S(1)} %pad_maximum_fusion.8.refs_2_, ...), custom_call_target="tpu_custom_call" | custom-call | flops 23592960 | bytes 11563076 | tf_op jit(solution)/shard_map/pallas_call | solution.py:739
  81.7 2.3 %shard_map.125.refs_10_.refs_7_ = f32[12,320,128]{2,1,0:T(8,128)S(1)} custom-call(s32[9]{0:T(128)S(1)} %copy-done.16, f32[16,24,320]{2,1,0:T(8,128)S(1)} %copy-done, f32[4,8,384]{2,1,0:T(8,128)S(1)} %shard_map.114.refs_7_.refs_5_.refs_2_.refs_1_.refs_4_, bf16[10,208,384]{2,1,0:T(8,128)(2,1)S(1)} %get-tuple-element.138.refs_3_.refs_6_, ...), custom_call_target="tpu_custom_call" | custom-call | flops 1415577600 | bytes 5578788 | tf_op jit(solution)/shard_map/pallas_call | solution.py:739
  85.7 4.8 %shard_map.126 = (f32[4,16,24,320]{3,2,1,0:T(8,128)}, f32[1,4,4,24,320]{4,3,2,1,0:T(8,128)S(1)}) custom-call(s32[9]{0:T(128)S(1)} %copy-done.16, f32[4,8,384]{2,1,0:T(8,128)S(1)} %shard_map.114.refs_7_.refs_5_.refs_2_.refs_1_.refs_4_, f32[16,24,320]{2,1,0:T(8,128)S(1)} %copy-done.5, f32[8,192,384]{2,1,0:T(8,128)S(1)} %get-tuple-element.104.refs_9_.refs_3_.refs_1_, ...), custom_call_target="tpu_custom_call" | custom-call | flops 1415577600 | bytes 12165156 | tf_op jit(solution)/shard_map/pallas_call | solution.py:739
  93.0 5.1 %shard_map.127 = (f32[4,16,24,320]{3,2,1,0:T(8,128)}, f32[1,4,4,24,320]{4,3,2,1,0:T(8,128)S(1)}) custom-call(s32[9]{0:T(128)S(1)} %copy-done.16, f32[4,8,384]{2,1,0:T(8,128)S(1)} %shard_map.114.refs_7_.refs_5_.refs_2_.refs_1_.refs_4_, f32[16,24,320]{2,1,0:T(8,128)S(1)} %copy-done.5, ...), custom_call_target="tpu_custom_call", output_to_operand_aliasing={{0}: (9, {})} | custom-call | flops 1415577600 | bytes 14131236 | tf_op jit(solution)/shard_map/pallas_call | solution.py:739
  101.1 2.8 %collective-permute-done.19 = f32[8,128]{1,0:T(8,128)S(1)} collective-permute-done((f32[8,128]{1,0:T(8,128)S(1)}, f32[8,128]{1,0:T(8,128)S(1)}, u32[]{:S(2)}, u32[]{:S(2)}) %collective-permute-start.19) | collective-permute-done | bytes 4128 | tf_op jit(solution)/shard_map/ppermute | solution.py:32
  103.9 6.2 %shard_map.128 = (f32[2,12,160,128]{3,2,1,0:T(8,128)}, f32[16,128]{1,0:T(8,128)S(1)}, bf16[320,1536]{1,0:T(8,128)(2,1)S(1)}) custom-call(s32[9]{0:T(128)S(1)} %copy-done.16, f32[8,192,384]{2,1,0:T(8,128)S(1)} %get-tuple-element.104.refs_9_.refs_3_.refs_1_, f32[2,8,384]{2,1,0:T(8,128)S(1)} %get-tuple-element.134.refs_2_, f32[8,128]{1,0:T(8,128)S(1)} %add.323.refs_3_, ...), custom_call_target="tpu_custom_call" | custom-call | flops 1415577600 | bytes 1000000 | tf_op jit(solution)/shard_map/pallas_call | solution.py:739
  123.5 6.5 %collective-permute-done.23 = f16[2,1,6,2,2,40,128]{6,5,4,3,2,1,0:T(8,128)(2,1)S(1)} collective-permute-done((f16[2,1,6,2,2,40,128]{6,5,4,3,2,1,0:T(8,128)(2,1)S(1)}, f16[2,1,6,2,2,40,128]{6,5,4,3,2,1,0:T(8,128)(2,1)S(1)}, u32[]{:S(2)}, u32[]{:S(2)}) %collective-permute-start.23) | collective-permute-done | bytes 491552 | tf_op jit(solution)/shard_map/ppermute | solution.py:823
  132.1 5.7 %collective-permute-done.24 = f16[2,1,6,1,2,40,128]{6,5,4,3,2,1,0:T(8,128)(2,1)S(1)} collective-permute-done((f16[2,1,6,1,2,40,128]{6,5,4,3,2,1,0:T(8,128)(2,1)S(1)}, f16[2,1,6,1,2,40,128]{6,5,4,3,2,1,0:T(8,128)(2,1)S(1)}, u32[]{:S(2)}, u32[]{:S(2)}) %collective-permute-start.24) | collective-permute-done | bytes 245792 | tf_op jit(solution)/shard_map/ppermute | solution.py:823
  142.4 2.4 %collective-permute-done.26 = f16[1,1,6,1,1,40,128]{6,5,4,3,2,1,0:T(8,128)(2,1)S(1)} collective-permute-done((f16[1,1,6,1,1,40,128]{6,5,4,3,2,1,0:T(8,128)(2,1)S(1)}, f16[1,1,6,1,1,40,128]{6,5,4,3,2,1,0:T(8,128)(2,1)S(1)}, u32[]{:S(2)}, u32[]{:S(2)}) %collective-permute-start.26) | collective-permute-done | bytes 61472 | tf_op jit(solution)/shard_map/ppermute | solution.py:830
  144.8 3.4 %collective-permute-done.27 = f16[1,1,6,1,1,40,128]{6,5,4,3,2,1,0:T(8,128)(2,1)S(1)} collective-permute-done((f16[1,1,6,1,1,40,128]{6,5,4,3,2,1,0:T(8,128)(2,1)S(1)}, f16[1,1,6,1,1,40,128]{6,5,4,3,2,1,0:T(8,128)(2,1)S(1)}, u32[]{:S(2)}, u32[]{:S(2)}) %collective-permute-start.27) | collective-permute-done | bytes 61472 | tf_op jit(solution)/shard_map/ppermute | solution.py:830
  148.5 4.2 %collective-permute-start.30 = (f16[1,1,6,1,1,40,128]{6,5,4,3,2,1,0:T(8,128)(2,1)S(1)}, f16[1,1,6,1,1,40,128]{6,5,4,3,2,1,0:T(8,128)(2,1)S(1)}, u32[]{:S(2)}, u32[]{:S(2)}) collective-permute-start(f16[1,1,6,1,1,40,128]{6,5,4,3,2,1,0:T(8,128)(2,1)S(1)} %add_convert_fusion.1), channel_id=1, source_target_pairs={{0,12},{1,11},{2,14},{3,9},{4,8},{5,15},{6,10},{7,13},{8,4},{9,3},... | collective-permute-start | bytes 184328 | tf_op jit(solution)/shard_map/ppermute | solution.py:823
  156.5 5.7 %collective-permute-done.31 = f16[1,1,6,2,2,40,128]{6,5,4,3,2,1,0:T(8,128)(2,1)S(1)} collective-permute-done((f16[1,1,6,2,2,40,128]{6,5,4,3,2,1,0:T(8,128)(2,1)S(1)}, f16[1,1,6,2,2,40,128]{6,5,4,3,2,1,0:T(8,128)(2,1)S(1)}, u32[]{:S(2)}, u32[]{:S(2)}) %collective-permute-start.31) | collective-permute-done | bytes 245792 | tf_op jit(solution)/shard_map/ppermute | solution.py:823
  (140 shorter events, 67.0 us)
Async XLA Ops:
  6.7 9.0 %collective-permute-start.4 = (f32[1,4,4,384]{3,2,1,0:T(4,128)}, f32[1,4,4,384]{3,2,1,0:T(4,128)S(1)}, u32[]{:S(2)}, u32[]{:S(2)}) collective-permute-start(f32[1,4,4,384]{3,2,1,0:T(4,128)} %bitcast.43), channel_id=1, source_target_pairs={{0,16},{16,0},{1,17},{17,1},{2,18},{18,2},{3,19},{19,3},{4,20},{20... | collective-permute-start | bytes 73736 | tf_op jit(solution)/shard_map/ppermute | solution.py:908
  9.7 16.0 %all-to-all-start = ((f32[16,32,128]{2,1,0:T(8,128)}), f32[16,32,128]{2,1,0:T(8,128)S(1)}, u32[]{:S(2)}, u32[]{:S(2)}) async-start(f32[16,32,128]{2,1,0:T(8,128)} %get-tuple-element.92), calls=%async_computation | async-start | bytes 524288 | tf_op jit(solution)/shard_map/all_to_all | solution.py:41
  15.6 15.9 %collective-permute-start.5 = (bf16[1,4,8,24,320]{4,3,2,1,0:T(8,128)(2,1)}, bf16[1,4,8,24,320]{4,3,2,1,0:T(8,128)(2,1)S(1)}, u32[]{:S(2)}, u32[]{:S(2)}) collective-permute-start(bf16[1,4,8,24,320]{4,3,2,1,0:T(8,128)(2,1)} %get-tuple-element.97), channel_id=1, source_target_pairs={{0,16},{16,0},{1,17},{17,1},{2,18},{18,2},{3,19},{19,3},{4,20},{20... | collective-permute-start | bytes 1474568 | tf_op jit(solution)/shard_map/ppermute | solution.py:908
  16.2 12.7 %collective-permute-start = (f32[2,24,320]{2,1,0:T(8,128)}, f32[2,24,320]{2,1,0:T(8,128)S(1)}, u32[]{:S(2)}, u32[]{:S(2)}) collective-permute-start(f32[2,24,320]{2,1,0:T(8,128)} %get-tuple-element.88), channel_id=1, source_target_pairs={{0,4},{4,8},{8,12},{1,5},{5,9},{9,13},{2,6},{6,10},{10,14},{3,7},{... | collective-permute-start | bytes 184328 | tf_op jit(solution)/shard_map/ppermute | solution.py:913
  20.1 8.8 %collective-permute-start.1 = (f32[2,24,320]{2,1,0:T(8,128)}, f32[2,24,320]{2,1,0:T(8,128)S(1)}, u32[]{:S(2)}, u32[]{:S(2)}) collective-permute-start(f32[2,24,320]{2,1,0:T(8,128)} %get-tuple-element.89), channel_id=1, source_target_pairs={{4,0},{8,4},{12,8},{5,1},{9,5},{13,9},{6,2},{10,6},{14,10},{7,3},{... | collective-permute-start | bytes 184328 | tf_op jit(solution)/shard_map/ppermute | solution.py:914
  21.4 7.5 %collective-permute-start.2 = (f32[2,16,320]{2,1,0:T(8,128)}, f32[2,16,320]{2,1,0:T(8,128)S(1)}, u32[]{:S(2)}, u32[]{:S(2)}) collective-permute-start(f32[2,16,320]{2,1,0:T(8,128)} %get-tuple-element.90), channel_id=1, source_target_pairs={{0,1},{1,2},{2,3},{4,5},{5,6},{6,7},{8,9},{9,10},{10,11},{12,13},{... | collective-permute-start | bytes 122888 | tf_op jit(solution)/shard_map/ppermute | solution.py:915
  22.9 6.0 %collective-permute-start.3 = (f32[2,16,320]{2,1,0:T(8,128)}, f32[2,16,320]{2,1,0:T(8,128)S(1)}, u32[]{:S(2)}, u32[]{:S(2)}) collective-permute-start(f32[2,16,320]{2,1,0:T(8,128)} %get-tuple-element.91), channel_id=1, source_target_pairs={{1,0},{2,1},{3,2},{5,4},{6,5},{7,6},{9,8},{10,9},{11,10},{13,12},{... | collective-permute-start | bytes 122888 | tf_op jit(solution)/shard_map/ppermute | solution.py:916
  35.7 10.5 %collective-permute-start.6 = (f32[1,192,384]{2,1,0:T(8,128)S(1)}, f32[1,192,384]{2,1,0:T(8,128)S(1)}, u32[]{:S(2)}, u32[]{:S(2)}) collective-permute-start(f32[1,192,384]{2,1,0:T(8,128)S(1)} %get-tuple-element.101.refs_2_), channel_id=1, source_target_pairs={{0,16},{16,20},{20,4},{4,8},{8,24},{24,28},{28,12},{1,17},{17,21},... | collective-permute-start | bytes 884744 | tf_op jit(solution)/shard_map/ppermute | solution.py:950
  38.1 11.3 %collective-permute-start.7 = (f32[1,192,384]{2,1,0:T(8,128)S(1)}, f32[1,192,384]{2,1,0:T(8,128)S(1)}, u32[]{:S(2)}, u32[]{:S(2)}) collective-permute-start(f32[1,192,384]{2,1,0:T(8,128)S(1)} %get-tuple-element.100.refs_1_), channel_id=1, source_target_pairs={{16,0},{20,16},{4,20},{8,4},{24,8},{28,24},{12,28},{17,1},{21,17},... | collective-permute-start | bytes 884744 | tf_op jit(solution)/shard_map/ppermute | solution.py:951
  49.4 8.3 %collective-permute-start.10 = (f32[10,8,384]{2,1,0:T(8,128)S(1)}, f32[10,8,384]{2,1,0:T(8,128)S(1)}, u32[]{:S(2)}, u32[]{:S(2)}) collective-permute-start(f32[10,8,384]{2,1,0:T(8,128)S(1)} %get-tuple-element.114), channel_id=1, source_target_pairs={{1,0},{2,1},{3,2},{5,4},{6,5},{7,6},{9,8},{10,9},{11,10},{13,12},{... | collective-permute-start | bytes 368648 | tf_op jit(solution)/shard_map/ppermute | solution.py:968
  50.7 7.0 %collective-permute-start.9 = (f32[10,8,384]{2,1,0:T(8,128)S(1)}, f32[10,8,384]{2,1,0:T(8,128)S(1)}, u32[]{:S(2)}, u32[]{:S(2)}) collective-permute-start(f32[10,8,384]{2,1,0:T(8,128)S(1)} %get-tuple-element.113), channel_id=1, source_target_pairs={{0,1},{1,2},{2,3},{4,5},{5,6},{6,7},{8,9},{9,10},{10,11},{12,13},{... | collective-permute-start | bytes 368648 | tf_op jit(solution)/shard_map/ppermute | solution.py:968
  84.1 6.4 %collective-permute-start.17 = (f32[8,128]{1,0:T(8,128)S(1)}, f32[8,128]{1,0:T(8,128)S(1)}, u32[]{:S(2)}, u32[]{:S(2)}) collective-permute-start(f32[8,128]{1,0:T(8,128)S(1)} %add.320), channel_id=1, source_target_pairs={{0,2},{1,3},{2,0},{3,1},{4,6},{5,7},{6,4},{7,5},{8,10},{9,11},{10,... | collective-permute-start | bytes 12296 | tf_op jit(solution)/shard_map/ppermute | solution.py:32
  90.5 7.5 %collective-permute-start.18 = (f32[8,128]{1,0:T(8,128)S(1)}, f32[8,128]{1,0:T(8,128)S(1)}, u32[]{:S(2)}, u32[]{:S(2)}) collective-permute-start(f32[8,128]{1,0:T(8,128)S(1)} %add.321), channel_id=1, source_target_pairs={{0,4},{4,0},{8,12},{12,8},{1,5},{5,1},{9,13},{13,9},{2,6},{6,2},{1... | collective-permute-start | bytes 12296 | tf_op jit(solution)/shard_map/ppermute | solution.py:32
  92.1 19.1 %collective-permute-start.20 = (f16[1,4,4,24,320]{4,3,2,1,0:T(8,128)(2,1)S(1)}, f16[1,4,4,24,320]{4,3,2,1,0:T(8,128)(2,1)S(1)}, u32[]{:S(2)}, u32[]{:S(2)}) collective-permute-start(f16[1,4,4,24,320]{4,3,2,1,0:T(8,128)(2,1)S(1)} %convert_element_type.60), channel_id=1, source_target_pairs={{0,16},{16,0},{1,17},{17,1},{2,18},{18,2},{3,19},{19,3},{4,20},{20... | collective-permute-start | bytes 737288 | tf_op jit(solution)/shard_map/ppermute | solution.py:908
  98.1 13.1 %collective-permute-start.21 = (f16[1,4,4,24,320]{4,3,2,1,0:T(8,128)(2,1)S(1)}, f16[1,4,4,24,320]{4,3,2,1,0:T(8,128)(2,1)S(1)}, u32[]{:S(2)}, u32[]{:S(2)}) collective-permute-start(f16[1,4,4,24,320]{4,3,2,1,0:T(8,128)(2,1)S(1)} %convert_element_type.61), channel_id=1, source_target_pairs={{0,16},{16,0},{1,17},{17,1},{2,18},{18,2},{3,19},{19,3},{4,20},{20... | collective-permute-start | bytes 737288 | tf_op jit(solution)/shard_map/ppermute | solution.py:908
  111.2 8.6 %collective-permute-start.22 = (f32[2,12,160,128]{3,2,1,0:T(8,128)}, f32[2,12,160,128]{3,2,1,0:T(8,128)}, u32[]{:S(2)}, u32[]{:S(2)}) collective-permute-start(f32[2,12,160,128]{3,2,1,0:T(8,128)} %get-tuple-element.164), channel_id=1, source_target_pairs={{0,1},{1,0},{2,3},{3,2},{4,5},{5,4},{6,7},{7,6},{8,9},{9,8},{10,11... | collective-permute-start | bytes 5898248 | tf_op jit(solution)/shard_map/ppermute | solution.py:32
  121.2 8.9 %collective-permute-start.23 = (f16[2,1,6,2,2,40,128]{6,5,4,3,2,1,0:T(8,128)(2,1)S(1)}, f16[2,1,6,2,2,40,128]{6,5,4,3,2,1,0:T(8,128)(2,1)S(1)}, u32[]{:S(2)}, u32[]{:S(2)}) collective-permute-start(f16[2,1,6,2,2,40,128]{6,5,4,3,2,1,0:T(8,128)(2,1)S(1)} %add_convert_fusion), channel_id=1, source_target_pairs={{0,2},{1,5},{2,0},{3,7},{4,6},{5,1},{6,4},{7,3},{8,10},{9,13},{10,... | collective-permute-start | bytes 1474568 | tf_op jit(solution)/shard_map/ppermute | solution.py:823
  131.5 6.3 %collective-permute-start.24 = (f16[2,1,6,1,2,40,128]{6,5,4,3,2,1,0:T(8,128)(2,1)S(1)}, f16[2,1,6,1,2,40,128]{6,5,4,3,2,1,0:T(8,128)(2,1)S(1)}, u32[]{:S(2)}, u32[]{:S(2)}) collective-permute-start(f16[2,1,6,1,2,40,128]{6,5,4,3,2,1,0:T(8,128)(2,1)S(1)} %dynamic-slice_convert_fusion), channel_id=1, source_target_pairs={{0,4},{1,3},{2,6},{3,1},{4,0},{5,7},{6,2},{7,5},{8,12},{9,11},{10,... | collective-permute-start | bytes 737288 | tf_op jit(solution)/shard_map/ppermute | solution.py:823
  138.8 6.0 %collective-permute-start.26 = (f16[1,1,6,1,1,40,128]{6,5,4,3,2,1,0:T(8,128)(2,1)S(1)}, f16[1,1,6,1,1,40,128]{6,5,4,3,2,1,0:T(8,128)(2,1)S(1)}, u32[]{:S(2)}, u32[]{:S(2)}) collective-permute-start(f16[1,1,6,1,1,40,128]{6,5,4,3,2,1,0:T(8,128)(2,1)S(1)} %get-tuple-element.182), channel_id=1, source_target_pairs={{0,8},{4,12},{8,0},{12,4},{16,24},{20,28},{24,16},{28,20},{1,9},{5... | collective-permute-start | bytes 184328 | tf_op jit(solution)/shard_map/ppermute | solution.py:830
  140.9 7.3 %collective-permute-start.27 = (f16[1,1,6,1,1,40,128]{6,5,4,3,2,1,0:T(8,128)(2,1)S(1)}, f16[1,1,6,1,1,40,128]{6,5,4,3,2,1,0:T(8,128)(2,1)S(1)}, u32[]{:S(2)}, u32[]{:S(2)}) collective-permute-start(f16[1,1,6,1,1,40,128]{6,5,4,3,2,1,0:T(8,128)(2,1)S(1)} %get-tuple-element.181), channel_id=1, source_target_pairs={{0,24},{4,28},{8,16},{12,20},{16,8},{20,12},{24,0},{28,4},{1,25},{... | collective-permute-start | bytes 184328 | tf_op jit(solution)/shard_map/ppermute | solution.py:830
  148.3 5.2 %collective-permute-start.28 = (f16[1,1,6,1,1,40,128]{6,5,4,3,2,1,0:T(8,128)(2,1)S(1)}, f16[1,1,6,1,1,40,128]{6,5,4,3,2,1,0:T(8,128)(2,1)S(1)}, u32[]{:S(2)}, u32[]{:S(2)}) collective-permute-start(f16[1,1,6,1,1,40,128]{6,5,4,3,2,1,0:T(8,128)(2,1)S(1)} %add_convert_fusion.1), channel_id=1, source_target_pairs={{0,8},{1,9},{2,10},{3,11},{4,12},{5,13},{6,14},{7,15},{8,0},{9,1},... | collective-permute-start | bytes 184328 | tf_op jit(solution)/shard_map/ppermute | solution.py:823
  148.4 5.1 %collective-permute-start.29 = (f16[1,1,6,1,1,40,128]{6,5,4,3,2,1,0:T(8,128)(2,1)S(1)}, f16[1,1,6,1,1,40,128]{6,5,4,3,2,1,0:T(8,128)(2,1)S(1)}, u32[]{:S(2)}, u32[]{:S(2)}) collective-permute-start(f16[1,1,6,1,1,40,128]{6,5,4,3,2,1,0:T(8,128)(2,1)S(1)} %add_convert_fusion.1), channel_id=1, source_target_pairs={{0,4},{1,3},{2,6},{3,1},{4,0},{5,7},{6,2},{7,5},{8,12},{9,11},{10,... | collective-permute-start | bytes 184328 | tf_op jit(solution)/shard_map/ppermute | solution.py:823
  148.5 7.3 %collective-permute-start.30 = (f16[1,1,6,1,1,40,128]{6,5,4,3,2,1,0:T(8,128)(2,1)S(1)}, f16[1,1,6,1,1,40,128]{6,5,4,3,2,1,0:T(8,128)(2,1)S(1)}, u32[]{:S(2)}, u32[]{:S(2)}) collective-permute-start(f16[1,1,6,1,1,40,128]{6,5,4,3,2,1,0:T(8,128)(2,1)S(1)} %add_convert_fusion.1), channel_id=1, source_target_pairs={{0,12},{1,11},{2,14},{3,9},{4,8},{5,15},{6,10},{7,13},{8,4},{9,3},... | collective-permute-start | bytes 184328 | tf_op jit(solution)/shard_map/ppermute | solution.py:823
  155.9 6.3 %collective-permute-start.31 = (f16[1,1,6,2,2,40,128]{6,5,4,3,2,1,0:T(8,128)(2,1)S(1)}, f16[1,1,6,2,2,40,128]{6,5,4,3,2,1,0:T(8,128)(2,1)S(1)}, u32[]{:S(2)}, u32[]{:S(2)}) collective-permute-start(f16[1,1,6,2,2,40,128]{6,5,4,3,2,1,0:T(8,128)(2,1)S(1)} %pad_maximum_fusion.1), channel_id=1, source_target_pairs={{0,2},{1,5},{2,0},{3,7},{4,6},{5,1},{6,4},{7,3},{8,10},{9,13},{10,... | collective-permute-start | bytes 737288 | tf_op jit(solution)/shard_map/ppermute | solution.py:823
  (30 other events, 319.4 us)

commit v2 on v1

--- a/solution.py
+++ b/solution.py
@@ -570,6 +570,24 @@
     wait_copies(start_copies(pairs, out_sem))
 
 
+def land_kernel(first, ready, place_ref, lat_ref, part_ref, base_hbm, out_hbm, hold_ref, sem):
+    others, steps, count = part_ref.shape[:3]
+    copies = []
+    for i in range(others):
+        at = place_ref[8 + others + i] * place_ref[3] + first
+
+        def add(row, _):
+            own = lat_ref[at + row]
+            for k in range(steps):
+                hold_ref[i, k, row] = own + 8.0 * part_ref[i, k, row]
+            return 0
+
+        lax.fori_loop(0, count, add, 0)
+        copies.append(pltpu.make_async_copy(hold_ref.at[i], out_hbm.at[:, pl.ds(at, count)], sem.at[i]))
+        copies[-1].start()
+    wait_copies(copies)
+
+
 def weight_terms(half, up_t, even_ref, odd_ref, steps, put):
     rows = odd_ref.shape[0] - 2
     span, lanes = odd_ref.shape[1:]
@@ -755,28 +773,38 @@
     return (lax.axis_index(axis) // bit) % 2
 
 
-def half_of_dim(value, which, dim):
-    count = value.shape[dim] // 2
-    return lax.dynamic_slice_in_dim(value, which * count, count, dim)
+def side(which, count=1):
+    unsigned = jnp.uint32
+    return (which * count).astype(unsigned), ((1 - which) * count).astype(unsigned), which == 0
+
+
+def part_of(value, start, count, dim):
+    starts = [start if i == dim else jnp.uint32(0) for i in range(value.ndim)]
+    sizes = [count if i == dim else size for i, size in enumerate(value.shape)]
+    return lax.dynamic_slice(value, starts, sizes)
+
+
+def half_of_dim(value, start, dim):
+    return part_of(value, start, value.shape[dim] // 2, dim)
 
 
 def half_sum(value, mine, send, dim):
-    arrived = send(half_of_dim(value, 1 - mine, dim).astype(F16))
-    return half_of_dim(value, mine, dim) + arrived.astype(value.dtype)
+    arrived = send(half_of_dim(value, mine[1], dim).astype(F16))
+    return half_of_dim(value, mine[0], dim) + arrived.astype(value.dtype)
 
 
 def both_halves(value, mine, send, dim):
     other = send(value)
-    low = jnp.where(mine == 0, value, other)
-    high = jnp.where(mine == 0, other, value)
+    low = jnp.where(mine[2], value, other)
+    high = jnp.where(mine[2], other, value)
     return jnp.concatenate([low, high], axis=dim)
 
 
 def joint_sum(value, sides, dims, sends):
     def quarter(flips):
         part = value
-        for side, dim, flip in zip(sides, dims, flips):
-            part = half_of_dim(part, 1 - side if flip else side, dim)
+        for mine, dim, flip in zip(sides, dims, flips):
+            part = half_of_dim(part, mine[1 if flip else 0], dim)
         return part
 
     total = quarter((0, 0))
@@ -791,9 +819,9 @@
     for flips, send in sends:
         parts[flips] = send(value)
 
-    def order(first, second, side, dim):
-        low = jnp.where(side == 0, first, second)
-        high = jnp.where(side == 0, second, first)
+    def order(first, second, mine, dim):
+        low = jnp.where(mine[2], first, second)
+        high = jnp.where(mine[2], second, first)
         return jnp.concatenate([low, high], axis=dim)
 
     rows = [order(parts[(0, flip)], parts[(1, flip)], sides[0], dims[0]) for flip in (0, 1)]
@@ -803,12 +831,11 @@
 FLIPS = ((1, 0), (0, 1), (1, 1))
 
 
-def reduce_weights(kept, arrived, ready):
+def reduce_weights(kept, arrived, latent, sweeps, travel, land, sides):
     slabs, tiles, share_rows, lanes = kept.shape
     shape = (slabs, 2, tiles // 2, 2, 2, share_rows // 4, lanes)
     pieces = (kept.reshape(shape), arrived.reshape(shape))
     tall, wide = lax.axis_size("sy"), lax.axis_size("sx")
-    even = bit_of("sx", 1) == 0
 
     def turned(sy, sx, turn):
         return (sy, sx ^ 2) if sx % 2 == turn else (sy ^ 1, sx)
@@ -829,31 +856,40 @@
             pairs.append((i, (tm ^ (bit * flip_slab)) * tall + (sy ^ (2 * flip_far))))
         return lambda value: lax.ppermute(value, ("tm", "sy"), pairs)
 
-    mine = [bit_of("sx", 2), bit_of("sy", 1)]
-    first, second = (jnp.where(even, mine[turn], mine[1 - turn]) for turn in (0, 1))
-    far = bit_of("sy", 2)
+    first, second, far, core, *slab_sides = sides
 
     def half(which):
         return sum(half_of_dim(x, which, 1) for x in pieces)
 
-    other = send_tile(0, 1, 0)(half(1 - first).astype(F16))
-    other, ready = lax.optimization_barrier((other, ready))
-    value = half(first) + other.astype(F32)
-    value = half_sum(value, second, send_tile(1, 1, 0), 3)
+    outgoing, latent = lax.optimization_barrier((half(first[1]).astype(F16), latent))
+    other = send_tile(0, 1, 0)(outgoing)
+    other, (base, leaving) = lax.optimization_barrier((other, sweeps[0]((latent,))))
+    value = half(first[0]) + other.astype(F32)
+    landing = travel(leaving)
+    outgoing = half_of_dim(value, second[1], 3).astype(F16)
+    outgoing, latent, base = lax.optimization_barrier((outgoing, latent, base))
+    other = send_tile(1, 1, 0)(outgoing)
+    other, (base, leaving), landing = lax.optimization_barrier((other, sweeps[1]((latent, base)), landing))
+    value = half_of_dim(value, second[0], 3) + other.astype(F32)
     bits = axis_bits(("tm",))[::-1]
-    for axis, bit in bits[:-1]:
-        value = half_sum(value, bit_of(axis, bit), lambda x, bit=bit: swap(x, "tm", bit), 0)
+    for (_, bit), mine in zip(bits[:-1], slab_sides):
+        value = half_sum(value, mine, lambda x, bit=bit: swap(x, "tm", bit), 0)
     if bits:
         sends = [(flips, send_slab(bits[-1][1], *flips)) for flips in FLIPS]
-        value = joint_sum(value, (bit_of(*bits[-1]), far), (0, 4), sends)
+        value = joint_sum(value, (slab_sides[-1], far), (0, 4), sends)
     else:
         value = half_sum(value, far, lambda x: swap(x, "sy", 2), 4)
     value = value.astype(F16)
+    trajectory = land(landing, base, 0)
+    landing = travel(leaving)
     sends = [(flips, send_tile(1, flips[1], flips[0])) for flips in FLIPS]
     value = joint_gather(value, (far, second), (4, 3), sends)
+    value, landing, trajectory = lax.optimization_barrier((value, landing, trajectory))
+    trajectory = land(landing, trajectory, 1)
     value = both_halves(value, first, send_tile(0, 1, 0), 1)
-    value = both_halves(value[None], bit_of("sx", 1), lambda x: swap(x, "sx", 1), 0)
-    return value.astype(F32).reshape(2 * tiles, share_rows, lanes), ready
+    value, trajectory = lax.optimization_barrier((value, trajectory))
+    value = both_halves(value[None], core, lambda x: swap(x, "sx", 1), 0)
+    return value.astype(F32).reshape(2 * tiles, share_rows, lanes), trajectory
 
 
 def shards(
@@ -877,11 +913,26 @@
     tall, wide = lax.axis_size("sy"), lax.axis_size("sx")
     diagonal = [(sy + dy, sx + dx) for dy in (-1, 1) for dx in (-1, 1)]
     corners = [jnp.clip(y, 0, tall - 1) * wide + jnp.clip(x, 0, wide - 1) for y, x in diagonal]
-    place = [half, sx % 2, tm, jnp.int32(rows)] + corners + targets
+    origins = [half_of((tm - offset + slabs) % slabs, sy) for offset in range(1, slabs)]
+    place = [half, sx % 2, tm, jnp.int32(rows)] + corners + targets + origins
     place = jnp.stack(place).astype(jnp.int32)
     flags = [(sy > 0) | (half > 0), (sy < tall - 1) | (half < slabs - 1), sx > 0, sx < wide - 1]
     flags += [(y >= 0) & (y < tall) & (x >= 0) & (x < wide) for y, x in diagonal]
     flags = jnp.stack(flags).astype(F32)
+    turns = [bit_of("sx", 2), bit_of("sy", 1)]
+    core = bit_of("sx", 1)
+    halves = [
+        side(jnp.where(core == 0, turns[0], turns[1])),
+        side(jnp.where(core == 0, turns[1], turns[0])),
+        side(bit_of("sy", 2)),
+        side(core),
+    ]
+    held = slabs
+    for _, bit in axis_bits(("tm",))[::-1]:
+        held //= 2
+        halves.append(side(bit_of("tm", bit), held))
+    cut = rows // 2
+    place, flags, halves, latent_init = lax.optimization_barrier((place, flags, halves, latent_init))
 
     def shifted(offset):
         return [(i, (i + offset) % slabs) for i in range(slabs)]
@@ -910,6 +961,9 @@
 
     down, up = chain("sy")
     right_way, left_way = chain("sx")
+    parts1, low_rows, high_rows, first_cols, last_cols, conv_weight = lax.optimization_barrier(
+        (share(moments, tiles_axes), low_rows, high_rows, first_cols, last_cols, conv_weight)
+    )
     low = lax.ppermute(low_rows, "sy", down)
     high = lax.ppermute(high_rows, "sy", up)
     left = lax.ppermute(last_cols, "sx", right_way)
@@ -917,8 +971,6 @@
     other_tables = to_slabs(jnp.broadcast_to(table[None], (slabs - 1,) + table.shape))
     other_tables, leaving = lax.optimization_barrier((other_tables, leaving))
     others = to_slabs(leaving)
-    parts1 = share(moments, tiles_axes)
-    parts1, conv_weight = lax.optimization_barrier((parts1, conv_weight))
     (coefs,) = call(
         table_kernel, [((4, steps, lanes), F32)], [], 10**5, smem=[place], vmem=[table, other_tables],
         grant=SMALL_BYTES,
@@ -982,8 +1034,8 @@
         return run
 
     order = ("sx", "sy", "tm")
-    cut = max(1, rows // 4)
-    pieces = [(at, min(cut, rows - at)) for at in range(0, rows, cut)]
+    quarter = max(1, rows // 4)
+    pieces = [(at, min(quarter, rows - at)) for at in range(0, rows, quarter)]
 
     def cols_and_first(args):
         return side_cols(args[1:]), act_gradient(*pieces[0])(args[0])
@@ -1043,18 +1095,12 @@
 
         return run
 
-    sums, (late_a, late_b, (base, sent_a), (trajectory, sent_b)) = butterfly(
+    sums, (late_a, late_b) = butterfly(
         sums,
-        ("tm", "sx", "sy"),
+        order,
         join_sums,
-        [
-            late_weight(0),
-            late_weight(1),
-            lambda done: (second_sweep(0, rows // 2), (latent_init,)),
-            lambda done: (second_sweep(rows // 2, rows - rows // 2), (latent_init, done[2][0])),
-        ],
-    )
-    landing = [to_slabs(sent_a.astype(F16)), to_slabs(sent_b.astype(F16))]
+        [late_weight(0), late_weight(1)],
+    )
 
     payload = ((slabs, tiles // 2, share_rows, LANES), F32)
     up_shape = ((channels, rows * span), BF16)
@@ -1079,18 +1125,30 @@
         )
         return kept
 
-    sent, landing = lax.optimization_barrier((sent, landing))
     arrived, kept = beside(sent, "sx", 1, kept_weight, (up_t,))
 
-    cut = rows // 2
-    for offset in range(1, slabs):
-        source = half_of((tm - offset) % slabs, sy) * rows
-        for part, at, count in zip(landing, (0, cut), (cut, rows - cut)):
-            own = lax.dynamic_slice_in_dim(latent_init, source + at, count, 0)
-            part = own[None] + 8.0 * part[offset - 1].astype(F32)
-            trajectory = lax.dynamic_update_slice_in_dim(trajectory, part, source + at, 1)
-
-    summed, trajectory = reduce_weights(kept, arrived, trajectory)
+    def land(part, trajectory, which):
+        (trajectory,) = call(
+            functools.partial(land_kernel, (0, cut)[which]),
+            [(step_noise.shape, F32, pltpu.HBM)],
+            [(part.shape, F32), pltpu.SemaphoreType.DMA((slabs - 1,))],
+            10**6,
+            smem=[place],
+            vmem=[latent_init, part.astype(F32)],
+            hbm=[trajectory],
+            aliases={3: 0},
+        )
+        return trajectory
+
+    summed, trajectory = reduce_weights(
+        kept,
+        arrived,
+        latent_init,
+        (second_sweep(0, cut), second_sweep(cut, rows - cut)),
+        lambda leaving: to_slabs(leaving.astype(F16)),
+        land,
+        halves,
+    )
     (grad,) = call(
         unpack_kernel, [((9, share_rows, channels), F32)], [], 10**6, vmem=[summed, scales],
         grant=SMALL_BYTES,

time: 168 us -> 169 us (level)
  starting transfers between devices: 52.8 us -> 57.1 us
  waiting for transfers between devices: 41.4 us -> 38.7 us
  other arithmetic: 6.12 us -> 3.5 us
    ppermute x6, waiting for transfers between devices: 20.9 us -> 12.5 us  [send_tile(): return lambda value: lax.ppermute(value, ('sy', 'sx'), pairs)]
    ppermute x12, waiting for transfers between devices: 8.69 us -> 14.7 us  [swap(): return lax.ppermute(value, axis, pairs)]
    all_to_all x1, waiting for transfers between devices: 0.04 us -> 4.45 us  [share(): return lax.all_to_all(copies, axes, 0, 0)]
    ppermute x1, waiting for transfers between devices: 3.22 us -> 0.01 us  [shards(): bottom = lax.ppermute(first_row, ('tm', 'sy'), up_rows)]
    ppermute x1, starting transfers between devices: 2.46 us -> 4.56 us  [shards(): top = lax.ppermute(last_row, ('tm', 'sy'), down_rows)]
    ppermute x1, starting transfers between devices: 3.82 us -> 1.92 us  [shards(): low = lax.ppermute(low_rows, 'sy', down)]
    dynamic_update_slice x2 -> x0, other arithmetic: 1.75 us -> none  [shards(): lax.dynamic_update_slice_in_dim(trajectory, part, source + at, 1)]
    pallas_call x18 -> x20, Pallas kernels: 54.7 us -> 56.3 us  [call(): pl.pallas_call(body, out_shape=shapes, in_specs=specs, out_specs=out_spec...]
  transfers between devices with their start and end apart: 34 -> 34, of which waited for: 14 -> 15; matrix products, arithmetic and copies ran while one was open for 1% -> 1% of each run, Pallas kernels for 24% -> 22%
where the time goes in v2:
time: 169 us; the launch traced here: 168 us
  starting transfers between devices  57.1 us (34%)
  Pallas kernels  56.3 us (33%)
  waiting for transfers between devices  38.7 us (23%)
  local copies, waits for them, and re-layouts  10.9 us (6%)
  other arithmetic  3.5 us (2%)
    pallas_call x20, Pallas kernels, call(): pl.pallas_call(body, out_shape=shapes, in_specs=specs, out_specs=out_spec...  56.3 us
    ppermute x12, starting transfers between devices, swap(): return lax.ppermute(value, axis, pairs)  15.9 us
    ppermute x12, waiting for transfers between devices, swap(): return lax.ppermute(value, axis, pairs)  14.7 us
    ppermute x6, waiting for transfers between devices, send_tile(): return lambda value: lax.ppermute(value, ('sy', 'sx'), pairs)  12.5 us
    unnamed x40, local copies, waits for them, and re-layouts  10.2 us
    all_to_all x1, starting transfers between devices, share(): return lax.all_to_all(copies, axes, 0, 0)  7.53 us
    ppermute x6, starting transfers between devices, send_tile(): return lambda value: lax.ppermute(value, ('sy', 'sx'), pairs)  7.17 us
    ppermute x4, starting transfers between devices, to_slabs(): return lax.ppermute(pieces, 'tm', shifted(1))  5.13 us
  transfers between devices with their start and end apart: 34, of which 15 were waited for; matrix products, arithmetic and copies ran while one was open for 1% of the time, Pallas kernels for 22%

profile of v2, /device:TPU:0, one launch (start us, length us, event | category | flops | bytes accessed | tf_op | source)
XLA Modules:
  0.0 168.1 jit_solution(7581095483994604063)
XLA Ops:
  1.5 5.3 %shard_map.113 = (f32[16,32,128]{2,1,0:T(8,128)}, f32[4,4,384]{2,1,0:T(4,128)}, f32[2,24,320]{2,1,0:T(8,128)}, f32[2,24,320]{2,1,0:T(8,128)}, f32[2,16,320]{2,1,...) custom-call(s32[4]{0:T(128)} %refs_0_.1, s32[10]{0:T(128)} %stack.88.refs_1_.refs_0_, f32[4]{0:T(128)} %refs_2_.1, ...), custom_call_target="tpu_custom_call" | custom-call | flops 1000000 | bytes 4230504 | tf_op jit(solution)/shard_map/pallas_call | solution.py:757
  6.9 7.5 %all-to-all-start = ((f32[16,32,128]{2,1,0:T(8,128)}), f32[16,32,128]{2,1,0:T(8,128)S(1)}, u32[]{:S(2)}, u32[]{:S(2)}) async-start(f32[16,32,128]{2,1,0:T(8,128)} %get-tuple-element.114), calls=%async_computation | async-start | bytes 524288 | tf_op jit(solution)/shard_map/all_to_all | solution.py:41
  16.0 2.5 %collective-permute-done.4.refs_2_ = f32[1,4,4,384]{3,2,1,0:T(4,128)S(1)} collective-permute-done((f32[1,4,4,384]{3,2,1,0:T(4,128)}, f32[1,4,4,384]{3,2,1,0:T(4,128)S(1)}, u32[]{:S(2)}, u32[]{:S(2)}) %collective-permute-start.4) | collective-permute-done | bytes 24608 | tf_op jit(solution)/shard_map/ppermute | solution.py:959
  20.0 4.5 %all-to-all-done.refs_6_ = f32[16,32,128]{2,1,0:T(8,128)S(1)} async-done(((f32[16,32,128]{2,1,0:T(8,128)}), f32[16,32,128]{2,1,0:T(8,128)S(1)}, u32[]{:S(2)}, u32[]{:S(2)}) %all-to-all-start) | async-done | bytes 262176 | tf_op jit(solution)/shard_map/all_to_all | solution.py:41
  27.7 2.3 %collective-permute-start.2 = (f32[2,16,320]{2,1,0:T(8,128)}, f32[2,16,320]{2,1,0:T(8,128)S(1)}, u32[]{:S(2)}, u32[]{:S(2)}) collective-permute-start(f32[2,16,320]{2,1,0:T(8,128)} %get-tuple-element.121), channel_id=1, source_target_pairs={{0,1},{1,2},{2,3},{4,5},{5,6},{6,7},{8,9},{9,10},{10,11},{12,13},{... | collective-permute-start | bytes 122888 | tf_op jit(solution)/shard_map/ppermute | solution.py:969
  35.9 4.0 %shard_map.116 = (bf16[10,208,384]{2,1,0:T(8,128)(2,1)S(1)}, bf16[10,192,384]{2,1,0:T(8,128)(2,1)S(1)}, f32[2,2,18,384]{3,2,1,0:T(8,128)S(1)}, f32[1,192,384]{2,1,0:T(8,128)S(1)}, f32[1,192,384]{2,1,0:T(8,128)S(1)}) custom-call(f32[8]{0:T(128)S(1)} %convert_element_type.83.refs_0_, s32[10]{0:T(128)S(1)} %copy-done.16, ...), custom_call_target="tpu_custom_call" | custom-call | flops 707788800 | bytes 8515656 | tf_op jit(solution)/shard_map/pallas_call | solution.py:757
  41.3 4.6 %collective-permute-start.6 = (f32[1,192,384]{2,1,0:T(8,128)S(1)}, f32[1,192,384]{2,1,0:T(8,128)S(1)}, u32[]{:S(2)}, u32[]{:S(2)}) collective-permute-start(f32[1,192,384]{2,1,0:T(8,128)S(1)} %get-tuple-element.131.refs_2_), channel_id=1, source_target_pairs={{0,16},{16,20},{20,4},{4,8},{8,24},{24,28},{28,12},{1,17},{17,21},... | collective-permute-start | bytes 884744 | tf_op jit(solution)/shard_map/ppermute | solution.py:1002
  46.9 6.7 %shard_map.117 = (f32[8,192,384]{2,1,0:T(8,128)S(1)}, f32[2,8,128]{2,1,0:T(8,128)S(1)}, f32[8,8,384]{2,1,0:T(8,128)S(1)}, f32[8,8,384]{2,1,0:T(8,128)S(1)}) custom-call(s32[10]{0:T(128)S(1)} %copy-done.16, f32[1,192,384]{2,1,0:T(8,128)S(1)} %get-tuple-element.130.refs_1_, f32[1,192,384]{2,1,0:T(8,128)S(1)} %get-tuple-element.131.refs_2_, ...), custom_call_target="tpu_custom_call" | custom-call | flops 2831155200 | bytes 10502184 | tf_op jit(solution)/shard_map/pallas_call | solution.py:757
  53.7 2.8 %collective-permute-start.9 = (f32[10,8,384]{2,1,0:T(8,128)S(1)}, f32[10,8,384]{2,1,0:T(8,128)S(1)}, u32[]{:S(2)}, u32[]{:S(2)}) collective-permute-start(f32[10,8,384]{2,1,0:T(8,128)S(1)} %get-tuple-element.143), channel_id=1, source_target_pairs={{0,1},{1,2},{2,3},{4,5},{5,6},{6,7},{8,9},{9,10},{10,11},{12,13},{... | collective-permute-start | bytes 368648 | tf_op jit(solution)/shard_map/ppermute | solution.py:1020
  58.0 3.0 %collective-permute-start.8 = (f32[2,8,128]{2,1,0:T(8,128)S(1)}, f32[2,8,128]{2,1,0:T(8,128)S(1)}, u32[]{:S(2)}, u32[]{:S(2)}) collective-permute-start(f32[2,8,128]{2,1,0:T(8,128)S(1)} %get-tuple-element.138), channel_id=1, source_target_pairs={{0,1},{1,0},{2,3},{3,2},{4,5},{5,4},{6,7},{7,6},{8,9},{9,8},{10,11... | collective-permute-start | bytes 24584 | tf_op jit(solution)/shard_map/ppermute | solution.py:32
  67.1 2.7 %collective-permute-start.12 = (f32[2,8,128]{2,1,0:T(8,128)S(1)}, f32[2,8,128]{2,1,0:T(8,128)S(1)}, u32[]{:S(2)}, u32[]{:S(2)}) collective-permute-start(f32[2,8,128]{2,1,0:T(8,128)S(1)} %pad_maximum_fusion.6), channel_id=1, source_target_pairs={{0,4},{4,0},{8,12},{12,8},{1,5},{5,1},{9,13},{13,9},{2,6},{6,2},{1... | collective-permute-start | bytes 24584 | tf_op jit(solution)/shard_map/ppermute | solution.py:32
  80.3 3.4 %shard_map.123 = (bf16[10,208,384]{2,1,0:T(8,128)(2,1)S(1)}, bf16[10,192,384]{2,1,0:T(8,128)(2,1)S(1)}, f32[8,192,384]{2,1,0:T(8,128)S(1)}, f32[8,128]{1,0:T(8,128)S(1)}, f32[2,8,384]{2,1,0:T(8,128)S(1)}) custom-call(f32[8]{0:T(128)S(1)} %convert_element_type.83.refs_0_, s32[10]{0:T(128)S(1)} %copy-done.16, f32[2,8,128]{2,1,0:T(8,128)S(1)} %pad_maximum_fusion.9.refs_2_, ...), custom_call_target="tpu_custom_call" | custom-call | flops 23592960 | bytes 11563080 | tf_op jit(solution)/shard_map/pallas_call | solution.py:757
  83.7 2.3 %shard_map.124.refs_9_.refs_6_ = f32[12,320,128]{2,1,0:T(8,128)S(1)} custom-call(s32[10]{0:T(128)S(1)} %copy-done.16, f32[16,24,320]{2,1,0:T(8,128)S(1)} %copy-done, f32[4,8,384]{2,1,0:T(8,128)S(1)} %shard_map.114.refs_7_.refs_5_.refs_2_.refs_4_.refs_1_, bf16[10,208,384]{2,1,0:T(8,128)(2,1)S(1)} %get-tuple-element.168.refs_3_.refs_6_, ...), custom_call_target="tpu_custom_call" | custom-call | flops 1415577600 | bytes 5578792 | tf_op jit(solution)/shard_map/pallas_call | solution.py:757
  87.6 2.3 %shard_map.125.refs_10_.refs_7_ = f32[12,320,128]{2,1,0:T(8,128)S(1)} custom-call(s32[10]{0:T(128)S(1)} %copy-done.16, f32[16,24,320]{2,1,0:T(8,128)S(1)} %copy-done, f32[4,8,384]{2,1,0:T(8,128)S(1)} %shard_map.114.refs_7_.refs_5_.refs_2_.refs_4_.refs_1_, bf16[10,208,384]{2,1,0:T(8,128)(2,1)S(1)} %get-tuple-element.168.refs_3_.refs_6_, ...), custom_call_target="tpu_custom_call" | custom-call | flops 1415577600 | bytes 5578792 | tf_op jit(solution)/shard_map/pallas_call | solution.py:757
  94.7 3.4 %collective-permute-done.18 = f32[8,128]{1,0:T(8,128)S(1)} collective-permute-done((f32[8,128]{1,0:T(8,128)S(1)}, f32[8,128]{1,0:T(8,128)S(1)}, u32[]{:S(2)}, u32[]{:S(2)}) %collective-permute-start.18) | collective-permute-done | bytes 4128 | tf_op jit(solution)/shard_map/ppermute | solution.py:32
  101.7 5.1 %shard_map.126 = (f32[2,12,160,128]{3,2,1,0:T(8,128)S(1)}, f32[16,128]{1,0:T(8,128)S(1)}, bf16[320,1536]{1,0:T(8,128)(2,1)S(1)}) custom-call(s32[10]{0:T(128)S(1)} %copy-done.16, f32[8,192,384]{2,1,0:T(8,128)S(1)} %get-tuple-element.134.refs_9_.refs_1_.refs_3_, f32[2,8,384]{2,1,0:T(8,128)S(1)} %get-tuple-element.164.refs_2_, f32[8,128]{1,0:T(8,128)S(1)} %add.262.refs_3_, ...), custom_call_target="tpu_custom_call" | custom-call | flops 1415577600 | bytes 1000000 | tf_op jit(solution)/shard_map/pallas_call | solution.py:757
  107.0 2.3 %shard_map.127 = f32[2,12,160,128]{3,2,1,0:T(8,128)S(1)} custom-call(s32[10]{0:T(128)S(1)} %copy-done.16, bf16[320,1536]{1,0:T(8,128)(2,1)S(1)} %get-tuple-element.180.refs_1_, f32[4,8,384]{2,1,0:T(8,128)S(1)} %shard_map.114.refs_7_.refs_5_.refs_2_.refs_4_.refs_1_, f32[16,128]{1,0:T(8,128)S(1)} %get-tuple-element.181.refs_3_.refs_1_, ...), custom_call_target="tpu_custom_call" | custom-call | flops 1415577600 | bytes 10010664 | tf_op jit(solution)/shard_map/pallas_call | solution.py:757
  112.3 4.9 %shard_map.128 = (f32[4,16,24,320]{3,2,1,0:T(8,128)}, f32[1,4,4,24,320]{4,3,2,1,0:T(8,128)S(1)}) custom-call(s32[10]{0:T(128)S(1)} %copy-done.16, f32[4,8,384]{2,1,0:T(8,128)S(1)} %shard_map.114.refs_7_.refs_5_.refs_2_.refs_4_.refs_1_, f32[16,24,320]{2,1,0:T(8,128)S(1)} %copy-done.5, f32[8,192,384]{2,1,0:T(8,128)S(1)} %get-tuple-element.134.refs_9_.refs_1_.refs_3_, ...), custom_call_target="tpu_custom_call" | custom-call | flops 1415577600 | bytes 12165160 | tf_op jit(solution)/shard_map/pallas_call | solution.py:757
  117.2 2.8 %collective-permute-done.21 = f16[2,1,6,2,2,40,128]{6,5,4,3,2,1,0:T(8,128)(2,1)S(1)} collective-permute-done((f16[2,1,6,2,2,40,128]{6,5,4,3,2,1,0:T(8,128)(2,1)S(1)}, f16[2,1,6,2,2,40,128]{6,5,4,3,2,1,0:T(8,128)(2,1)S(1)}, u32[]{:S(2)}, u32[]{:S(2)}) %collective-permute-start.21) | collective-permute-done | bytes 491552 | tf_op jit(solution)/shard_map/ppermute | solution.py:850
  131.5 4.9 %shard_map.129 = (f32[4,16,24,320]{3,2,1,0:T(8,128)}, f32[1,4,4,24,320]{4,3,2,1,0:T(8,128)S(1)}) custom-call(s32[10]{0:T(128)S(1)} %copy-done.16, f32[4,8,384]{2,1,0:T(8,128)S(1)} %shard_map.114.refs_7_.refs_5_.refs_2_.refs_4_.refs_1_, f32[16,24,320]{2,1,0:T(8,128)S(1)} %copy-done.5, ...), custom_call_target="tpu_custom_call", output_to_operand_aliasing={{0}: (9, {})} | custom-call | flops 1415577600 | bytes 14131240 | tf_op jit(solution)/shard_map/pallas_call | solution.py:757
  137.1 2.6 %collective-permute-start.26 = (f16[1,1,6,1,1,40,128]{6,5,4,3,2,1,0:T(8,128)(2,1)S(1)}, f16[1,1,6,1,1,40,128]{6,5,4,3,2,1,0:T(8,128)(2,1)S(1)}, u32[]{:S(2)}, u32[]{:S(2)}) collective-permute-start(f16[1,1,6,1,1,40,128]{6,5,4,3,2,1,0:T(8,128)(2,1)S(1)} %get-tuple-element.219), channel_id=1, source_target_pairs={{0,24},{4,28},{8,16},{12,20},{16,8},{20,12},{24,0},{28,4},{1,25},{... | collective-permute-start | bytes 184328 | tf_op jit(solution)/shard_map/ppermute | solution.py:857
  141.0 3.5 %collective-permute-done.26 = f16[1,1,6,1,1,40,128]{6,5,4,3,2,1,0:T(8,128)(2,1)S(1)} collective-permute-done((f16[1,1,6,1,1,40,128]{6,5,4,3,2,1,0:T(8,128)(2,1)S(1)}, f16[1,1,6,1,1,40,128]{6,5,4,3,2,1,0:T(8,128)(2,1)S(1)}, u32[]{:S(2)}, u32[]{:S(2)}) %collective-permute-start.26) | collective-permute-done | bytes 61472 | tf_op jit(solution)/shard_map/ppermute | solution.py:857
  152.7 4.3 %collective-permute-done.29 = f16[1,1,6,1,1,40,128]{6,5,4,3,2,1,0:T(8,128)(2,1)S(1)} collective-permute-done((f16[1,1,6,1,1,40,128]{6,5,4,3,2,1,0:T(8,128)(2,1)S(1)}, f16[1,1,6,1,1,40,128]{6,5,4,3,2,1,0:T(8,128)(2,1)S(1)}, u32[]{:S(2)}, u32[]{:S(2)}) %collective-permute-start.29) | collective-permute-done | bytes 61472 | tf_op jit(solution)/shard_map/ppermute | solution.py:850
  158.8 4.7 %collective-permute-done.31 = f16[1,1,6,2,2,40,128]{6,5,4,3,2,1,0:T(8,128)(2,1)S(1)} collective-permute-done((f16[1,1,6,2,2,40,128]{6,5,4,3,2,1,0:T(8,128)(2,1)S(1)}, f16[1,1,6,2,2,40,128]{6,5,4,3,2,1,0:T(8,128)(2,1)S(1)}, u32[]{:S(2)}, u32[]{:S(2)}) %collective-permute-start.31) | collective-permute-done | bytes 245792 | tf_op jit(solution)/shard_map/ppermute | solution.py:850
  (141 shorter events, 74.1 us)
Async XLA Ops:
  6.9 17.6 %all-to-all-start = ((f32[16,32,128]{2,1,0:T(8,128)}), f32[16,32,128]{2,1,0:T(8,128)S(1)}, u32[]{:S(2)}, u32[]{:S(2)}) async-start(f32[16,32,128]{2,1,0:T(8,128)} %get-tuple-element.114), calls=%async_computation | async-start | bytes 524288 | tf_op jit(solution)/shard_map/all_to_all | solution.py:41
  18.5 17.3 %collective-permute-start.5 = (bf16[1,4,8,24,320]{4,3,2,1,0:T(8,128)(2,1)}, bf16[1,4,8,24,320]{4,3,2,1,0:T(8,128)(2,1)S(1)}, u32[]{:S(2)}, u32[]{:S(2)}) collective-permute-start(bf16[1,4,8,24,320]{4,3,2,1,0:T(8,128)(2,1)} %get-tuple-element.127), channel_id=1, source_target_pairs={{0,16},{16,0},{1,17},{17,1},{2,18},{18,2},{3,19},{19,3},{4,20},{20... | collective-permute-start | bytes 1474568 | tf_op jit(solution)/shard_map/ppermute | solution.py:959
  24.5 11.4 %collective-permute-start = (f32[2,24,320]{2,1,0:T(8,128)}, f32[2,24,320]{2,1,0:T(8,128)S(1)}, u32[]{:S(2)}, u32[]{:S(2)}) collective-permute-start(f32[2,24,320]{2,1,0:T(8,128)} %get-tuple-element.119), channel_id=1, source_target_pairs={{0,4},{4,8},{8,12},{1,5},{5,9},{9,13},{2,6},{6,10},{10,14},{3,7},{... | collective-permute-start | bytes 184328 | tf_op jit(solution)/shard_map/ppermute | solution.py:967
  26.4 9.5 %collective-permute-start.1 = (f32[2,24,320]{2,1,0:T(8,128)}, f32[2,24,320]{2,1,0:T(8,128)S(1)}, u32[]{:S(2)}, u32[]{:S(2)}) collective-permute-start(f32[2,24,320]{2,1,0:T(8,128)} %get-tuple-element.120), channel_id=1, source_target_pairs={{4,0},{8,4},{12,8},{5,1},{9,5},{13,9},{6,2},{10,6},{14,10},{7,3},{... | collective-permute-start | bytes 184328 | tf_op jit(solution)/shard_map/ppermute | solution.py:968
  27.7 8.2 %collective-permute-start.2 = (f32[2,16,320]{2,1,0:T(8,128)}, f32[2,16,320]{2,1,0:T(8,128)S(1)}, u32[]{:S(2)}, u32[]{:S(2)}) collective-permute-start(f32[2,16,320]{2,1,0:T(8,128)} %get-tuple-element.121), channel_id=1, source_target_pairs={{0,1},{1,2},{2,3},{4,5},{5,6},{6,7},{8,9},{9,10},{10,11},{12,13},{... | collective-permute-start | bytes 122888 | tf_op jit(solution)/shard_map/ppermute | solution.py:969
  30.0 5.8 %collective-permute-start.3 = (f32[2,16,320]{2,1,0:T(8,128)}, f32[2,16,320]{2,1,0:T(8,128)S(1)}, u32[]{:S(2)}, u32[]{:S(2)}) collective-permute-start(f32[2,16,320]{2,1,0:T(8,128)} %get-tuple-element.122), channel_id=1, source_target_pairs={{1,0},{2,1},{3,2},{5,4},{6,5},{7,6},{9,8},{10,9},{11,10},{13,12},{... | collective-permute-start | bytes 122888 | tf_op jit(solution)/shard_map/ppermute | solution.py:970
  40.0 13.7 %collective-permute-start.7 = (f32[1,192,384]{2,1,0:T(8,128)S(1)}, f32[1,192,384]{2,1,0:T(8,128)S(1)}, u32[]{:S(2)}, u32[]{:S(2)}) collective-permute-start(f32[1,192,384]{2,1,0:T(8,128)S(1)} %get-tuple-element.130.refs_1_), channel_id=1, source_target_pairs={{16,0},{20,16},{4,20},{8,4},{24,8},{28,24},{12,28},{17,1},{21,17},... | collective-permute-start | bytes 884744 | tf_op jit(solution)/shard_map/ppermute | solution.py:1003
  41.3 12.4 %collective-permute-start.6 = (f32[1,192,384]{2,1,0:T(8,128)S(1)}, f32[1,192,384]{2,1,0:T(8,128)S(1)}, u32[]{:S(2)}, u32[]{:S(2)}) collective-permute-start(f32[1,192,384]{2,1,0:T(8,128)S(1)} %get-tuple-element.131.refs_2_), channel_id=1, source_target_pairs={{0,16},{16,20},{20,4},{4,8},{8,24},{24,28},{28,12},{1,17},{17,21},... | collective-permute-start | bytes 884744 | tf_op jit(solution)/shard_map/ppermute | solution.py:1002
  53.7 9.4 %collective-permute-start.9 = (f32[10,8,384]{2,1,0:T(8,128)S(1)}, f32[10,8,384]{2,1,0:T(8,128)S(1)}, u32[]{:S(2)}, u32[]{:S(2)}) collective-permute-start(f32[10,8,384]{2,1,0:T(8,128)S(1)} %get-tuple-element.143), channel_id=1, source_target_pairs={{0,1},{1,2},{2,3},{4,5},{5,6},{6,7},{8,9},{9,10},{10,11},{12,13},{... | collective-permute-start | bytes 368648 | tf_op jit(solution)/shard_map/ppermute | solution.py:1020
  56.5 6.6 %collective-permute-start.10 = (f32[10,8,384]{2,1,0:T(8,128)S(1)}, f32[10,8,384]{2,1,0:T(8,128)S(1)}, u32[]{:S(2)}, u32[]{:S(2)}) collective-permute-start(f32[10,8,384]{2,1,0:T(8,128)S(1)} %get-tuple-element.144), channel_id=1, source_target_pairs={{1,0},{2,1},{3,2},{5,4},{6,5},{7,6},{9,8},{10,9},{11,10},{13,12},{... | collective-permute-start | bytes 368648 | tf_op jit(solution)/shard_map/ppermute | solution.py:1020
  58.0 5.1 %collective-permute-start.8 = (f32[2,8,128]{2,1,0:T(8,128)S(1)}, f32[2,8,128]{2,1,0:T(8,128)S(1)}, u32[]{:S(2)}, u32[]{:S(2)}) collective-permute-start(f32[2,8,128]{2,1,0:T(8,128)S(1)} %get-tuple-element.138), channel_id=1, source_target_pairs={{0,1},{1,0},{2,3},{3,2},{4,5},{5,4},{6,7},{7,6},{8,9},{9,8},{10,11... | collective-permute-start | bytes 24584 | tf_op jit(solution)/shard_map/ppermute | solution.py:32
  67.1 4.8 %collective-permute-start.12 = (f32[2,8,128]{2,1,0:T(8,128)S(1)}, f32[2,8,128]{2,1,0:T(8,128)S(1)}, u32[]{:S(2)}, u32[]{:S(2)}) collective-permute-start(f32[2,8,128]{2,1,0:T(8,128)S(1)} %pad_maximum_fusion.6), channel_id=1, source_target_pairs={{0,4},{4,0},{8,12},{12,8},{1,5},{5,1},{9,13},{13,9},{2,6},{6,2},{1... | collective-permute-start | bytes 24584 | tf_op jit(solution)/shard_map/ppermute | solution.py:32
  71.9 4.6 %collective-permute-start.13 = (f32[2,8,128]{2,1,0:T(8,128)S(1)}, f32[2,8,128]{2,1,0:T(8,128)S(1)}, u32[]{:S(2)}, u32[]{:S(2)}) collective-permute-start(f32[2,8,128]{2,1,0:T(8,128)S(1)} %pad_maximum_fusion.7), channel_id=1, source_target_pairs={{0,8},{4,12},{8,0},{12,4},{1,9},{5,13},{9,1},{13,5},{2,10},{6,14},... | collective-permute-start | bytes 24584 | tf_op jit(solution)/shard_map/ppermute | solution.py:32
  93.6 4.5 %collective-permute-start.18 = (f32[8,128]{1,0:T(8,128)S(1)}, f32[8,128]{1,0:T(8,128)S(1)}, u32[]{:S(2)}, u32[]{:S(2)}) collective-permute-start(f32[8,128]{1,0:T(8,128)S(1)} %add.260), channel_id=1, source_target_pairs={{0,8},{4,12},{8,0},{12,4},{1,9},{5,13},{9,1},{13,5},{2,10},{6,14},... | collective-permute-start | bytes 12296 | tf_op jit(solution)/shard_map/ppermute | solution.py:32
  111.0 8.9 %collective-permute-start.21 = (f16[2,1,6,2,2,40,128]{6,5,4,3,2,1,0:T(8,128)(2,1)S(1)}, f16[2,1,6,2,2,40,128]{6,5,4,3,2,1,0:T(8,128)(2,1)S(1)}, u32[]{:S(2)}, u32[]{:S(2)}) collective-permute-start(f16[2,1,6,2,2,40,128]{6,5,4,3,2,1,0:T(8,128)(2,1)S(1)} %add_convert_fusion), channel_id=1, source_target_pairs={{0,2},{1,5},{2,0},{3,7},{4,6},{5,1},{6,4},{7,3},{8,10},{9,13},{10,... | collective-permute-start | bytes 1474568 | tf_op jit(solution)/shard_map/ppermute | solution.py:850
  121.0 15.4 %collective-permute-start.22 = (f16[2,1,6,1,2,40,128]{6,5,4,3,2,1,0:T(8,128)(2,1)}, f16[2,1,6,1,2,40,128]{6,5,4,3,2,1,0:T(8,128)(2,1)S(1)}, u32[]{:S(2)}, u32[]{:S(2)}) collective-permute-start(f16[2,1,6,1,2,40,128]{6,5,4,3,2,1,0:T(8,128)(2,1)} %dynamic-slice_convert_fusion), channel_id=1, source_target_pairs={{0,4},{1,3},{2,6},{3,1},{4,0},{5,7},{6,2},{7,5},{8,12},{9,11},{10,... | collective-permute-start | bytes 737288 | tf_op jit(solution)/shard_map/ppermute | solution.py:850
  123.2 13.2 %collective-permute-start.23 = (f16[1,4,4,24,320]{4,3,2,1,0:T(8,128)(2,1)}, f16[1,4,4,24,320]{4,3,2,1,0:T(8,128)(2,1)S(1)}, u32[]{:S(2)}, u32[]{:S(2)}) collective-permute-start(f16[1,4,4,24,320]{4,3,2,1,0:T(8,128)(2,1)} %convert_element_type.95), channel_id=1, source_target_pairs={{0,16},{16,0},{1,17},{17,1},{2,18},{18,2},{3,19},{19,3},{4,20},{20... | collective-permute-start | bytes 737288 | tf_op jit(solution)/shard_map/ppermute | solution.py:959
  136.5 4.5 %collective-permute-start.24 = (f16[1,1,6,1,1,40,128]{6,5,4,3,2,1,0:T(8,128)(2,1)S(1)}, f16[1,1,6,1,1,40,128]{6,5,4,3,2,1,0:T(8,128)(2,1)S(1)}, u32[]{:S(2)}, u32[]{:S(2)}) collective-permute-start(f16[1,1,6,1,1,40,128]{6,5,4,3,2,1,0:T(8,128)(2,1)S(1)} %get-tuple-element.218), channel_id=1, source_target_pairs={{0,16},{4,20},{8,24},{12,28},{16,0},{20,4},{24,8},{28,12},{1,17},{... | collective-permute-start | bytes 184328 | tf_op jit(solution)/shard_map/ppermute | solution.py:857
  137.1 7.4 %collective-permute-start.26 = (f16[1,1,6,1,1,40,128]{6,5,4,3,2,1,0:T(8,128)(2,1)S(1)}, f16[1,1,6,1,1,40,128]{6,5,4,3,2,1,0:T(8,128)(2,1)S(1)}, u32[]{:S(2)}, u32[]{:S(2)}) collective-permute-start(f16[1,1,6,1,1,40,128]{6,5,4,3,2,1,0:T(8,128)(2,1)S(1)} %get-tuple-element.219), channel_id=1, source_target_pairs={{0,24},{4,28},{8,16},{12,20},{16,8},{20,12},{24,0},{28,4},{1,25},{... | collective-permute-start | bytes 184328 | tf_op jit(solution)/shard_map/ppermute | solution.py:857
  139.7 5.7 %collective-permute-start.25 = (f16[1,1,6,1,1,40,128]{6,5,4,3,2,1,0:T(8,128)(2,1)S(1)}, f16[1,1,6,1,1,40,128]{6,5,4,3,2,1,0:T(8,128)(2,1)S(1)}, u32[]{:S(2)}, u32[]{:S(2)}) collective-permute-start(f16[1,1,6,1,1,40,128]{6,5,4,3,2,1,0:T(8,128)(2,1)S(1)} %get-tuple-element.220), channel_id=1, source_target_pairs={{0,8},{4,12},{8,0},{12,4},{16,24},{20,28},{24,16},{28,20},{1,9},{5... | collective-permute-start | bytes 184328 | tf_op jit(solution)/shard_map/ppermute | solution.py:857
  145.5 6.5 %collective-permute-start.27 = (f16[1,1,6,1,1,40,128]{6,5,4,3,2,1,0:T(8,128)(2,1)S(1)}, f16[1,1,6,1,1,40,128]{6,5,4,3,2,1,0:T(8,128)(2,1)S(1)}, u32[]{:S(2)}, u32[]{:S(2)}) collective-permute-start(f16[1,1,6,1,1,40,128]{6,5,4,3,2,1,0:T(8,128)(2,1)S(1)} %add_convert_fusion.1), channel_id=1, source_target_pairs={{0,8},{1,9},{2,10},{3,11},{4,12},{5,13},{6,14},{7,15},{8,0},{9,1},... | collective-permute-start | bytes 184328 | tf_op jit(solution)/shard_map/ppermute | solution.py:850
  146.4 10.9 %collective-permute-start.30 = (f16[1,4,4,24,320]{4,3,2,1,0:T(8,128)(2,1)S(1)}, f16[1,4,4,24,320]{4,3,2,1,0:T(8,128)(2,1)S(1)}, u32[]{:S(2)}, u32[]{:S(2)}) collective-permute-start(f16[1,4,4,24,320]{4,3,2,1,0:T(8,128)(2,1)S(1)} %convert_element_type.104), channel_id=1, source_target_pairs={{0,16},{16,0},{1,17},{17,1},{2,18},{18,2},{3,19},{19,3},{4,20},{20... | collective-permute-start | bytes 737288 | tf_op jit(solution)/shard_map/ppermute | solution.py:959
  150.5 6.6 %collective-permute-start.29 = (f16[1,1,6,1,1,40,128]{6,5,4,3,2,1,0:T(8,128)(2,1)S(1)}, f16[1,1,6,1,1,40,128]{6,5,4,3,2,1,0:T(8,128)(2,1)S(1)}, u32[]{:S(2)}, u32[]{:S(2)}) collective-permute-start(f16[1,1,6,1,1,40,128]{6,5,4,3,2,1,0:T(8,128)(2,1)S(1)} %add_convert_fusion.1), channel_id=1, source_target_pairs={{0,12},{1,11},{2,14},{3,9},{4,8},{5,15},{6,10},{7,13},{8,4},{9,3},... | collective-permute-start | bytes 184328 | tf_op jit(solution)/shard_map/ppermute | solution.py:850
  157.3 6.3 %collective-permute-start.31 = (f16[1,1,6,2,2,40,128]{6,5,4,3,2,1,0:T(8,128)(2,1)S(1)}, f16[1,1,6,2,2,40,128]{6,5,4,3,2,1,0:T(8,128)(2,1)S(1)}, u32[]{:S(2)}, u32[]{:S(2)}) collective-permute-start(f16[1,1,6,2,2,40,128]{6,5,4,3,2,1,0:T(8,128)(2,1)S(1)} %pad_maximum_fusion.2), channel_id=1, source_target_pairs={{0,2},{1,5},{2,0},{3,7},{4,6},{5,1},{6,4},{7,3},{8,10},{9,13},{10,... | collective-permute-start | bytes 737288 | tf_op jit(solution)/shard_map/ppermute | solution.py:850
  (30 other events, 306.4 us)

commit v3 on v2

--- a/solution.py
+++ b/solution.py
@@ -230,7 +230,7 @@
         out[rows + 1] = bottom_ref[0, at : at + steps]
 
 
-def table_kernel(ready, place_ref, own_ref, others_ref, out_ref):
+def join_tables(place_ref, own_ref, others_ref, out_ref):
     slabs = others_ref.shape[0] + 1
     kinds, steps, _ = own_ref.shape
     for offset in range(slabs):
@@ -250,13 +250,12 @@
     return whole, places
 
 
-def pack_weight_kernel(ready, w_ref, out_ref, back_ref):
+def pack_weights(w_ref, out_ref, back_ref):
     taps, channels, _ = w_ref.shape
     lanes = out_ref.shape[1]
     whole, places = packed_rows(taps, channels)
     out_ref[...] = jnp.zeros(out_ref.shape, BF16)
     back_ref[...] = jnp.zeros(back_ref.shape, BF16)
-    ready()
     for tap, (at, rest) in enumerate(places):
         for ref, value in ((out_ref, w_ref[tap]), (back_ref, jnp.transpose(w_ref[taps - 1 - tap]))):
             ref[at : at + whole, 0:channels] = value[:whole]
@@ -332,9 +331,9 @@
 
 def edge_sweep_kernel(
     group, total_cells, ready, flag_ref, place_ref, low_ref, high_ref, left_ref, right_ref,
-    parts_ref, coef_ref, lat_ref, others_ref, w_ref, noise_hbm,
-    even_ref, odd_ref, sides_ref, first_row, last_row,
-    noise_ref, y_ref, row_ref, sem,
+    parts_ref, table_ref, tables_ref, lat_ref, others_ref, noise_hbm, w_hbm,
+    even_ref, odd_ref, sides_ref, first_row, last_row, coef_ref, w_ref, back_ref,
+    noise_ref, y_ref, row_ref, raw_ref, sem,
 ):
     rows, span, lanes = odd_ref.shape
     rows = rows - 2
@@ -343,7 +342,8 @@
     half = place_ref[0]
     tall = lat_ref.shape[0]
     own_noise = noise_hbm.at[:, pl.ds(half * rows, rows)]
-    loads = start_copies([(own_noise, noise_ref)], sem)
+    loads = start_copies([(own_noise, noise_ref), (w_hbm, raw_ref)], sem)
+    join_tables(place_ref, table_ref, tables_ref, coef_ref)
     center, inv = merged_moments(parts_ref[:, :CORNERS], float(total_cells * group), lanes, group)
     center, inv = center[0:1], inv[0:1]
     pieces = lanes // LANES
@@ -377,6 +377,7 @@
 
     lax.fori_loop(0, rows + 2, activate, 0)
     wait_copies(loads)
+    pack_weights(raw_ref, w_ref, back_ref)
     for row, out in ((0, first_row), (rows - 1, last_row)):
         put_tiles(y_ref, convolve_rows(even_ref, odd_ref, w_ref, row, 1, steps))
         noise = (noise_ref, others_ref)
@@ -831,7 +832,7 @@
 FLIPS = ((1, 0), (0, 1), (1, 1))
 
 
-def reduce_weights(kept, arrived, latent, sweeps, travel, land, sides):
+def reduce_weights(kept, arrived, needs, sweep, travel, land, landing, sides):
     slabs, tiles, share_rows, lanes = kept.shape
     shape = (slabs, 2, tiles // 2, 2, 2, share_rows // 4, lanes)
     pieces = (kept.reshape(shape), arrived.reshape(shape))
@@ -861,16 +862,14 @@
     def half(which):
         return sum(half_of_dim(x, which, 1) for x in pieces)
 
-    outgoing, latent = lax.optimization_barrier((half(first[1]).astype(F16), latent))
+    outgoing, needs = lax.optimization_barrier((half(first[1]).astype(F16), needs))
     other = send_tile(0, 1, 0)(outgoing)
-    other, (base, leaving) = lax.optimization_barrier((other, sweeps[0]((latent,))))
+    other, (trajectory, leaving) = lax.optimization_barrier((other, sweep(needs)))
     value = half(first[0]) + other.astype(F32)
+    trajectory = land(landing, trajectory, 0)
     landing = travel(leaving)
-    outgoing = half_of_dim(value, second[1], 3).astype(F16)
-    outgoing, latent, base = lax.optimization_barrier((outgoing, latent, base))
-    other = send_tile(1, 1, 0)(outgoing)
-    other, (base, leaving), landing = lax.optimization_barrier((other, sweeps[1]((latent, base)), landing))
-    value = half_of_dim(value, second[0], 3) + other.astype(F32)
+    value = half_sum(value, second, send_tile(1, 1, 0), 3)
+    value, landing, trajectory = lax.optimization_barrier((value, landing, trajectory))
     bits = axis_bits(("tm",))[::-1]
     for (_, bit), mine in zip(bits[:-1], slab_sides):
         value = half_sum(value, mine, lambda x, bit=bit: swap(x, "tm", bit), 0)
@@ -880,14 +879,10 @@
     else:
         value = half_sum(value, far, lambda x: swap(x, "sy", 2), 4)
     value = value.astype(F16)
-    trajectory = land(landing, base, 0)
-    landing = travel(leaving)
     sends = [(flips, send_tile(1, flips[1], flips[0])) for flips in FLIPS]
     value = joint_gather(value, (far, second), (4, 3), sends)
-    value, landing, trajectory = lax.optimization_barrier((value, landing, trajectory))
-    trajectory = land(landing, trajectory, 1)
     value = both_halves(value, first, send_tile(0, 1, 0), 1)
-    value, trajectory = lax.optimization_barrier((value, trajectory))
+    value, trajectory = lax.optimization_barrier((value, land(landing, trajectory, 1)))
     value = both_halves(value[None], core, lambda x: swap(x, "sx", 1), 0)
     return value.astype(F32).reshape(2 * tiles, share_rows, lanes), trajectory
 
@@ -961,9 +956,6 @@
 
     down, up = chain("sy")
     right_way, left_way = chain("sx")
-    parts1, low_rows, high_rows, first_cols, last_cols, conv_weight = lax.optimization_barrier(
-        (share(moments, tiles_axes), low_rows, high_rows, first_cols, last_cols, conv_weight)
-    )
     low = lax.ppermute(low_rows, "sy", down)
     high = lax.ppermute(high_rows, "sy", up)
     left = lax.ppermute(last_cols, "sx", right_way)
@@ -971,14 +963,8 @@
     other_tables = to_slabs(jnp.broadcast_to(table[None], (slabs - 1,) + table.shape))
     other_tables, leaving = lax.optimization_barrier((other_tables, leaving))
     others = to_slabs(leaving)
-    (coefs,) = call(
-        table_kernel, [((4, steps, lanes), F32)], [], 10**5, smem=[place], vmem=[table, other_tables],
-        grant=SMALL_BYTES,
-    )
+    parts1 = share(moments, tiles_axes)
     packed = ((9 * (lanes - LANES) + 5 * LANES, lanes), BF16)
-    weight_out, weight_back = call(
-        pack_weight_kernel, [packed, packed], [], 10**7, load=[conv_weight.reshape(9, channels, channels)],
-    )
 
     even_shape = (rows + 2, (cols + 2) * steps, lanes)
     odd_shape = (rows + 2, span, lanes)
@@ -989,14 +975,16 @@
     even_out, odd_out, field_out = (even_shape, BF16), (odd_shape, BF16), (field_shape, F32)
     edge_row, edge_col = ((1, span, lanes), F32), ((rows, steps, lanes), F32)
     noise_scratch = [(noise_shape, BF16)]
-    even1, odd1, sides, first_row, last_row = call(
+    even1, odd1, sides, first_row, last_row, coefs, weight_out, weight_back = call(
         functools.partial(edge_sweep_kernel, group, cells),
-        [even_out, odd_out, ((2, 2, tile_rows + 2, lanes), F32), edge_row, edge_row],
-        noise_scratch + [(row_shape, F32), (row_shape, F32), pltpu.SemaphoreType.DMA((1,))],
+        [even_out, odd_out, ((2, 2, tile_rows + 2, lanes), F32), edge_row, edge_row]
+        + [((4, steps, lanes), F32), packed, packed],
+        noise_scratch + [(row_shape, F32), (row_shape, F32), ((9, channels, channels), BF16)]
+        + [pltpu.SemaphoreType.DMA((2,))],
         conv_flops // 4,
         smem=[flags, place],
-        vmem=[low, high, left, right, parts1, coefs, latent_init, others, weight_out],
-        hbm=[step_noise],
+        vmem=[low, high, left, right, parts1, table, other_tables, latent_init, others],
+        hbm=[step_noise, conv_weight.reshape(9, channels, channels)],
     )
     down_rows, up_rows = row_chain()
     top = lax.ppermute(last_row, ("tm", "sy"), down_rows)
@@ -1095,12 +1083,17 @@
 
         return run
 
-    sums, (late_a, late_b) = butterfly(
+    sums, (late_a, late_b, (base, leaving)) = butterfly(
         sums,
-        order,
+        ("tm", "sx", "sy"),
         join_sums,
-        [late_weight(0), late_weight(1)],
-    )
+        [
+            late_weight(0),
+            late_weight(1),
+            lambda done: (second_sweep(0, cut), (latent_init,)),
+        ],
+    )
+    landing = to_slabs(leaving.astype(F16))
 
     payload = ((slabs, tiles // 2, share_rows, LANES), F32)
     up_shape = ((channels, rows * span), BF16)
@@ -1125,6 +1118,7 @@
         )
         return kept
 
+    sent, landing = lax.optimization_barrier((sent, landing))
     arrived, kept = beside(sent, "sx", 1, kept_weight, (up_t,))
 
     def land(part, trajectory, which):
@@ -1143,10 +1137,11 @@
     summed, trajectory = reduce_weights(
         kept,
         arrived,
-        latent_init,
-        (second_sweep(0, cut), second_sweep(cut, rows - cut)),
+        (latent_init, base),
+        second_sweep(cut, rows - cut),
         lambda leaving: to_slabs(leaving.astype(F16)),
         land,
+        landing,
         halves,
     )
     (grad,) = call(

time: 169 us -> 159 us (0.941)
  local copies, waits for them, and re-layouts: 10.9 us -> 3.08 us
  waiting for transfers between devices: 38.7 us -> 41.7 us
    unnamed x40 -> x12, local copies, waits for them, and re-layouts: 10.2 us -> 2.37 us
    all_to_all x1, waiting for transfers between devices: 4.45 us -> 0.01 us  [share(): return lax.all_to_all(copies, axes, 0, 0)]
    ppermute x12, waiting for transfers between devices: 14.7 us -> 10.9 us  [swap(): return lax.ppermute(value, axis, pairs)]
    ppermute x4, waiting for transfers between devices: 2.56 us -> 6.17 us  [to_slabs(): return lax.ppermute(pieces, 'tm', shifted(1))]
    ppermute x1, waiting for transfers between devices: 0.01 us -> 3.52 us  [shards(): right = lax.ppermute(first_cols, 'sx', left_way)]
    ppermute x6, waiting for transfers between devices: 12.5 us -> 15.2 us  [send_tile(): return lambda value: lax.ppermute(value, ('sy', 'sx'), pairs)]
    ppermute x1, starting transfers between devices: 1.92 us -> 3.82 us  [shards(): low = lax.ppermute(low_rows, 'sy', down)]
    pallas_call x20 -> x18, Pallas kernels: 56.3 us -> 54.7 us  [call(): pl.pallas_call(body, out_shape=shapes, in_specs=specs, out_specs=out_spec...]
  transfers between devices with their start and end apart: 34 -> 34, of which waited for: 15 -> 19; matrix products, arithmetic and copies ran while one was open for 1% -> 0% of each run, Pallas kernels for 22% -> 25%
where the time goes in v3:
time: 159 us; the launch traced here: 158 us
  starting transfers between devices  55.7 us (35%)
  Pallas kernels  54.7 us (34%)
  waiting for transfers between devices  41.7 us (26%)
  local copies, waits for them, and re-layouts  3.08 us (2%)
  other arithmetic  1.99 us (1%)
    pallas_call x18, Pallas kernels, call(): pl.pallas_call(body, out_shape=shapes, in_specs=specs, out_specs=out_spec...  54.7 us
    ppermute x12, starting transfers between devices, swap(): return lax.ppermute(value, axis, pairs)  16.3 us
    ppermute x6, waiting for transfers between devices, send_tile(): return lambda value: lax.ppermute(value, ('sy', 'sx'), pairs)  15.2 us
    ppermute x12, waiting for transfers between devices, swap(): return lax.ppermute(value, axis, pairs)  10.9 us
    ppermute x6, starting transfers between devices, send_tile(): return lambda value: lax.ppermute(value, ('sy', 'sx'), pairs)  6.27 us
    ppermute x4, waiting for transfers between devices, to_slabs(): return lax.ppermute(pieces, 'tm', shifted(1))  6.17 us
    ppermute x4, starting transfers between devices, to_slabs(): return lax.ppermute(pieces, 'tm', shifted(1))  6.12 us
    ppermute x3, waiting for transfers between devices, send_slab(): return lambda value: lax.ppermute(value, ('tm', 'sy'), pairs)  5.96 us
  transfers between devices with their start and end apart: 34, of which 19 were waited for; matrix products, arithmetic and copies ran while one was open for 0% of the time, Pallas kernels for 25%

profile of v3, /device:TPU:0, one launch (start us, length us, event | category | flops | bytes accessed | tf_op | source)
XLA Modules:
  0.0 158.5 jit_solution(9154186383466127239)
XLA Ops:
  1.5 5.4 %shard_map.113 = (f32[16,32,128]{2,1,0:T(8,128)}, f32[4,4,384]{2,1,0:T(4,128)}, f32[2,24,320]{2,1,0:T(8,128)}, f32[2,24,320]{2,1,0:T(8,128)}, f32[2,16,320]{2,1,...) custom-call(s32[4]{0:T(128)} %refs_0_.1, s32[10]{0:T(128)} %stack.88.refs_1_.refs_0_, f32[4]{0:T(128)} %refs_2_.1, ...), custom_call_target="tpu_custom_call" | custom-call | flops 1000000 | bytes 4230504 | tf_op jit(solution)/shard_map/pallas_call | solution.py:758
  7.0 3.0 %collective-permute-start.4 = (f32[1,4,4,384]{3,2,1,0:T(4,128)}, f32[1,4,4,384]{3,2,1,0:T(4,128)S(1)}, u32[]{:S(2)}, u32[]{:S(2)}) collective-permute-start(f32[1,4,4,384]{3,2,1,0:T(4,128)} %bitcast.32), channel_id=1, source_target_pairs={{0,16},{16,0},{1,17},{17,1},{2,18},{18,2},{3,19},{19,3},{4,20},{20... | collective-permute-start | bytes 73736 | tf_op jit(solution)/shard_map/ppermute | solution.py:954
  10.0 5.9 %all-to-all-start = ((f32[16,32,128]{2,1,0:T(8,128)}), f32[16,32,128]{2,1,0:T(8,128)S(1)}, u32[]{:S(2)}, u32[]{:S(2)}) async-start(f32[16,32,128]{2,1,0:T(8,128)} %get-tuple-element.114), calls=%async_computation | async-start | bytes 524288 | tf_op jit(solution)/shard_map/all_to_all | solution.py:41
  16.5 3.8 %collective-permute-start = (f32[2,24,320]{2,1,0:T(8,128)}, f32[2,24,320]{2,1,0:T(8,128)S(1)}, u32[]{:S(2)}, u32[]{:S(2)}) collective-permute-start(f32[2,24,320]{2,1,0:T(8,128)} %get-tuple-element.110), channel_id=1, source_target_pairs={{0,4},{4,8},{8,12},{1,5},{5,9},{9,13},{2,6},{6,10},{10,14},{3,7},{... | collective-permute-start | bytes 184328 | tf_op jit(solution)/shard_map/ppermute | solution.py:959
  24.4 3.5 %collective-permute-done.3.refs_5_ = f32[2,16,320]{2,1,0:T(8,128)S(1)} collective-permute-done((f32[2,16,320]{2,1,0:T(8,128)}, f32[2,16,320]{2,1,0:T(8,128)S(1)}, u32[]{:S(2)}, u32[]{:S(2)}) %collective-permute-start.3) | collective-permute-done | bytes 40992 | tf_op jit(solution)/shard_map/ppermute | solution.py:962
  28.0 3.9 %collective-permute-done.5.refs_10_.refs_7_.refs_4_ = bf16[1,4,8,24,320]{4,3,2,1,0:T(8,128)(2,1)S(1)} collective-permute-done((bf16[1,4,8,24,320]{4,3,2,1,0:T(8,128)(2,1)}, bf16[1,4,8,24,320]{4,3,2,1,0:T(8,128)(2,1)S(1)}, u32[]{:S(2)}, u32[]{:S(2)}) %collective-permute-start.5) | collective-permute-done | bytes 491552 | tf_op jit(solution)/shard_map/ppermute | solution.py:954
  34.2 4.6 %shard_map.114 = (bf16[10,208,384]{2,1,0:T(8,128)(2,1)S(1)}, bf16[10,192,384]{2,1,0:T(8,128)(2,1)S(1)}, f32[2,2,18,384]{3,2,1,0:T(8,128)S(1)}, f32[1,192,384]{2,...) custom-call(f32[8]{0:T(128)S(1)} %convert_element_type.83.refs_0_, ...), custom_call_target="tpu_custom_call" | custom-call | flops 707788800 | bytes 12669000 | tf_op jit(solution)/shard_map/pallas_call | solution.py:758
  40.1 4.6 %collective-permute-start.6 = (f32[1,192,384]{2,1,0:T(8,128)S(1)}, f32[1,192,384]{2,1,0:T(8,128)S(1)}, u32[]{:S(2)}, u32[]{:S(2)}) collective-permute-start(f32[1,192,384]{2,1,0:T(8,128)S(1)} %get-tuple-element.120.refs_2_), channel_id=1, source_target_pairs={{0,16},{16,20},{20,4},{4,8},{8,24},{24,28},{28,12},{1,17},{17,21},... | collective-permute-start | bytes 884744 | tf_op jit(solution)/shard_map/ppermute | solution.py:990
  44.7 6.7 %shard_map.115 = (f32[8,192,384]{2,1,0:T(8,128)S(1)}, f32[2,8,128]{2,1,0:T(8,128)S(1)}, f32[8,8,384]{2,1,0:T(8,128)S(1)}, f32[8,8,384]{2,1,0:T(8,128)S(1)}) custom-call(s32[10]{0:T(128)S(1)} %copy-done.4, f32[1,192,384]{2,1,0:T(8,128)S(1)} %get-tuple-element.119.refs_1_, f32[1,192,384]{2,1,0:T(8,128)S(1)} %get-tuple-element.120.refs_2_, ...), custom_call_target="tpu_custom_call" | custom-call | flops 2831155200 | bytes 10502184 | tf_op jit(solution)/shard_map/pallas_call | solution.py:758
  54.2 3.1 %collective-permute-start.8 = (f32[2,8,128]{2,1,0:T(8,128)S(1)}, f32[2,8,128]{2,1,0:T(8,128)S(1)}, u32[]{:S(2)}, u32[]{:S(2)}) collective-permute-start(f32[2,8,128]{2,1,0:T(8,128)S(1)} %get-tuple-element.129), channel_id=1, source_target_pairs={{0,1},{1,0},{2,3},{3,2},{4,5},{5,4},{6,7},{7,6},{8,9},{9,8},{10,11... | collective-permute-start | bytes 24584 | tf_op jit(solution)/shard_map/ppermute | solution.py:32
  67.1 2.4 %collective-permute-start.13 = (f32[2,8,128]{2,1,0:T(8,128)S(1)}, f32[2,8,128]{2,1,0:T(8,128)S(1)}, u32[]{:S(2)}, u32[]{:S(2)}) collective-permute-start(f32[2,8,128]{2,1,0:T(8,128)S(1)} %pad_maximum_fusion.7), channel_id=1, source_target_pairs={{0,8},{4,12},{8,0},{12,4},{1,9},{5,13},{9,1},{13,5},{2,10},{6,14},... | collective-permute-start | bytes 24584 | tf_op jit(solution)/shard_map/ppermute | solution.py:32
  73.0 2.4 %collective-permute-done.14 = f32[2,8,128]{2,1,0:T(8,128)S(1)} collective-permute-done((f32[2,8,128]{2,1,0:T(8,128)S(1)}, f32[2,8,128]{2,1,0:T(8,128)S(1)}, u32[]{:S(2)}, u32[]{:S(2)}) %collective-permute-start.14) | collective-permute-done | bytes 8224 | tf_op jit(solution)/shard_map/ppermute | solution.py:32
  75.4 3.4 %shard_map.121 = (bf16[10,208,384]{2,1,0:T(8,128)(2,1)S(1)}, bf16[10,192,384]{2,1,0:T(8,128)(2,1)S(1)}, f32[8,192,384]{2,1,0:T(8,128)S(1)}, f32[8,128]{1,0:T(8,128)S(1)}, f32[2,8,384]{2,1,0:T(8,128)S(1)}) custom-call(f32[8]{0:T(128)S(1)} %convert_element_type.83.refs_0_, s32[10]{0:T(128)S(1)} %copy-done.4, f32[2,8,128]{2,1,0:T(8,128)S(1)} %pad_maximum_fusion.9.refs_2_, ...), custom_call_target="tpu_custom_call" | custom-call | flops 23592960 | bytes 11563080 | tf_op jit(solution)/shard_map/pallas_call | solution.py:758
  86.4 4.8 %shard_map.124 = (f32[4,16,24,320]{3,2,1,0:T(8,128)}, f32[1,4,4,24,320]{4,3,2,1,0:T(8,128)S(1)}) custom-call(s32[10]{0:T(128)S(1)} %copy-done.4, f32[4,8,384]{2,1,0:T(8,128)S(1)} %get-tuple-element.123.refs_5_.refs_7_.refs_2_.refs_1_.refs_4_, f32[16,24,320]{2,1,0:T(8,128)S(1)} %copy-done.1, f32[8,192,384]{2,1,0:T(8,128)S(1)} %get-tuple-element.125.refs_9_.refs_3_.refs_1_, ...), custom_call_target="tpu_custom_call" | custom-call | flops 1415577600 | bytes 12165160 | tf_op jit(solution)/shard_map/pallas_call | solution.py:758
  93.6 2.5 %collective-permute-done.18 = f32[8,128]{1,0:T(8,128)S(1)} collective-permute-done((f32[8,128]{1,0:T(8,128)S(1)}, f32[8,128]{1,0:T(8,128)S(1)}, u32[]{:S(2)}, u32[]{:S(2)}) %collective-permute-start.18) | collective-permute-done | bytes 4128 | tf_op jit(solution)/shard_map/ppermute | solution.py:32
  100.7 5.1 %shard_map.125 = (f32[2,12,160,128]{3,2,1,0:T(8,128)S(1)}, f32[16,128]{1,0:T(8,128)S(1)}, bf16[320,1536]{1,0:T(8,128)(2,1)S(1)}) custom-call(s32[10]{0:T(128)S(1)} %copy-done.4, f32[8,192,384]{2,1,0:T(8,128)S(1)} %get-tuple-element.125.refs_9_.refs_3_.refs_1_, f32[2,8,384]{2,1,0:T(8,128)S(1)} %get-tuple-element.155.refs_2_, f32[8,128]{1,0:T(8,128)S(1)} %add.262.refs_3_, ...), custom_call_target="tpu_custom_call" | custom-call | flops 1415577600 | bytes 1000000 | tf_op jit(solution)/shard_map/pallas_call | solution.py:758
  110.6 4.8 %shard_map.127 = (f32[4,16,24,320]{3,2,1,0:T(8,128)}, f32[1,4,4,24,320]{4,3,2,1,0:T(8,128)S(1)}) custom-call(s32[10]{0:T(128)S(1)} %copy-done.4, f32[4,8,384]{2,1,0:T(8,128)S(1)} %get-tuple-element.123.refs_5_.refs_7_.refs_2_.refs_1_.refs_4_, f32[16,24,320]{2,1,0:T(8,128)S(1)} %copy-done.1, ...), custom_call_target="tpu_custom_call", output_to_operand_aliasing={{0}: (9, {})} | custom-call | flops 1415577600 | bytes 14131240 | tf_op jit(solution)/shard_map/pallas_call | solution.py:758
  115.4 3.5 %collective-permute-done.22 = f16[2,1,6,2,2,40,128]{6,5,4,3,2,1,0:T(8,128)(2,1)S(1)} collective-permute-done((f16[2,1,6,2,2,40,128]{6,5,4,3,2,1,0:T(8,128)(2,1)S(1)}, f16[2,1,6,2,2,40,128]{6,5,4,3,2,1,0:T(8,128)(2,1)S(1)}, u32[]{:S(2)}, u32[]{:S(2)}) %collective-permute-start.22) | collective-permute-done | bytes 491552 | tf_op jit(solution)/shard_map/ppermute | solution.py:851
  128.7 2.9 %collective-permute-start.27 = (f16[1,1,6,1,1,40,128]{6,5,4,3,2,1,0:T(8,128)(2,1)S(1)}, f16[1,1,6,1,1,40,128]{6,5,4,3,2,1,0:T(8,128)(2,1)S(1)}, u32[]{:S(2)}, u32[]{:S(2)}) collective-permute-start(f16[1,1,6,1,1,40,128]{6,5,4,3,2,1,0:T(8,128)(2,1)S(1)} %get-tuple-element.211), channel_id=1, source_target_pairs={{0,24},{4,28},{8,16},{12,20},{16,8},{20,12},{24,0},{28,4},{1,25},{... | collective-permute-start | bytes 184328 | tf_op jit(solution)/shard_map/ppermute | solution.py:858
  132.2 3.4 %collective-permute-done.27 = f16[1,1,6,1,1,40,128]{6,5,4,3,2,1,0:T(8,128)(2,1)S(1)} collective-permute-done((f16[1,1,6,1,1,40,128]{6,5,4,3,2,1,0:T(8,128)(2,1)S(1)}, f16[1,1,6,1,1,40,128]{6,5,4,3,2,1,0:T(8,128)(2,1)S(1)}, u32[]{:S(2)}, u32[]{:S(2)}) %collective-permute-start.27) | collective-permute-done | bytes 61472 | tf_op jit(solution)/shard_map/ppermute | solution.py:858
  135.7 2.5 %collective-permute-done.26 = f16[1,1,6,1,1,40,128]{6,5,4,3,2,1,0:T(8,128)(2,1)S(1)} collective-permute-done((f16[1,1,6,1,1,40,128]{6,5,4,3,2,1,0:T(8,128)(2,1)S(1)}, f16[1,1,6,1,1,40,128]{6,5,4,3,2,1,0:T(8,128)(2,1)S(1)}, u32[]{:S(2)}, u32[]{:S(2)}) %collective-permute-start.26) | collective-permute-done | bytes 61472 | tf_op jit(solution)/shard_map/ppermute | solution.py:858
  138.3 2.9 %collective-permute-start.29 = (f16[1,1,6,1,1,40,128]{6,5,4,3,2,1,0:T(8,128)(2,1)S(1)}, f16[1,1,6,1,1,40,128]{6,5,4,3,2,1,0:T(8,128)(2,1)S(1)}, u32[]{:S(2)}, u32[]{:S(2)}) collective-permute-start(f16[1,1,6,1,1,40,128]{6,5,4,3,2,1,0:T(8,128)(2,1)S(1)} %add_convert_fusion.1), channel_id=1, source_target_pairs={{0,4},{1,3},{2,6},{3,1},{4,0},{5,7},{6,2},{7,5},{8,12},{9,11},{10,... | collective-permute-start | bytes 184328 | tf_op jit(solution)/shard_map/ppermute | solution.py:851
  144.1 3.3 %collective-permute-done.30 = f16[1,1,6,1,1,40,128]{6,5,4,3,2,1,0:T(8,128)(2,1)S(1)} collective-permute-done((f16[1,1,6,1,1,40,128]{6,5,4,3,2,1,0:T(8,128)(2,1)S(1)}, f16[1,1,6,1,1,40,128]{6,5,4,3,2,1,0:T(8,128)(2,1)S(1)}, u32[]{:S(2)}, u32[]{:S(2)}) %collective-permute-start.30) | collective-permute-done | bytes 61472 | tf_op jit(solution)/shard_map/ppermute | solution.py:851
  149.2 4.7 %collective-permute-done.31 = f16[1,1,6,2,2,40,128]{6,5,4,3,2,1,0:T(8,128)(2,1)S(1)} collective-permute-done((f16[1,1,6,2,2,40,128]{6,5,4,3,2,1,0:T(8,128)(2,1)S(1)}, f16[1,1,6,2,2,40,128]{6,5,4,3,2,1,0:T(8,128)(2,1)S(1)}, u32[]{:S(2)}, u32[]{:S(2)}) %collective-permute-start.31) | collective-permute-done | bytes 245792 | tf_op jit(solution)/shard_map/ppermute | solution.py:851
  (111 shorter events, 63.8 us)
Async XLA Ops:
  7.0 9.0 %collective-permute-start.4 = (f32[1,4,4,384]{3,2,1,0:T(4,128)}, f32[1,4,4,384]{3,2,1,0:T(4,128)S(1)}, u32[]{:S(2)}, u32[]{:S(2)}) collective-permute-start(f32[1,4,4,384]{3,2,1,0:T(4,128)} %bitcast.32), channel_id=1, source_target_pairs={{0,16},{16,0},{1,17},{17,1},{2,18},{18,2},{3,19},{19,3},{4,20},{20... | collective-permute-start | bytes 73736 | tf_op jit(solution)/shard_map/ppermute | solution.py:954
  10.0 18.0 %all-to-all-start = ((f32[16,32,128]{2,1,0:T(8,128)}), f32[16,32,128]{2,1,0:T(8,128)S(1)}, u32[]{:S(2)}, u32[]{:S(2)}) async-start(f32[16,32,128]{2,1,0:T(8,128)} %get-tuple-element.114), calls=%async_computation | async-start | bytes 524288 | tf_op jit(solution)/shard_map/all_to_all | solution.py:41
  15.9 15.9 %collective-permute-start.5 = (bf16[1,4,8,24,320]{4,3,2,1,0:T(8,128)(2,1)}, bf16[1,4,8,24,320]{4,3,2,1,0:T(8,128)(2,1)S(1)}, u32[]{:S(2)}, u32[]{:S(2)}) collective-permute-start(bf16[1,4,8,24,320]{4,3,2,1,0:T(8,128)(2,1)} %get-tuple-element.118), channel_id=1, source_target_pairs={{0,16},{16,0},{1,17},{17,1},{2,18},{18,2},{3,19},{19,3},{4,20},{20... | collective-permute-start | bytes 1474568 | tf_op jit(solution)/shard_map/ppermute | solution.py:954
  16.5 11.5 %collective-permute-start = (f32[2,24,320]{2,1,0:T(8,128)}, f32[2,24,320]{2,1,0:T(8,128)S(1)}, u32[]{:S(2)}, u32[]{:S(2)}) collective-permute-start(f32[2,24,320]{2,1,0:T(8,128)} %get-tuple-element.110), channel_id=1, source_target_pairs={{0,4},{4,8},{8,12},{1,5},{5,9},{9,13},{2,6},{6,10},{10,14},{3,7},{... | collective-permute-start | bytes 184328 | tf_op jit(solution)/shard_map/ppermute | solution.py:959
  20.3 7.6 %collective-permute-start.1 = (f32[2,24,320]{2,1,0:T(8,128)}, f32[2,24,320]{2,1,0:T(8,128)S(1)}, u32[]{:S(2)}, u32[]{:S(2)}) collective-permute-start(f32[2,24,320]{2,1,0:T(8,128)} %get-tuple-element.111), channel_id=1, source_target_pairs={{4,0},{8,4},{12,8},{5,1},{9,5},{13,9},{6,2},{10,6},{14,10},{7,3},{... | collective-permute-start | bytes 184328 | tf_op jit(solution)/shard_map/ppermute | solution.py:960
  23.1 4.8 %collective-permute-start.3 = (f32[2,16,320]{2,1,0:T(8,128)}, f32[2,16,320]{2,1,0:T(8,128)S(1)}, u32[]{:S(2)}, u32[]{:S(2)}) collective-permute-start(f32[2,16,320]{2,1,0:T(8,128)} %get-tuple-element.113), channel_id=1, source_target_pairs={{1,0},{2,1},{3,2},{5,4},{6,5},{7,6},{9,8},{10,9},{11,10},{13,12},{... | collective-permute-start | bytes 122888 | tf_op jit(solution)/shard_map/ppermute | solution.py:962
  38.8 12.6 %collective-permute-start.7 = (f32[1,192,384]{2,1,0:T(8,128)S(1)}, f32[1,192,384]{2,1,0:T(8,128)S(1)}, u32[]{:S(2)}, u32[]{:S(2)}) collective-permute-start(f32[1,192,384]{2,1,0:T(8,128)S(1)} %get-tuple-element.119.refs_1_), channel_id=1, source_target_pairs={{16,0},{20,16},{4,20},{8,4},{24,8},{28,24},{12,28},{17,1},{21,17},... | collective-permute-start | bytes 884744 | tf_op jit(solution)/shard_map/ppermute | solution.py:991
  40.1 11.3 %collective-permute-start.6 = (f32[1,192,384]{2,1,0:T(8,128)S(1)}, f32[1,192,384]{2,1,0:T(8,128)S(1)}, u32[]{:S(2)}, u32[]{:S(2)}) collective-permute-start(f32[1,192,384]{2,1,0:T(8,128)S(1)} %get-tuple-element.120.refs_2_), channel_id=1, source_target_pairs={{0,16},{16,20},{20,4},{4,8},{8,24},{24,28},{28,12},{1,17},{17,21},... | collective-permute-start | bytes 884744 | tf_op jit(solution)/shard_map/ppermute | solution.py:990
  51.4 8.0 %collective-permute-start.9 = (f32[10,8,384]{2,1,0:T(8,128)S(1)}, f32[10,8,384]{2,1,0:T(8,128)S(1)}, u32[]{:S(2)}, u32[]{:S(2)}) collective-permute-start(f32[10,8,384]{2,1,0:T(8,128)S(1)} %get-tuple-element.134), channel_id=1, source_target_pairs={{0,1},{1,2},{2,3},{4,5},{5,6},{6,7},{8,9},{9,10},{10,11},{12,13},{... | collective-permute-start | bytes 368648 | tf_op jit(solution)/shard_map/ppermute | solution.py:1008
  52.7 6.7 %collective-permute-start.10 = (f32[10,8,384]{2,1,0:T(8,128)S(1)}, f32[10,8,384]{2,1,0:T(8,128)S(1)}, u32[]{:S(2)}, u32[]{:S(2)}) collective-permute-start(f32[10,8,384]{2,1,0:T(8,128)S(1)} %get-tuple-element.135), channel_id=1, source_target_pairs={{1,0},{2,1},{3,2},{5,4},{6,5},{7,6},{9,8},{10,9},{11,10},{13,12},{... | collective-permute-start | bytes 368648 | tf_op jit(solution)/shard_map/ppermute | solution.py:1008
  54.2 5.2 %collective-permute-start.8 = (f32[2,8,128]{2,1,0:T(8,128)S(1)}, f32[2,8,128]{2,1,0:T(8,128)S(1)}, u32[]{:S(2)}, u32[]{:S(2)}) collective-permute-start(f32[2,8,128]{2,1,0:T(8,128)S(1)} %get-tuple-element.129), channel_id=1, source_target_pairs={{0,1},{1,0},{2,3},{3,2},{4,5},{5,4},{6,7},{7,6},{8,9},{9,8},{10,11... | collective-permute-start | bytes 24584 | tf_op jit(solution)/shard_map/ppermute | solution.py:32
  67.1 4.6 %collective-permute-start.13 = (f32[2,8,128]{2,1,0:T(8,128)S(1)}, f32[2,8,128]{2,1,0:T(8,128)S(1)}, u32[]{:S(2)}, u32[]{:S(2)}) collective-permute-start(f32[2,8,128]{2,1,0:T(8,128)S(1)} %pad_maximum_fusion.7), channel_id=1, source_target_pairs={{0,8},{4,12},{8,0},{12,4},{1,9},{5,13},{9,1},{13,5},{2,10},{6,14},... | collective-permute-start | bytes 24584 | tf_op jit(solution)/shard_map/ppermute | solution.py:32
  84.8 6.4 %collective-permute-start.17 = (f32[8,128]{1,0:T(8,128)S(1)}, f32[8,128]{1,0:T(8,128)S(1)}, u32[]{:S(2)}, u32[]{:S(2)}) collective-permute-start(f32[8,128]{1,0:T(8,128)S(1)} %add.259), channel_id=1, source_target_pairs={{0,2},{1,3},{2,0},{3,1},{4,6},{5,7},{6,4},{7,5},{8,10},{9,11},{10,... | collective-permute-start | bytes 12296 | tf_op jit(solution)/shard_map/ppermute | solution.py:32
  91.3 14.5 %collective-permute-start.20 = (f16[1,4,4,24,320]{4,3,2,1,0:T(8,128)(2,1)S(1)}, f16[1,4,4,24,320]{4,3,2,1,0:T(8,128)(2,1)S(1)}, u32[]{:S(2)}, u32[]{:S(2)}) collective-permute-start(f16[1,4,4,24,320]{4,3,2,1,0:T(8,128)(2,1)S(1)} %convert_element_type.92), channel_id=1, source_target_pairs={{0,16},{16,0},{1,17},{17,1},{2,18},{18,2},{3,19},{19,3},{4,20},{20... | collective-permute-start | bytes 737288 | tf_op jit(solution)/shard_map/ppermute | solution.py:954
  96.1 4.5 %collective-permute-start.19 = (f32[8,128]{1,0:T(8,128)S(1)}, f32[8,128]{1,0:T(8,128)S(1)}, u32[]{:S(2)}, u32[]{:S(2)}) collective-permute-start(f32[8,128]{1,0:T(8,128)S(1)} %add.261), channel_id=1, source_target_pairs={{0,8},{4,12},{8,0},{12,4},{1,9},{5,13},{9,1},{13,5},{2,10},{6,14},... | collective-permute-start | bytes 12296 | tf_op jit(solution)/shard_map/ppermute | solution.py:32
  110.0 8.9 %collective-permute-start.22 = (f16[2,1,6,2,2,40,128]{6,5,4,3,2,1,0:T(8,128)(2,1)S(1)}, f16[2,1,6,2,2,40,128]{6,5,4,3,2,1,0:T(8,128)(2,1)S(1)}, u32[]{:S(2)}, u32[]{:S(2)}) collective-permute-start(f16[2,1,6,2,2,40,128]{6,5,4,3,2,1,0:T(8,128)(2,1)S(1)} %add_convert_fusion), channel_id=1, source_target_pairs={{0,2},{1,5},{2,0},{3,7},{4,6},{5,1},{6,4},{7,3},{8,10},{9,13},{10,... | collective-permute-start | bytes 1474568 | tf_op jit(solution)/shard_map/ppermute | solution.py:851
  119.1 6.3 %collective-permute-start.23 = (f16[2,1,6,1,2,40,128]{6,5,4,3,2,1,0:T(8,128)(2,1)S(1)}, f16[2,1,6,1,2,40,128]{6,5,4,3,2,1,0:T(8,128)(2,1)S(1)}, u32[]{:S(2)}, u32[]{:S(2)}) collective-permute-start(f16[2,1,6,1,2,40,128]{6,5,4,3,2,1,0:T(8,128)(2,1)S(1)} %dynamic-slice_convert_fusion), channel_id=1, source_target_pairs={{0,4},{1,3},{2,6},{3,1},{4,0},{5,7},{6,2},{7,5},{8,12},{9,11},{10,... | collective-permute-start | bytes 737288 | tf_op jit(solution)/shard_map/ppermute | solution.py:851
  120.3 7.4 %collective-permute-start.24 = (f16[1,4,4,24,320]{4,3,2,1,0:T(8,128)(2,1)S(1)}, f16[1,4,4,24,320]{4,3,2,1,0:T(8,128)(2,1)S(1)}, u32[]{:S(2)}, u32[]{:S(2)}) collective-permute-start(f16[1,4,4,24,320]{4,3,2,1,0:T(8,128)(2,1)S(1)} %convert_element_type.97), channel_id=1, source_target_pairs={{0,16},{16,0},{1,17},{17,1},{2,18},{18,2},{3,19},{19,3},{4,20},{20... | collective-permute-start | bytes 737288 | tf_op jit(solution)/shard_map/ppermute | solution.py:954
  128.7 6.9 %collective-permute-start.27 = (f16[1,1,6,1,1,40,128]{6,5,4,3,2,1,0:T(8,128)(2,1)S(1)}, f16[1,1,6,1,1,40,128]{6,5,4,3,2,1,0:T(8,128)(2,1)S(1)}, u32[]{:S(2)}, u32[]{:S(2)}) collective-permute-start(f16[1,1,6,1,1,40,128]{6,5,4,3,2,1,0:T(8,128)(2,1)S(1)} %get-tuple-element.211), channel_id=1, source_target_pairs={{0,24},{4,28},{8,16},{12,20},{16,8},{20,12},{24,0},{28,4},{1,25},{... | collective-permute-start | bytes 184328 | tf_op jit(solution)/shard_map/ppermute | solution.py:858
  131.7 6.5 %collective-permute-start.26 = (f16[1,1,6,1,1,40,128]{6,5,4,3,2,1,0:T(8,128)(2,1)S(1)}, f16[1,1,6,1,1,40,128]{6,5,4,3,2,1,0:T(8,128)(2,1)S(1)}, u32[]{:S(2)}, u32[]{:S(2)}) collective-permute-start(f16[1,1,6,1,1,40,128]{6,5,4,3,2,1,0:T(8,128)(2,1)S(1)} %get-tuple-element.212), channel_id=1, source_target_pairs={{0,8},{4,12},{8,0},{12,4},{16,24},{20,28},{24,16},{28,20},{1,9},{5... | collective-permute-start | bytes 184328 | tf_op jit(solution)/shard_map/ppermute | solution.py:858
  138.2 5.5 %collective-permute-start.28 = (f16[1,1,6,1,1,40,128]{6,5,4,3,2,1,0:T(8,128)(2,1)S(1)}, f16[1,1,6,1,1,40,128]{6,5,4,3,2,1,0:T(8,128)(2,1)S(1)}, u32[]{:S(2)}, u32[]{:S(2)}) collective-permute-start(f16[1,1,6,1,1,40,128]{6,5,4,3,2,1,0:T(8,128)(2,1)S(1)} %add_convert_fusion.1), channel_id=1, source_target_pairs={{0,8},{1,9},{2,10},{3,11},{4,12},{5,13},{6,14},{7,15},{8,0},{9,1},... | collective-permute-start | bytes 184328 | tf_op jit(solution)/shard_map/ppermute | solution.py:851
  138.3 5.8 %collective-permute-start.29 = (f16[1,1,6,1,1,40,128]{6,5,4,3,2,1,0:T(8,128)(2,1)S(1)}, f16[1,1,6,1,1,40,128]{6,5,4,3,2,1,0:T(8,128)(2,1)S(1)}, u32[]{:S(2)}, u32[]{:S(2)}) collective-permute-start(f16[1,1,6,1,1,40,128]{6,5,4,3,2,1,0:T(8,128)(2,1)S(1)} %add_convert_fusion.1), channel_id=1, source_target_pairs={{0,4},{1,3},{2,6},{3,1},{4,0},{5,7},{6,2},{7,5},{8,12},{9,11},{10,... | collective-permute-start | bytes 184328 | tf_op jit(solution)/shard_map/ppermute | solution.py:851
  141.2 6.2 %collective-permute-start.30 = (f16[1,1,6,1,1,40,128]{6,5,4,3,2,1,0:T(8,128)(2,1)S(1)}, f16[1,1,6,1,1,40,128]{6,5,4,3,2,1,0:T(8,128)(2,1)S(1)}, u32[]{:S(2)}, u32[]{:S(2)}) collective-permute-start(f16[1,1,6,1,1,40,128]{6,5,4,3,2,1,0:T(8,128)(2,1)S(1)} %add_convert_fusion.1), channel_id=1, source_target_pairs={{0,12},{1,11},{2,14},{3,9},{4,8},{5,15},{6,10},{7,13},{8,4},{9,3},... | collective-permute-start | bytes 184328 | tf_op jit(solution)/shard_map/ppermute | solution.py:851
  147.7 6.3 %collective-permute-start.31 = (f16[1,1,6,2,2,40,128]{6,5,4,3,2,1,0:T(8,128)(2,1)S(1)}, f16[1,1,6,2,2,40,128]{6,5,4,3,2,1,0:T(8,128)(2,1)S(1)}, u32[]{:S(2)}, u32[]{:S(2)}) collective-permute-start(f16[1,1,6,2,2,40,128]{6,5,4,3,2,1,0:T(8,128)(2,1)S(1)} %pad_maximum_fusion.2), channel_id=1, source_target_pairs={{0,2},{1,5},{2,0},{3,7},{4,6},{5,1},{6,4},{7,3},{8,10},{9,13},{10,... | collective-permute-start | bytes 737288 | tf_op jit(solution)/shard_map/ppermute | solution.py:851
  (16 other events, 140.1 us)

commit v4 on v3

--- a/solution.py
+++ b/solution.py
@@ -230,7 +230,7 @@
         out[rows + 1] = bottom_ref[0, at : at + steps]
 
 
-def join_tables(place_ref, own_ref, others_ref, out_ref):
+def table_kernel(ready, place_ref, own_ref, others_ref, out_ref):
     slabs = others_ref.shape[0] + 1
     kinds, steps, _ = own_ref.shape
     for offset in range(slabs):
@@ -250,12 +250,13 @@
     return whole, places
 
 
-def pack_weights(w_ref, out_ref, back_ref):
+def pack_weight_kernel(ready, w_ref, out_ref, back_ref):
     taps, channels, _ = w_ref.shape
     lanes = out_ref.shape[1]
     whole, places = packed_rows(taps, channels)
     out_ref[...] = jnp.zeros(out_ref.shape, BF16)
     back_ref[...] = jnp.zeros(back_ref.shape, BF16)
+    ready()
     for tap, (at, rest) in enumerate(places):
         for ref, value in ((out_ref, w_ref[tap]), (back_ref, jnp.transpose(w_ref[taps - 1 - tap]))):
             ref[at : at + whole, 0:channels] = value[:whole]
@@ -331,9 +332,9 @@
 
 def edge_sweep_kernel(
     group, total_cells, ready, flag_ref, place_ref, low_ref, high_ref, left_ref, right_ref,
-    parts_ref, table_ref, tables_ref, lat_ref, others_ref, noise_hbm, w_hbm,
-    even_ref, odd_ref, sides_ref, first_row, last_row, coef_ref, w_ref, back_ref,
-    noise_ref, y_ref, row_ref, raw_ref, sem,
+    parts_ref, coef_ref, lat_ref, others_ref, w_ref, noise_hbm,
+    even_ref, odd_ref, sides_ref, first_row, last_row,
+    noise_ref, y_ref, row_ref, sem,
 ):
     rows, span, lanes = odd_ref.shape
     rows = rows - 2
@@ -342,8 +343,7 @@
     half = place_ref[0]
     tall = lat_ref.shape[0]
     own_noise = noise_hbm.at[:, pl.ds(half * rows, rows)]
-    loads = start_copies([(own_noise, noise_ref), (w_hbm, raw_ref)], sem)
-    join_tables(place_ref, table_ref, tables_ref, coef_ref)
+    loads = start_copies([(own_noise, noise_ref)], sem)
     center, inv = merged_moments(parts_ref[:, :CORNERS], float(total_cells * group), lanes, group)
     center, inv = center[0:1], inv[0:1]
     pieces = lanes // LANES
@@ -377,7 +377,6 @@
 
     lax.fori_loop(0, rows + 2, activate, 0)
     wait_copies(loads)
-    pack_weights(raw_ref, w_ref, back_ref)
     for row, out in ((0, first_row), (rows - 1, last_row)):
         put_tiles(y_ref, convolve_rows(even_ref, odd_ref, w_ref, row, 1, steps))
         noise = (noise_ref, others_ref)
@@ -716,16 +715,23 @@
             half_gradient(half, up_t_ref[...], late_ref, scale, even_ref, odd_ref, steps, out_ref)
 
 
-def unpack_kernel(ready, x_ref, scale_ref, out_ref):
-    ready()
+def unpack_kernel(ready, place_ref, own_ref, other_ref, scale_ref, out_ref):
     whole = out_ref.shape[2] // LANES
     half = LANES // 2
     scale = scale_ref[8:9]
+    tiles = own_ref.shape[0]
+    first = place_ref[1] == 0
+
+    def tile(index):
+        low, at = index < tiles, index % tiles
+        mine, other = (own_ref[at], other_ref[at]) if low else (other_ref[at], own_ref[at])
+        return jnp.where(first, mine, other) * scale
+
     for tap in range(9):
         for piece in range(whole):
             at = piece * LANES
-            out_ref[tap, :, at : at + LANES] = x_ref[tap * whole + piece] * scale
-        rest = x_ref[9 * whole + tap // 2] * scale
+            out_ref[tap, :, at : at + LANES] = tile(tap * whole + piece)
+        rest = tile(9 * whole + tap // 2)
         if tap % 2:
             rest = pltpu.roll(rest, half, 1)
         out_ref[tap, :, whole * LANES :] = rest[:, :half]
@@ -857,7 +863,7 @@
             pairs.append((i, (tm ^ (bit * flip_slab)) * tall + (sy ^ (2 * flip_far))))
         return lambda value: lax.ppermute(value, ("tm", "sy"), pairs)
 
-    first, second, far, core, *slab_sides = sides
+    first, second, far, *slab_sides = sides
 
     def half(which):
         return sum(half_of_dim(x, which, 1) for x in pieces)
@@ -869,7 +875,7 @@
     trajectory = land(landing, trajectory, 0)
     landing = travel(leaving)
     value = half_sum(value, second, send_tile(1, 1, 0), 3)
-    value, landing, trajectory = lax.optimization_barrier((value, landing, trajectory))
+    value, trajectory = lax.optimization_barrier((value, trajectory))
     bits = axis_bits(("tm",))[::-1]
     for (_, bit), mine in zip(bits[:-1], slab_sides):
         value = half_sum(value, mine, lambda x, bit=bit: swap(x, "tm", bit), 0)
@@ -881,10 +887,11 @@
     value = value.astype(F16)
     sends = [(flips, send_tile(1, flips[1], flips[0])) for flips in FLIPS]
     value = joint_gather(value, (far, second), (4, 3), sends)
+    value, landing = lax.optimization_barrier((value, landing))
     value = both_halves(value, first, send_tile(0, 1, 0), 1)
     value, trajectory = lax.optimization_barrier((value, land(landing, trajectory, 1)))
-    value = both_halves(value[None], core, lambda x: swap(x, "sx", 1), 0)
-    return value.astype(F32).reshape(2 * tiles, share_rows, lanes), trajectory
+    value = value.reshape(tiles, share_rows, lanes)
+    return value.astype(F32), swap(value, "sx", 1).astype(F32), trajectory
 
 
 def shards(
@@ -920,7 +927,6 @@
         side(jnp.where(core == 0, turns[0], turns[1])),
         side(jnp.where(core == 0, turns[1], turns[0])),
         side(bit_of("sy", 2)),
-        side(core),
     ]
     held = slabs
     for _, bit in axis_bits(("tm",))[::-1]:
@@ -964,7 +970,15 @@
     other_tables, leaving = lax.optimization_barrier((other_tables, leaving))
     others = to_slabs(leaving)
     parts1 = share(moments, tiles_axes)
+    parts1, conv_weight = lax.optimization_barrier((parts1, conv_weight))
+    (coefs,) = call(
+        table_kernel, [((4, steps, lanes), F32)], [], 10**5, smem=[place], vmem=[table, other_tables],
+        grant=SMALL_BYTES,
+    )
     packed = ((9 * (lanes - LANES) + 5 * LANES, lanes), BF16)
+    weight_out, weight_back = call(
+        pack_weight_kernel, [packed, packed], [], 10**7, load=[conv_weight.reshape(9, channels, channels)],
+    )
 
     even_shape = (rows + 2, (cols + 2) * steps, lanes)
     odd_shape = (rows + 2, span, lanes)
@@ -975,16 +989,14 @@
     even_out, odd_out, field_out = (even_shape, BF16), (odd_shape, BF16), (field_shape, F32)
     edge_row, edge_col = ((1, span, lanes), F32), ((rows, steps, lanes), F32)
     noise_scratch = [(noise_shape, BF16)]
-    even1, odd1, sides, first_row, last_row, coefs, weight_out, weight_back = call(
+    even1, odd1, sides, first_row, last_row = call(
         functools.partial(edge_sweep_kernel, group, cells),
-        [even_out, odd_out, ((2, 2, tile_rows + 2, lanes), F32), edge_row, edge_row]
-        + [((4, steps, lanes), F32), packed, packed],
-        noise_scratch + [(row_shape, F32), (row_shape, F32), ((9, channels, channels), BF16)]
-        + [pltpu.SemaphoreType.DMA((2,))],
+        [even_out, odd_out, ((2, 2, tile_rows + 2, lanes), F32), edge_row, edge_row],
+        noise_scratch + [(row_shape, F32), (row_shape, F32), pltpu.SemaphoreType.DMA((1,))],
         conv_flops // 4,
         smem=[flags, place],
-        vmem=[low, high, left, right, parts1, table, other_tables, latent_init, others],
-        hbm=[step_noise, conv_weight.reshape(9, channels, channels)],
+        vmem=[low, high, left, right, parts1, coefs, latent_init, others, weight_out],
+        hbm=[step_noise],
     )
     down_rows, up_rows = row_chain()
     top = lax.ppermute(last_row, ("tm", "sy"), down_rows)
@@ -1134,7 +1146,7 @@
         )
         return trajectory
 
-    summed, trajectory = reduce_weights(
+    own, other, trajectory = reduce_weights(
         kept,
         arrived,
         (latent_init, base),
@@ -1145,7 +1157,7 @@
         halves,
     )
     (grad,) = call(
-        unpack_kernel, [((9, share_rows, channels), F32)], [], 10**6, vmem=[summed, scales],
+        unpack_kernel, [((9, share_rows, channels), F32)], [], 10**6, smem=[place], vmem=[own, other, scales],
         grant=SMALL_BYTES,
     )
     return trajectory, grad.transpose(0, 2, 1).reshape(3, 3, channels, share_rows)

time: 159 us -> 156 us (0.981)
  waiting for transfers between devices: 41.7 us -> 34.8 us
  starting transfers between devices: 55.7 us -> 58.1 us
  Pallas kernels: 54.7 us -> 56.9 us
    ppermute x1, waiting for transfers between devices: 3.52 us -> 0.01 us  [shards(): right = lax.ppermute(first_cols, 'sx', left_way)]
    ppermute x4, waiting for transfers between devices: 6.17 us -> 2.67 us  [to_slabs(): return lax.ppermute(pieces, 'tm', shifted(1))]
    pallas_call x18 -> x20, Pallas kernels: 54.7 us -> 56.9 us  [call(): pl.pallas_call(body, out_shape=shapes, in_specs=specs, out_specs=out_spec...]
    ppermute x6, waiting for transfers between devices: 15.2 us -> 17.3 us  [send_tile(): return lambda value: lax.ppermute(value, ('sy', 'sx'), pairs)]
    ppermute x12, starting transfers between devices: 16.3 us -> 18.3 us  [swap(): return lax.ppermute(value, axis, pairs)]
  transfers between devices with their start and end apart: 34 -> 34, of which waited for: 19 -> 16; matrix products, arithmetic and copies ran while one was open for 0% -> 0% of each run, Pallas kernels for 25% -> 27%
where the time goes in v4:
time: 156 us
  starting transfers between devices  58.1 us (37%)
  Pallas kernels  56.9 us (36%)
  waiting for transfers between devices  34.8 us (22%)
  local copies, waits for them, and re-layouts  3.08 us (2%)
    pallas_call x20, Pallas kernels, call(): pl.pallas_call(body, out_shape=shapes, in_specs=specs, out_specs=out_spec...  56.9 us
    ppermute x12, starting transfers between devices, swap(): return lax.ppermute(value, axis, pairs)  18.3 us
    ppermute x6, waiting for transfers between devices, send_tile(): return lambda value: lax.ppermute(value, ('sy', 'sx'), pairs)  17.3 us
    ppermute x12, waiting for transfers between devices, swap(): return lax.ppermute(value, axis, pairs)  9.98 us
    ppermute x6, starting transfers between devices, send_tile(): return lambda value: lax.ppermute(value, ('sy', 'sx'), pairs)  7.14 us
    all_to_all x1, starting transfers between devices, share(): return lax.all_to_all(copies, axes, 0, 0)  5.94 us
    ppermute x4, starting transfers between devices, to_slabs(): return lax.ppermute(pieces, 'tm', shifted(1))  5.75 us
    ppermute x3, waiting for transfers between devices, send_slab(): return lambda value: lax.ppermute(value, ('tm', 'sy'), pairs)  4.58 us
  transfers between devices with their start and end apart: 34, of which 16 were waited for; matrix products, arithmetic and copies ran while one was open for 0% of the time, Pallas kernels for 27%

profile of v4, /device:TPU:0, one launch (start us, length us, event | category | flops | bytes accessed | tf_op | source)
XLA Modules:
  0.0 155.6 jit_solution(6649900752950807052)
XLA Ops:
  1.5 5.3 %shard_map.113 = (f32[16,32,128]{2,1,0:T(8,128)}, f32[4,4,384]{2,1,0:T(4,128)}, f32[2,24,320]{2,1,0:T(8,128)}, f32[2,24,320]{2,1,0:T(8,128)}, f32[2,16,320]{2,1,...) custom-call(s32[4]{0:T(128)} %refs_0_.1, s32[10]{0:T(128)} %stack.88.refs_1_.refs_0_, f32[4]{0:T(128)} %refs_2_.1, ...), custom_call_target="tpu_custom_call" | custom-call | flops 1000000 | bytes 4230504 | tf_op jit(solution)/shard_map/pallas_call | solution.py:764
  6.9 3.0 %collective-permute-start.4 = (f32[1,4,4,384]{3,2,1,0:T(4,128)}, f32[1,4,4,384]{3,2,1,0:T(4,128)S(1)}, u32[]{:S(2)}, u32[]{:S(2)}) collective-permute-start(f32[1,4,4,384]{3,2,1,0:T(4,128)} %bitcast.28), channel_id=1, source_target_pairs={{0,16},{16,0},{1,17},{17,1},{2,18},{18,2},{3,19},{19,3},{4,20},{20... | collective-permute-start | bytes 73736 | tf_op jit(solution)/shard_map/ppermute | solution.py:960
  9.9 5.9 %all-to-all-start = ((f32[16,32,128]{2,1,0:T(8,128)}), f32[16,32,128]{2,1,0:T(8,128)S(1)}, u32[]{:S(2)}, u32[]{:S(2)}) async-start(f32[16,32,128]{2,1,0:T(8,128)} %get-tuple-element.115), calls=%async_computation | async-start | bytes 524288 | tf_op jit(solution)/shard_map/all_to_all | solution.py:41
  16.4 3.8 %collective-permute-start = (f32[2,24,320]{2,1,0:T(8,128)}, f32[2,24,320]{2,1,0:T(8,128)S(1)}, u32[]{:S(2)}, u32[]{:S(2)}) collective-permute-start(f32[2,24,320]{2,1,0:T(8,128)} %get-tuple-element.111), channel_id=1, source_target_pairs={{0,4},{4,8},{8,12},{1,5},{5,9},{9,13},{2,6},{6,10},{10,14},{3,7},{... | collective-permute-start | bytes 184328 | tf_op jit(solution)/shard_map/ppermute | solution.py:965
  29.1 2.7 %collective-permute-done.5.refs_9_.refs_7_.refs_4_ = bf16[1,4,8,24,320]{4,3,2,1,0:T(8,128)(2,1)S(1)} collective-permute-done((bf16[1,4,8,24,320]{4,3,2,1,0:T(8,128)(2,1)}, bf16[1,4,8,24,320]{4,3,2,1,0:T(8,128)(2,1)S(1)}, u32[]{:S(2)}, u32[]{:S(2)}) %collective-permute-start.5) | collective-permute-done | bytes 491552 | tf_op jit(solution)/shard_map/ppermute | solution.py:960
  31.8 4.0 %shard_map.116 = (bf16[10,208,384]{2,1,0:T(8,128)(2,1)S(1)}, bf16[10,192,384]{2,1,0:T(8,128)(2,1)S(1)}, f32[2,2,18,384]{3,2,1,0:T(8,128)S(1)}, f32[1,192,384]{2,1,0:T(8,128)S(1)}, f32[1,192,384]{2,1,0:T(8,128)S(1)}) custom-call(f32[8]{0:T(128)S(1)} %convert_element_type.78.refs_0_, s32[10]{0:T(128)S(1)} %copy-done.4, ...), custom_call_target="tpu_custom_call" | custom-call | flops 707788800 | bytes 8515656 | tf_op jit(solution)/shard_map/pallas_call | solution.py:764
  37.1 4.6 %collective-permute-start.6 = (f32[1,192,384]{2,1,0:T(8,128)S(1)}, f32[1,192,384]{2,1,0:T(8,128)S(1)}, u32[]{:S(2)}, u32[]{:S(2)}) collective-permute-start(f32[1,192,384]{2,1,0:T(8,128)S(1)} %get-tuple-element.124.refs_2_), channel_id=1, source_target_pairs={{0,16},{16,20},{20,4},{4,8},{8,24},{24,28},{28,12},{1,17},{17,21},... | collective-permute-start | bytes 884744 | tf_op jit(solution)/shard_map/ppermute | solution.py:1002
  41.7 6.7 %shard_map.117 = (f32[8,192,384]{2,1,0:T(8,128)S(1)}, f32[2,8,128]{2,1,0:T(8,128)S(1)}, f32[8,8,384]{2,1,0:T(8,128)S(1)}, f32[8,8,384]{2,1,0:T(8,128)S(1)}) custom-call(s32[10]{0:T(128)S(1)} %copy-done.4, f32[1,192,384]{2,1,0:T(8,128)S(1)} %get-tuple-element.123.refs_1_, f32[1,192,384]{2,1,0:T(8,128)S(1)} %get-tuple-element.124.refs_2_, ...), custom_call_target="tpu_custom_call" | custom-call | flops 2831155200 | bytes 10502184 | tf_op jit(solution)/shard_map/pallas_call | solution.py:764
  51.2 3.1 %collective-permute-start.8 = (f32[2,8,128]{2,1,0:T(8,128)S(1)}, f32[2,8,128]{2,1,0:T(8,128)S(1)}, u32[]{:S(2)}, u32[]{:S(2)}) collective-permute-start(f32[2,8,128]{2,1,0:T(8,128)S(1)} %get-tuple-element.131), channel_id=1, source_target_pairs={{0,1},{1,0},{2,3},{3,2},{4,5},{5,4},{6,7},{7,6},{8,9},{9,8},{10,11... | collective-permute-start | bytes 24584 | tf_op jit(solution)/shard_map/ppermute | solution.py:32
  60.4 2.6 %collective-permute-start.12 = (f32[2,8,128]{2,1,0:T(8,128)S(1)}, f32[2,8,128]{2,1,0:T(8,128)S(1)}, u32[]{:S(2)}, u32[]{:S(2)}) collective-permute-start(f32[2,8,128]{2,1,0:T(8,128)S(1)} %pad_maximum_fusion.5), channel_id=1, source_target_pairs={{0,4},{4,0},{8,12},{12,8},{1,5},{5,1},{9,13},{13,9},{2,6},{6,2},{1... | collective-permute-start | bytes 24584 | tf_op jit(solution)/shard_map/ppermute | solution.py:32
  65.1 2.4 %collective-permute-start.13 = (f32[2,8,128]{2,1,0:T(8,128)S(1)}, f32[2,8,128]{2,1,0:T(8,128)S(1)}, u32[]{:S(2)}, u32[]{:S(2)}) collective-permute-start(f32[2,8,128]{2,1,0:T(8,128)S(1)} %pad_maximum_fusion.6), channel_id=1, source_target_pairs={{0,8},{4,12},{8,0},{12,4},{1,9},{5,13},{9,1},{13,5},{2,10},{6,14},... | collective-permute-start | bytes 24584 | tf_op jit(solution)/shard_map/ppermute | solution.py:32
  73.5 3.4 %shard_map.123 = (bf16[10,208,384]{2,1,0:T(8,128)(2,1)S(1)}, bf16[10,192,384]{2,1,0:T(8,128)(2,1)S(1)}, f32[8,192,384]{2,1,0:T(8,128)S(1)}, f32[8,128]{1,0:T(8,128)S(1)}, f32[2,8,384]{2,1,0:T(8,128)S(1)}) custom-call(f32[8]{0:T(128)S(1)} %convert_element_type.78.refs_0_, s32[10]{0:T(128)S(1)} %copy-done.4, f32[2,8,128]{2,1,0:T(8,128)S(1)} %pad_maximum_fusion.8.refs_2_, ...), custom_call_target="tpu_custom_call" | custom-call | flops 23592960 | bytes 11563080 | tf_op jit(solution)/shard_map/pallas_call | solution.py:764
  80.7 2.3 %shard_map.125.refs_10_.refs_7_ = f32[12,320,128]{2,1,0:T(8,128)S(1)} custom-call(s32[10]{0:T(128)S(1)} %copy-done.4, f32[16,24,320]{2,1,0:T(8,128)S(1)} %copy-done, f32[4,8,384]{2,1,0:T(8,128)S(1)} %shard_map.114.refs_7_.refs_5_.refs_2_.refs_1_.refs_4_, bf16[10,208,384]{2,1,0:T(8,128)(2,1)S(1)} %get-tuple-element.161.refs_3_.refs_6_, ...), custom_call_target="tpu_custom_call" | custom-call | flops 1415577600 | bytes 5578792 | tf_op jit(solution)/shard_map/pallas_call | solution.py:764
  84.6 4.8 %shard_map.126 = (f32[4,16,24,320]{3,2,1,0:T(8,128)}, f32[1,4,4,24,320]{4,3,2,1,0:T(8,128)S(1)}) custom-call(s32[10]{0:T(128)S(1)} %copy-done.4, f32[4,8,384]{2,1,0:T(8,128)S(1)} %shard_map.114.refs_7_.refs_5_.refs_2_.refs_1_.refs_4_, f32[16,24,320]{2,1,0:T(8,128)S(1)} %copy-done.1, f32[8,192,384]{2,1,0:T(8,128)S(1)} %get-tuple-element.127.refs_9_.refs_3_.refs_1_, ...), custom_call_target="tpu_custom_call" | custom-call | flops 1415577600 | bytes 12165160 | tf_op jit(solution)/shard_map/pallas_call | solution.py:764
  94.4 2.4 %collective-permute-start.19 = (f32[8,128]{1,0:T(8,128)S(1)}, f32[8,128]{1,0:T(8,128)S(1)}, u32[]{:S(2)}, u32[]{:S(2)}) collective-permute-start(f32[8,128]{1,0:T(8,128)S(1)} %add.261), channel_id=1, source_target_pairs={{0,8},{4,12},{8,0},{12,4},{1,9},{5,13},{9,1},{13,5},{2,10},{6,14},... | collective-permute-start | bytes 12296 | tf_op jit(solution)/shard_map/ppermute | solution.py:32
  98.9 5.1 %shard_map.127 = (f32[2,12,160,128]{3,2,1,0:T(8,128)S(1)}, f32[16,128]{1,0:T(8,128)S(1)}, bf16[320,1536]{1,0:T(8,128)(2,1)S(1)}) custom-call(s32[10]{0:T(128)S(1)} %copy-done.4, f32[8,192,384]{2,1,0:T(8,128)S(1)} %get-tuple-element.127.refs_9_.refs_3_.refs_1_, f32[2,8,384]{2,1,0:T(8,128)S(1)} %get-tuple-element.157.refs_2_, f32[8,128]{1,0:T(8,128)S(1)} %add.262.refs_3_, ...), custom_call_target="tpu_custom_call" | custom-call | flops 1415577600 | bytes 1000000 | tf_op jit(solution)/shard_map/pallas_call | solution.py:764
  108.8 4.8 %shard_map.129 = (f32[4,16,24,320]{3,2,1,0:T(8,128)}, f32[1,4,4,24,320]{4,3,2,1,0:T(8,128)S(1)}) custom-call(s32[10]{0:T(128)S(1)} %copy-done.4, f32[4,8,384]{2,1,0:T(8,128)S(1)} %shard_map.114.refs_7_.refs_5_.refs_2_.refs_1_.refs_4_, f32[16,24,320]{2,1,0:T(8,128)S(1)} %copy-done.1, ...), custom_call_target="tpu_custom_call", output_to_operand_aliasing={{0}: (9, {})} | custom-call | flops 1415577600 | bytes 14131240 | tf_op jit(solution)/shard_map/pallas_call | solution.py:764
  113.7 3.5 %collective-permute-done.22 = f16[2,1,6,2,2,40,128]{6,5,4,3,2,1,0:T(8,128)(2,1)S(1)} collective-permute-done((f16[2,1,6,2,2,40,128]{6,5,4,3,2,1,0:T(8,128)(2,1)S(1)}, f16[2,1,6,2,2,40,128]{6,5,4,3,2,1,0:T(8,128)(2,1)S(1)}, u32[]{:S(2)}, u32[]{:S(2)}) %collective-permute-start.22) | collective-permute-done | bytes 491552 | tf_op jit(solution)/shard_map/ppermute | solution.py:857
  120.4 3.2 %collective-permute-done.23 = f16[2,1,6,1,2,40,128]{6,5,4,3,2,1,0:T(8,128)(2,1)S(1)} collective-permute-done((f16[2,1,6,1,2,40,128]{6,5,4,3,2,1,0:T(8,128)(2,1)S(1)}, f16[2,1,6,1,2,40,128]{6,5,4,3,2,1,0:T(8,128)(2,1)S(1)}, u32[]{:S(2)}, u32[]{:S(2)}) %collective-permute-start.23) | collective-permute-done | bytes 245792 | tf_op jit(solution)/shard_map/ppermute | solution.py:857
  124.6 3.0 %collective-permute-start.26 = (f16[1,1,6,1,1,40,128]{6,5,4,3,2,1,0:T(8,128)(2,1)S(1)}, f16[1,1,6,1,1,40,128]{6,5,4,3,2,1,0:T(8,128)(2,1)S(1)}, u32[]{:S(2)}, u32[]{:S(2)}) collective-permute-start(f16[1,1,6,1,1,40,128]{6,5,4,3,2,1,0:T(8,128)(2,1)S(1)} %get-tuple-element.211), channel_id=1, source_target_pairs={{0,24},{4,28},{8,16},{12,20},{16,8},{20,12},{24,0},{28,4},{1,25},{... | collective-permute-start | bytes 184328 | tf_op jit(solution)/shard_map/ppermute | solution.py:864
  128.5 3.5 %collective-permute-done.26 = f16[1,1,6,1,1,40,128]{6,5,4,3,2,1,0:T(8,128)(2,1)S(1)} collective-permute-done((f16[1,1,6,1,1,40,128]{6,5,4,3,2,1,0:T(8,128)(2,1)S(1)}, f16[1,1,6,1,1,40,128]{6,5,4,3,2,1,0:T(8,128)(2,1)S(1)}, u32[]{:S(2)}, u32[]{:S(2)}) %collective-permute-start.26) | collective-permute-done | bytes 61472 | tf_op jit(solution)/shard_map/ppermute | solution.py:864
  134.5 3.3 %collective-permute-start.28 = (f16[1,1,6,1,1,40,128]{6,5,4,3,2,1,0:T(8,128)(2,1)S(1)}, f16[1,1,6,1,1,40,128]{6,5,4,3,2,1,0:T(8,128)(2,1)S(1)}, u32[]{:S(2)}, u32[]{:S(2)}) collective-permute-start(f16[1,1,6,1,1,40,128]{6,5,4,3,2,1,0:T(8,128)(2,1)S(1)} %add_convert_fusion.1), channel_id=1, source_target_pairs={{0,4},{1,3},{2,6},{3,1},{4,0},{5,7},{6,2},{7,5},{8,12},{9,11},{10,... | collective-permute-start | bytes 184328 | tf_op jit(solution)/shard_map/ppermute | solution.py:857
  140.1 4.5 %collective-permute-done.29 = f16[1,1,6,1,1,40,128]{6,5,4,3,2,1,0:T(8,128)(2,1)S(1)} collective-permute-done((f16[1,1,6,1,1,40,128]{6,5,4,3,2,1,0:T(8,128)(2,1)S(1)}, f16[1,1,6,1,1,40,128]{6,5,4,3,2,1,0:T(8,128)(2,1)S(1)}, u32[]{:S(2)}, u32[]{:S(2)}) %collective-permute-start.29) | collective-permute-done | bytes 61472 | tf_op jit(solution)/shard_map/ppermute | solution.py:857
  146.9 4.2 %collective-permute-done.31 = f16[1,1,6,2,2,40,128]{6,5,4,3,2,1,0:T(8,128)(2,1)S(1)} collective-permute-done((f16[1,1,6,2,2,40,128]{6,5,4,3,2,1,0:T(8,128)(2,1)S(1)}, f16[1,1,6,2,2,40,128]{6,5,4,3,2,1,0:T(8,128)(2,1)S(1)}, u32[]{:S(2)}, u32[]{:S(2)}) %collective-permute-start.31) | collective-permute-done | bytes 245792 | tf_op jit(solution)/shard_map/ppermute | solution.py:857
  (112 shorter events, 61.8 us)
Async XLA Ops:
  6.9 9.0 %collective-permute-start.4 = (f32[1,4,4,384]{3,2,1,0:T(4,128)}, f32[1,4,4,384]{3,2,1,0:T(4,128)S(1)}, u32[]{:S(2)}, u32[]{:S(2)}) collective-permute-start(f32[1,4,4,384]{3,2,1,0:T(4,128)} %bitcast.28), channel_id=1, source_target_pairs={{0,16},{16,0},{1,17},{17,1},{2,18},{18,2},{3,19},{19,3},{4,20},{20... | collective-permute-start | bytes 73736 | tf_op jit(solution)/shard_map/ppermute | solution.py:960
  9.9 16.0 %all-to-all-start = ((f32[16,32,128]{2,1,0:T(8,128)}), f32[16,32,128]{2,1,0:T(8,128)S(1)}, u32[]{:S(2)}, u32[]{:S(2)}) async-start(f32[16,32,128]{2,1,0:T(8,128)} %get-tuple-element.115), calls=%async_computation | async-start | bytes 524288 | tf_op jit(solution)/shard_map/all_to_all | solution.py:41
  15.8 15.9 %collective-permute-start.5 = (bf16[1,4,8,24,320]{4,3,2,1,0:T(8,128)(2,1)}, bf16[1,4,8,24,320]{4,3,2,1,0:T(8,128)(2,1)S(1)}, u32[]{:S(2)}, u32[]{:S(2)}) collective-permute-start(bf16[1,4,8,24,320]{4,3,2,1,0:T(8,128)(2,1)} %get-tuple-element.120), channel_id=1, source_target_pairs={{0,16},{16,0},{1,17},{17,1},{2,18},{18,2},{3,19},{19,3},{4,20},{20... | collective-permute-start | bytes 1474568 | tf_op jit(solution)/shard_map/ppermute | solution.py:960
  16.4 12.7 %collective-permute-start = (f32[2,24,320]{2,1,0:T(8,128)}, f32[2,24,320]{2,1,0:T(8,128)S(1)}, u32[]{:S(2)}, u32[]{:S(2)}) collective-permute-start(f32[2,24,320]{2,1,0:T(8,128)} %get-tuple-element.111), channel_id=1, source_target_pairs={{0,4},{4,8},{8,12},{1,5},{5,9},{9,13},{2,6},{6,10},{10,14},{3,7},{... | collective-permute-start | bytes 184328 | tf_op jit(solution)/shard_map/ppermute | solution.py:965
  20.3 8.8 %collective-permute-start.1 = (f32[2,24,320]{2,1,0:T(8,128)}, f32[2,24,320]{2,1,0:T(8,128)S(1)}, u32[]{:S(2)}, u32[]{:S(2)}) collective-permute-start(f32[2,24,320]{2,1,0:T(8,128)} %get-tuple-element.112), channel_id=1, source_target_pairs={{4,0},{8,4},{12,8},{5,1},{9,5},{13,9},{6,2},{10,6},{14,10},{7,3},{... | collective-permute-start | bytes 184328 | tf_op jit(solution)/shard_map/ppermute | solution.py:966
  21.6 7.5 %collective-permute-start.2 = (f32[2,16,320]{2,1,0:T(8,128)}, f32[2,16,320]{2,1,0:T(8,128)S(1)}, u32[]{:S(2)}, u32[]{:S(2)}) collective-permute-start(f32[2,16,320]{2,1,0:T(8,128)} %get-tuple-element.113), channel_id=1, source_target_pairs={{0,1},{1,2},{2,3},{4,5},{5,6},{6,7},{8,9},{9,10},{10,11},{12,13},{... | collective-permute-start | bytes 122888 | tf_op jit(solution)/shard_map/ppermute | solution.py:967
  23.1 6.0 %collective-permute-start.3 = (f32[2,16,320]{2,1,0:T(8,128)}, f32[2,16,320]{2,1,0:T(8,128)S(1)}, u32[]{:S(2)}, u32[]{:S(2)}) collective-permute-start(f32[2,16,320]{2,1,0:T(8,128)} %get-tuple-element.114), channel_id=1, source_target_pairs={{1,0},{2,1},{3,2},{5,4},{6,5},{7,6},{9,8},{10,9},{11,10},{13,12},{... | collective-permute-start | bytes 122888 | tf_op jit(solution)/shard_map/ppermute | solution.py:968
  35.8 12.6 %collective-permute-start.7 = (f32[1,192,384]{2,1,0:T(8,128)S(1)}, f32[1,192,384]{2,1,0:T(8,128)S(1)}, u32[]{:S(2)}, u32[]{:S(2)}) collective-permute-start(f32[1,192,384]{2,1,0:T(8,128)S(1)} %get-tuple-element.123.refs_1_), channel_id=1, source_target_pairs={{16,0},{20,16},{4,20},{8,4},{24,8},{28,24},{12,28},{17,1},{21,17},... | collective-permute-start | bytes 884744 | tf_op jit(solution)/shard_map/ppermute | solution.py:1003
  37.1 11.3 %collective-permute-start.6 = (f32[1,192,384]{2,1,0:T(8,128)S(1)}, f32[1,192,384]{2,1,0:T(8,128)S(1)}, u32[]{:S(2)}, u32[]{:S(2)}) collective-permute-start(f32[1,192,384]{2,1,0:T(8,128)S(1)} %get-tuple-element.124.refs_2_), channel_id=1, source_target_pairs={{0,16},{16,20},{20,4},{4,8},{8,24},{24,28},{28,12},{1,17},{17,21},... | collective-permute-start | bytes 884744 | tf_op jit(solution)/shard_map/ppermute | solution.py:1002
  48.5 8.0 %collective-permute-start.9 = (f32[10,8,384]{2,1,0:T(8,128)S(1)}, f32[10,8,384]{2,1,0:T(8,128)S(1)}, u32[]{:S(2)}, u32[]{:S(2)}) collective-permute-start(f32[10,8,384]{2,1,0:T(8,128)S(1)} %get-tuple-element.136), channel_id=1, source_target_pairs={{0,1},{1,2},{2,3},{4,5},{5,6},{6,7},{8,9},{9,10},{10,11},{12,13},{... | collective-permute-start | bytes 368648 | tf_op jit(solution)/shard_map/ppermute | solution.py:1020
  49.8 6.7 %collective-permute-start.10 = (f32[10,8,384]{2,1,0:T(8,128)S(1)}, f32[10,8,384]{2,1,0:T(8,128)S(1)}, u32[]{:S(2)}, u32[]{:S(2)}) collective-permute-start(f32[10,8,384]{2,1,0:T(8,128)S(1)} %get-tuple-element.137), channel_id=1, source_target_pairs={{1,0},{2,1},{3,2},{5,4},{6,5},{7,6},{9,8},{10,9},{11,10},{13,12},{... | collective-permute-start | bytes 368648 | tf_op jit(solution)/shard_map/ppermute | solution.py:1020
  51.2 5.2 %collective-permute-start.8 = (f32[2,8,128]{2,1,0:T(8,128)S(1)}, f32[2,8,128]{2,1,0:T(8,128)S(1)}, u32[]{:S(2)}, u32[]{:S(2)}) collective-permute-start(f32[2,8,128]{2,1,0:T(8,128)S(1)} %get-tuple-element.131), channel_id=1, source_target_pairs={{0,1},{1,0},{2,3},{3,2},{4,5},{5,4},{6,7},{7,6},{8,9},{9,8},{10,11... | collective-permute-start | bytes 24584 | tf_op jit(solution)/shard_map/ppermute | solution.py:32
  83.1 6.4 %collective-permute-start.17 = (f32[8,128]{1,0:T(8,128)S(1)}, f32[8,128]{1,0:T(8,128)S(1)}, u32[]{:S(2)}, u32[]{:S(2)}) collective-permute-start(f32[8,128]{1,0:T(8,128)S(1)} %add.259), channel_id=1, source_target_pairs={{0,2},{1,3},{2,0},{3,1},{4,6},{5,7},{6,4},{7,5},{8,10},{9,11},{10,... | collective-permute-start | bytes 12296 | tf_op jit(solution)/shard_map/ppermute | solution.py:32
  89.5 14.5 %collective-permute-start.20 = (f16[1,4,4,24,320]{4,3,2,1,0:T(8,128)(2,1)S(1)}, f16[1,4,4,24,320]{4,3,2,1,0:T(8,128)(2,1)S(1)}, u32[]{:S(2)}, u32[]{:S(2)}) collective-permute-start(f16[1,4,4,24,320]{4,3,2,1,0:T(8,128)(2,1)S(1)} %convert_element_type.87), channel_id=1, source_target_pairs={{0,16},{16,0},{1,17},{17,1},{2,18},{18,2},{3,19},{19,3},{4,20},{20... | collective-permute-start | bytes 737288 | tf_op jit(solution)/shard_map/ppermute | solution.py:960
  108.2 8.9 %collective-permute-start.22 = (f16[2,1,6,2,2,40,128]{6,5,4,3,2,1,0:T(8,128)(2,1)S(1)}, f16[2,1,6,2,2,40,128]{6,5,4,3,2,1,0:T(8,128)(2,1)S(1)}, u32[]{:S(2)}, u32[]{:S(2)}) collective-permute-start(f16[2,1,6,2,2,40,128]{6,5,4,3,2,1,0:T(8,128)(2,1)S(1)} %add_convert_fusion), channel_id=1, source_target_pairs={{0,2},{1,5},{2,0},{3,7},{4,6},{5,1},{6,4},{7,3},{8,10},{9,13},{10,... | collective-permute-start | bytes 1474568 | tf_op jit(solution)/shard_map/ppermute | solution.py:857
  117.3 6.3 %collective-permute-start.23 = (f16[2,1,6,1,2,40,128]{6,5,4,3,2,1,0:T(8,128)(2,1)S(1)}, f16[2,1,6,1,2,40,128]{6,5,4,3,2,1,0:T(8,128)(2,1)S(1)}, u32[]{:S(2)}, u32[]{:S(2)}) collective-permute-start(f16[2,1,6,1,2,40,128]{6,5,4,3,2,1,0:T(8,128)(2,1)S(1)} %dynamic-slice_convert_fusion), channel_id=1, source_target_pairs={{0,4},{1,3},{2,6},{3,1},{4,0},{5,7},{6,2},{7,5},{8,12},{9,11},{10,... | collective-permute-start | bytes 737288 | tf_op jit(solution)/shard_map/ppermute | solution.py:857
  123.7 4.8 %collective-permute-start.24 = (f16[1,1,6,1,1,40,128]{6,5,4,3,2,1,0:T(8,128)(2,1)S(1)}, f16[1,1,6,1,1,40,128]{6,5,4,3,2,1,0:T(8,128)(2,1)S(1)}, u32[]{:S(2)}, u32[]{:S(2)}) collective-permute-start(f16[1,1,6,1,1,40,128]{6,5,4,3,2,1,0:T(8,128)(2,1)S(1)} %get-tuple-element.210), channel_id=1, source_target_pairs={{0,16},{4,20},{8,24},{12,28},{16,0},{20,4},{24,8},{28,12},{1,17},{... | collective-permute-start | bytes 184328 | tf_op jit(solution)/shard_map/ppermute | solution.py:864
  124.6 7.3 %collective-permute-start.26 = (f16[1,1,6,1,1,40,128]{6,5,4,3,2,1,0:T(8,128)(2,1)S(1)}, f16[1,1,6,1,1,40,128]{6,5,4,3,2,1,0:T(8,128)(2,1)S(1)}, u32[]{:S(2)}, u32[]{:S(2)}) collective-permute-start(f16[1,1,6,1,1,40,128]{6,5,4,3,2,1,0:T(8,128)(2,1)S(1)} %get-tuple-element.211), channel_id=1, source_target_pairs={{0,24},{4,28},{8,16},{12,20},{16,8},{20,12},{24,0},{28,4},{1,25},{... | collective-permute-start | bytes 184328 | tf_op jit(solution)/shard_map/ppermute | solution.py:864
  127.6 5.1 %collective-permute-start.25 = (f16[1,1,6,1,1,40,128]{6,5,4,3,2,1,0:T(8,128)(2,1)S(1)}, f16[1,1,6,1,1,40,128]{6,5,4,3,2,1,0:T(8,128)(2,1)S(1)}, u32[]{:S(2)}, u32[]{:S(2)}) collective-permute-start(f16[1,1,6,1,1,40,128]{6,5,4,3,2,1,0:T(8,128)(2,1)S(1)} %get-tuple-element.212), channel_id=1, source_target_pairs={{0,8},{4,12},{8,0},{12,4},{16,24},{20,28},{24,16},{28,20},{1,9},{5... | collective-permute-start | bytes 184328 | tf_op jit(solution)/shard_map/ppermute | solution.py:864
  132.8 6.5 %collective-permute-start.27 = (f16[1,1,6,1,1,40,128]{6,5,4,3,2,1,0:T(8,128)(2,1)S(1)}, f16[1,1,6,1,1,40,128]{6,5,4,3,2,1,0:T(8,128)(2,1)S(1)}, u32[]{:S(2)}, u32[]{:S(2)}) collective-permute-start(f16[1,1,6,1,1,40,128]{6,5,4,3,2,1,0:T(8,128)(2,1)S(1)} %add_convert_fusion.1), channel_id=1, source_target_pairs={{0,8},{1,9},{2,10},{3,11},{4,12},{5,13},{6,14},{7,15},{8,0},{9,1},... | collective-permute-start | bytes 184328 | tf_op jit(solution)/shard_map/ppermute | solution.py:857
  133.6 11.2 %collective-permute-start.30 = (f16[1,4,4,24,320]{4,3,2,1,0:T(8,128)(2,1)S(1)}, f16[1,4,4,24,320]{4,3,2,1,0:T(8,128)(2,1)S(1)}, u32[]{:S(2)}, u32[]{:S(2)}) collective-permute-start(f16[1,4,4,24,320]{4,3,2,1,0:T(8,128)(2,1)S(1)} %convert_element_type.100), channel_id=1, source_target_pairs={{0,16},{16,0},{1,17},{17,1},{2,18},{18,2},{3,19},{19,3},{4,20},{20... | collective-permute-start | bytes 737288 | tf_op jit(solution)/shard_map/ppermute | solution.py:960
  134.5 5.5 %collective-permute-start.28 = (f16[1,1,6,1,1,40,128]{6,5,4,3,2,1,0:T(8,128)(2,1)S(1)}, f16[1,1,6,1,1,40,128]{6,5,4,3,2,1,0:T(8,128)(2,1)S(1)}, u32[]{:S(2)}, u32[]{:S(2)}) collective-permute-start(f16[1,1,6,1,1,40,128]{6,5,4,3,2,1,0:T(8,128)(2,1)S(1)} %add_convert_fusion.1), channel_id=1, source_target_pairs={{0,4},{1,3},{2,6},{3,1},{4,0},{5,7},{6,2},{7,5},{8,12},{9,11},{10,... | collective-permute-start | bytes 184328 | tf_op jit(solution)/shard_map/ppermute | solution.py:857
  137.9 6.7 %collective-permute-start.29 = (f16[1,1,6,1,1,40,128]{6,5,4,3,2,1,0:T(8,128)(2,1)S(1)}, f16[1,1,6,1,1,40,128]{6,5,4,3,2,1,0:T(8,128)(2,1)S(1)}, u32[]{:S(2)}, u32[]{:S(2)}) collective-permute-start(f16[1,1,6,1,1,40,128]{6,5,4,3,2,1,0:T(8,128)(2,1)S(1)} %add_convert_fusion.1), channel_id=1, source_target_pairs={{0,12},{1,11},{2,14},{3,9},{4,8},{5,15},{6,10},{7,13},{8,4},{9,3},... | collective-permute-start | bytes 184328 | tf_op jit(solution)/shard_map/ppermute | solution.py:857
  144.8 6.3 %collective-permute-start.31 = (f16[1,1,6,2,2,40,128]{6,5,4,3,2,1,0:T(8,128)(2,1)S(1)}, f16[1,1,6,2,2,40,128]{6,5,4,3,2,1,0:T(8,128)(2,1)S(1)}, u32[]{:S(2)}, u32[]{:S(2)}) collective-permute-start(f16[1,1,6,2,2,40,128]{6,5,4,3,2,1,0:T(8,128)(2,1)S(1)} %pad_maximum_fusion.1), channel_id=1, source_target_pairs={{0,2},{1,5},{2,0},{3,7},{4,6},{5,1},{6,4},{7,3},{8,10},{9,13},{10,... | collective-permute-start | bytes 737288 | tf_op jit(solution)/shard_map/ppermute | solution.py:857
  (16 other events, 124.8 us)

commit v5 on v4

--- a/solution.py
+++ b/solution.py
@@ -887,11 +887,12 @@
     value = value.astype(F16)
     sends = [(flips, send_tile(1, flips[1], flips[0])) for flips in FLIPS]
     value = joint_gather(value, (far, second), (4, 3), sends)
+    value = both_halves(value, first, send_tile(0, 1, 0), 1)
     value, landing = lax.optimization_barrier((value, landing))
-    value = both_halves(value, first, send_tile(0, 1, 0), 1)
-    value, trajectory = lax.optimization_barrier((value, land(landing, trajectory, 1)))
     value = value.reshape(tiles, share_rows, lanes)
-    return value.astype(F32), swap(value, "sx", 1).astype(F32), trajectory
+    other = swap(value, "sx", 1)
+    other, trajectory = lax.optimization_barrier((other, land(landing, trajectory, 1)))
+    return value.astype(F32), other.astype(F32), trajectory
 
 
 def shards(
@@ -977,7 +978,7 @@
     )
     packed = ((9 * (lanes - LANES) + 5 * LANES, lanes), BF16)
     weight_out, weight_back = call(
-        pack_weight_kernel, [packed, packed], [], 10**7, load=[conv_weight.reshape(9, channels, channels)],
+        pack_weight_kernel, [packed, packed], [], 10**7, vmem=[conv_weight.reshape(9, channels, channels)],
     )
 
     even_shape = (rows + 2, (cols + 2) * steps, lanes)

time: 156 us -> 155 us (level)
  transfers between devices with their start and end apart: 34 -> 34, of which waited for: 16 -> 17; matrix products, arithmetic and copies ran while one was open for 0% -> 0% of each run, Pallas kernels for 27% -> 27%
where the time goes in v5:
time: 155 us
  starting transfers between devices  57.4 us (37%)
  Pallas kernels  56.2 us (36%)
  waiting for transfers between devices  35.3 us (23%)
  local copies, waits for them, and re-layouts  3.08 us (2%)
    pallas_call x20, Pallas kernels, call(): pl.pallas_call(body, out_shape=shapes, in_specs=specs, out_specs=out_spec...  56.2 us
    ppermute x6, waiting for transfers between devices, send_tile(): return lambda value: lax.ppermute(value, ('sy', 'sx'), pairs)  17.9 us
    ppermute x12, starting transfers between devices, swap(): return lax.ppermute(value, axis, pairs)  17.6 us
    ppermute x12, waiting for transfers between devices, swap(): return lax.ppermute(value, axis, pairs)  8.49 us
    ppermute x6, starting transfers between devices, send_tile(): return lambda value: lax.ppermute(value, ('sy', 'sx'), pairs)  7.12 us
    all_to_all x1, starting transfers between devices, share(): return lax.all_to_all(copies, axes, 0, 0)  5.94 us
    ppermute x4, starting transfers between devices, to_slabs(): return lax.ppermute(pieces, 'tm', shifted(1))  5.76 us
    ppermute x3, waiting for transfers between devices, send_slab(): return lambda value: lax.ppermute(value, ('tm', 'sy'), pairs)  4.59 us
  transfers between devices with their start and end apart: 34, of which 17 were waited for; matrix products, arithmetic and copies ran while one was open for 0% of the time, Pallas kernels for 27%

profile of v5, /device:TPU:0, one launch (start us, length us, event | category | flops | bytes accessed | tf_op | source)
XLA Modules:
  0.0 154.7 jit_solution(13673164306542757040)
XLA Ops:
  1.5 5.3 %shard_map.113 = (f32[16,32,128]{2,1,0:T(8,128)}, f32[4,4,384]{2,1,0:T(4,128)}, f32[2,24,320]{2,1,0:T(8,128)}, f32[2,24,320]{2,1,0:T(8,128)}, f32[2,16,320]{2,1,...) custom-call(s32[4]{0:T(128)} %refs_0_.1, s32[10]{0:T(128)} %stack.88.refs_1_.refs_0_, f32[4]{0:T(128)} %refs_2_.1, ...), custom_call_target="tpu_custom_call" | custom-call | flops 1000000 | bytes 4230504 | tf_op jit(solution)/shard_map/pallas_call | solution.py:764
  6.9 3.0 %collective-permute-start.4 = (f32[1,4,4,384]{3,2,1,0:T(4,128)}, f32[1,4,4,384]{3,2,1,0:T(4,128)S(1)}, u32[]{:S(2)}, u32[]{:S(2)}) collective-permute-start(f32[1,4,4,384]{3,2,1,0:T(4,128)} %bitcast.28), channel_id=1, source_target_pairs={{0,16},{16,0},{1,17},{17,1},{2,18},{18,2},{3,19},{19,3},{4,20},{20... | collective-permute-start | bytes 73736 | tf_op jit(solution)/shard_map/ppermute | solution.py:961
  9.9 5.9 %all-to-all-start = ((f32[16,32,128]{2,1,0:T(8,128)}), f32[16,32,128]{2,1,0:T(8,128)S(1)}, u32[]{:S(2)}, u32[]{:S(2)}) async-start(f32[16,32,128]{2,1,0:T(8,128)} %get-tuple-element.115), calls=%async_computation | async-start | bytes 524288 | tf_op jit(solution)/shard_map/all_to_all | solution.py:41
  16.4 3.8 %collective-permute-start = (f32[2,24,320]{2,1,0:T(8,128)}, f32[2,24,320]{2,1,0:T(8,128)S(1)}, u32[]{:S(2)}, u32[]{:S(2)}) collective-permute-start(f32[2,24,320]{2,1,0:T(8,128)} %get-tuple-element.111), channel_id=1, source_target_pairs={{0,4},{4,8},{8,12},{1,5},{5,9},{9,13},{2,6},{6,10},{10,14},{3,7},{... | collective-permute-start | bytes 184328 | tf_op jit(solution)/shard_map/ppermute | solution.py:966
  28.5 3.3 %collective-permute-done.5.refs_9_.refs_7_.refs_4_ = bf16[1,4,8,24,320]{4,3,2,1,0:T(8,128)(2,1)S(1)} collective-permute-done((bf16[1,4,8,24,320]{4,3,2,1,0:T(8,128)(2,1)}, bf16[1,4,8,24,320]{4,3,2,1,0:T(8,128)(2,1)S(1)}, u32[]{:S(2)}, u32[]{:S(2)}) %collective-permute-start.5) | collective-permute-done | bytes 491552 | tf_op jit(solution)/shard_map/ppermute | solution.py:961
  31.8 4.0 %shard_map.116 = (bf16[10,208,384]{2,1,0:T(8,128)(2,1)S(1)}, bf16[10,192,384]{2,1,0:T(8,128)(2,1)S(1)}, f32[2,2,18,384]{3,2,1,0:T(8,128)S(1)}, f32[1,192,384]{2,1,0:T(8,128)S(1)}, f32[1,192,384]{2,1,0:T(8,128)S(1)}) custom-call(f32[8]{0:T(128)S(1)} %convert_element_type.78.refs_0_, s32[10]{0:T(128)S(1)} %copy-done.4, ...), custom_call_target="tpu_custom_call" | custom-call | flops 707788800 | bytes 8515656 | tf_op jit(solution)/shard_map/pallas_call | solution.py:764
  37.1 4.6 %collective-permute-start.6 = (f32[1,192,384]{2,1,0:T(8,128)S(1)}, f32[1,192,384]{2,1,0:T(8,128)S(1)}, u32[]{:S(2)}, u32[]{:S(2)}) collective-permute-start(f32[1,192,384]{2,1,0:T(8,128)S(1)} %get-tuple-element.124.refs_2_), channel_id=1, source_target_pairs={{0,16},{16,20},{20,4},{4,8},{8,24},{24,28},{28,12},{1,17},{17,21},... | collective-permute-start | bytes 884744 | tf_op jit(solution)/shard_map/ppermute | solution.py:1003
  41.7 6.7 %shard_map.117 = (f32[8,192,384]{2,1,0:T(8,128)S(1)}, f32[2,8,128]{2,1,0:T(8,128)S(1)}, f32[8,8,384]{2,1,0:T(8,128)S(1)}, f32[8,8,384]{2,1,0:T(8,128)S(1)}) custom-call(s32[10]{0:T(128)S(1)} %copy-done.4, f32[1,192,384]{2,1,0:T(8,128)S(1)} %get-tuple-element.123.refs_1_, f32[1,192,384]{2,1,0:T(8,128)S(1)} %get-tuple-element.124.refs_2_, ...), custom_call_target="tpu_custom_call" | custom-call | flops 2831155200 | bytes 10502184 | tf_op jit(solution)/shard_map/pallas_call | solution.py:764
  51.2 3.1 %collective-permute-start.8 = (f32[2,8,128]{2,1,0:T(8,128)S(1)}, f32[2,8,128]{2,1,0:T(8,128)S(1)}, u32[]{:S(2)}, u32[]{:S(2)}) collective-permute-start(f32[2,8,128]{2,1,0:T(8,128)S(1)} %get-tuple-element.131), channel_id=1, source_target_pairs={{0,1},{1,0},{2,3},{3,2},{4,5},{5,4},{6,7},{7,6},{8,9},{9,8},{10,11... | collective-permute-start | bytes 24584 | tf_op jit(solution)/shard_map/ppermute | solution.py:32
  64.5 2.4 %collective-permute-start.13 = (f32[2,8,128]{2,1,0:T(8,128)S(1)}, f32[2,8,128]{2,1,0:T(8,128)S(1)}, u32[]{:S(2)}, u32[]{:S(2)}) collective-permute-start(f32[2,8,128]{2,1,0:T(8,128)S(1)} %pad_maximum_fusion.6), channel_id=1, source_target_pairs={{0,8},{4,12},{8,0},{12,4},{1,9},{5,13},{9,1},{13,5},{2,10},{6,14},... | collective-permute-start | bytes 24584 | tf_op jit(solution)/shard_map/ppermute | solution.py:32
  72.8 3.4 %shard_map.123 = (bf16[10,208,384]{2,1,0:T(8,128)(2,1)S(1)}, bf16[10,192,384]{2,1,0:T(8,128)(2,1)S(1)}, f32[8,192,384]{2,1,0:T(8,128)S(1)}, f32[8,128]{1,0:T(8,128)S(1)}, f32[2,8,384]{2,1,0:T(8,128)S(1)}) custom-call(f32[8]{0:T(128)S(1)} %convert_element_type.78.refs_0_, s32[10]{0:T(128)S(1)} %copy-done.4, f32[2,8,128]{2,1,0:T(8,128)S(1)} %pad_maximum_fusion.8.refs_2_, ...), custom_call_target="tpu_custom_call" | custom-call | flops 23592960 | bytes 11563080 | tf_op jit(solution)/shard_map/pallas_call | solution.py:764
  77.6 2.3 %shard_map.124.refs_9_.refs_6_ = f32[12,320,128]{2,1,0:T(8,128)S(1)} custom-call(s32[10]{0:T(128)S(1)} %copy-done.4, f32[16,24,320]{2,1,0:T(8,128)S(1)} %copy-done, f32[4,8,384]{2,1,0:T(8,128)S(1)} %shard_map.114.refs_7_.refs_5_.refs_2_.refs_1_.refs_4_, bf16[10,208,384]{2,1,0:T(8,128)(2,1)S(1)} %get-tuple-element.161.refs_3_.refs_6_, ...), custom_call_target="tpu_custom_call" | custom-call | flops 1415577600 | bytes 5578792 | tf_op jit(solution)/shard_map/pallas_call | solution.py:764
  80.0 2.3 %shard_map.125.refs_10_.refs_7_ = f32[12,320,128]{2,1,0:T(8,128)S(1)} custom-call(s32[10]{0:T(128)S(1)} %copy-done.4, f32[16,24,320]{2,1,0:T(8,128)S(1)} %copy-done, f32[4,8,384]{2,1,0:T(8,128)S(1)} %shard_map.114.refs_7_.refs_5_.refs_2_.refs_1_.refs_4_, bf16[10,208,384]{2,1,0:T(8,128)(2,1)S(1)} %get-tuple-element.161.refs_3_.refs_6_, ...), custom_call_target="tpu_custom_call" | custom-call | flops 1415577600 | bytes 5578792 | tf_op jit(solution)/shard_map/pallas_call | solution.py:764
  84.0 4.8 %shard_map.126 = (f32[4,16,24,320]{3,2,1,0:T(8,128)}, f32[1,4,4,24,320]{4,3,2,1,0:T(8,128)S(1)}) custom-call(s32[10]{0:T(128)S(1)} %copy-done.4, f32[4,8,384]{2,1,0:T(8,128)S(1)} %shard_map.114.refs_7_.refs_5_.refs_2_.refs_1_.refs_4_, f32[16,24,320]{2,1,0:T(8,128)S(1)} %copy-done.1, f32[8,192,384]{2,1,0:T(8,128)S(1)} %get-tuple-element.127.refs_9_.refs_3_.refs_1_, ...), custom_call_target="tpu_custom_call" | custom-call | flops 1415577600 | bytes 12165160 | tf_op jit(solution)/shard_map/pallas_call | solution.py:764
  93.7 2.4 %collective-permute-start.19 = (f32[8,128]{1,0:T(8,128)S(1)}, f32[8,128]{1,0:T(8,128)S(1)}, u32[]{:S(2)}, u32[]{:S(2)}) collective-permute-start(f32[8,128]{1,0:T(8,128)S(1)} %add.261), channel_id=1, source_target_pairs={{0,8},{4,12},{8,0},{12,4},{1,9},{5,13},{9,1},{13,5},{2,10},{6,14},... | collective-permute-start | bytes 12296 | tf_op jit(solution)/shard_map/ppermute | solution.py:32
  98.3 5.1 %shard_map.127 = (f32[2,12,160,128]{3,2,1,0:T(8,128)S(1)}, f32[16,128]{1,0:T(8,128)S(1)}, bf16[320,1536]{1,0:T(8,128)(2,1)S(1)}) custom-call(s32[10]{0:T(128)S(1)} %copy-done.4, f32[8,192,384]{2,1,0:T(8,128)S(1)} %get-tuple-element.127.refs_9_.refs_3_.refs_1_, f32[2,8,384]{2,1,0:T(8,128)S(1)} %get-tuple-element.157.refs_2_, f32[8,128]{1,0:T(8,128)S(1)} %add.262.refs_3_, ...), custom_call_target="tpu_custom_call" | custom-call | flops 1415577600 | bytes 1000000 | tf_op jit(solution)/shard_map/pallas_call | solution.py:764
  108.2 4.8 %shard_map.129 = (f32[4,16,24,320]{3,2,1,0:T(8,128)}, f32[1,4,4,24,320]{4,3,2,1,0:T(8,128)S(1)}) custom-call(s32[10]{0:T(128)S(1)} %copy-done.4, f32[4,8,384]{2,1,0:T(8,128)S(1)} %shard_map.114.refs_7_.refs_5_.refs_2_.refs_1_.refs_4_, f32[16,24,320]{2,1,0:T(8,128)S(1)} %copy-done.1, ...), custom_call_target="tpu_custom_call", output_to_operand_aliasing={{0}: (9, {})} | custom-call | flops 1415577600 | bytes 14131240 | tf_op jit(solution)/shard_map/pallas_call | solution.py:764
  113.0 3.4 %collective-permute-done.22 = f16[2,1,6,2,2,40,128]{6,5,4,3,2,1,0:T(8,128)(2,1)S(1)} collective-permute-done((f16[2,1,6,2,2,40,128]{6,5,4,3,2,1,0:T(8,128)(2,1)S(1)}, f16[2,1,6,2,2,40,128]{6,5,4,3,2,1,0:T(8,128)(2,1)S(1)}, u32[]{:S(2)}, u32[]{:S(2)}) %collective-permute-start.22) | collective-permute-done | bytes 491552 | tf_op jit(solution)/shard_map/ppermute | solution.py:857
  119.7 3.2 %collective-permute-done.23 = f16[2,1,6,1,2,40,128]{6,5,4,3,2,1,0:T(8,128)(2,1)S(1)} collective-permute-done((f16[2,1,6,1,2,40,128]{6,5,4,3,2,1,0:T(8,128)(2,1)S(1)}, f16[2,1,6,1,2,40,128]{6,5,4,3,2,1,0:T(8,128)(2,1)S(1)}, u32[]{:S(2)}, u32[]{:S(2)}) %collective-permute-start.23) | collective-permute-done | bytes 245792 | tf_op jit(solution)/shard_map/ppermute | solution.py:857
  123.9 3.0 %collective-permute-start.26 = (f16[1,1,6,1,1,40,128]{6,5,4,3,2,1,0:T(8,128)(2,1)S(1)}, f16[1,1,6,1,1,40,128]{6,5,4,3,2,1,0:T(8,128)(2,1)S(1)}, u32[]{:S(2)}, u32[]{:S(2)}) collective-permute-start(f16[1,1,6,1,1,40,128]{6,5,4,3,2,1,0:T(8,128)(2,1)S(1)} %get-tuple-element.211), channel_id=1, source_target_pairs={{0,24},{4,28},{8,16},{12,20},{16,8},{20,12},{24,0},{28,4},{1,25},{... | collective-permute-start | bytes 184328 | tf_op jit(solution)/shard_map/ppermute | solution.py:864
  127.8 3.5 %collective-permute-done.26 = f16[1,1,6,1,1,40,128]{6,5,4,3,2,1,0:T(8,128)(2,1)S(1)} collective-permute-done((f16[1,1,6,1,1,40,128]{6,5,4,3,2,1,0:T(8,128)(2,1)S(1)}, f16[1,1,6,1,1,40,128]{6,5,4,3,2,1,0:T(8,128)(2,1)S(1)}, u32[]{:S(2)}, u32[]{:S(2)}) %collective-permute-start.26) | collective-permute-done | bytes 61472 | tf_op jit(solution)/shard_map/ppermute | solution.py:864
  132.9 3.3 %collective-permute-start.28 = (f16[1,1,6,1,1,40,128]{6,5,4,3,2,1,0:T(8,128)(2,1)S(1)}, f16[1,1,6,1,1,40,128]{6,5,4,3,2,1,0:T(8,128)(2,1)S(1)}, u32[]{:S(2)}, u32[]{:S(2)}) collective-permute-start(f16[1,1,6,1,1,40,128]{6,5,4,3,2,1,0:T(8,128)(2,1)S(1)} %add_convert_fusion.1), channel_id=1, source_target_pairs={{0,4},{1,3},{2,6},{3,1},{4,0},{5,7},{6,2},{7,5},{8,12},{9,11},{10,... | collective-permute-start | bytes 184328 | tf_op jit(solution)/shard_map/ppermute | solution.py:857
  138.5 4.5 %collective-permute-done.29 = f16[1,1,6,1,1,40,128]{6,5,4,3,2,1,0:T(8,128)(2,1)S(1)} collective-permute-done((f16[1,1,6,1,1,40,128]{6,5,4,3,2,1,0:T(8,128)(2,1)S(1)}, f16[1,1,6,1,1,40,128]{6,5,4,3,2,1,0:T(8,128)(2,1)S(1)}, u32[]{:S(2)}, u32[]{:S(2)}) %collective-permute-start.29) | collective-permute-done | bytes 61472 | tf_op jit(solution)/shard_map/ppermute | solution.py:857
  144.7 4.8 %collective-permute-done.30 = f16[1,1,6,2,2,40,128]{6,5,4,3,2,1,0:T(8,128)(2,1)S(1)} collective-permute-done((f16[1,1,6,2,2,40,128]{6,5,4,3,2,1,0:T(8,128)(2,1)S(1)}, f16[1,1,6,2,2,40,128]{6,5,4,3,2,1,0:T(8,128)(2,1)S(1)}, u32[]{:S(2)}, u32[]{:S(2)}) %collective-permute-start.30) | collective-permute-done | bytes 245792 | tf_op jit(solution)/shard_map/ppermute | solution.py:857
  (112 shorter events, 60.0 us)
Async XLA Ops:
  6.9 9.0 %collective-permute-start.4 = (f32[1,4,4,384]{3,2,1,0:T(4,128)}, f32[1,4,4,384]{3,2,1,0:T(4,128)S(1)}, u32[]{:S(2)}, u32[]{:S(2)}) collective-permute-start(f32[1,4,4,384]{3,2,1,0:T(4,128)} %bitcast.28), channel_id=1, source_target_pairs={{0,16},{16,0},{1,17},{17,1},{2,18},{18,2},{3,19},{19,3},{4,20},{20... | collective-permute-start | bytes 73736 | tf_op jit(solution)/shard_map/ppermute | solution.py:961
  9.9 16.0 %all-to-all-start = ((f32[16,32,128]{2,1,0:T(8,128)}), f32[16,32,128]{2,1,0:T(8,128)S(1)}, u32[]{:S(2)}, u32[]{:S(2)}) async-start(f32[16,32,128]{2,1,0:T(8,128)} %get-tuple-element.115), calls=%async_computation | async-start | bytes 524288 | tf_op jit(solution)/shard_map/all_to_all | solution.py:41
  15.8 15.9 %collective-permute-start.5 = (bf16[1,4,8,24,320]{4,3,2,1,0:T(8,128)(2,1)}, bf16[1,4,8,24,320]{4,3,2,1,0:T(8,128)(2,1)S(1)}, u32[]{:S(2)}, u32[]{:S(2)}) collective-permute-start(bf16[1,4,8,24,320]{4,3,2,1,0:T(8,128)(2,1)} %get-tuple-element.120), channel_id=1, source_target_pairs={{0,16},{16,0},{1,17},{17,1},{2,18},{18,2},{3,19},{19,3},{4,20},{20... | collective-permute-start | bytes 1474568 | tf_op jit(solution)/shard_map/ppermute | solution.py:961
  16.4 12.0 %collective-permute-start = (f32[2,24,320]{2,1,0:T(8,128)}, f32[2,24,320]{2,1,0:T(8,128)S(1)}, u32[]{:S(2)}, u32[]{:S(2)}) collective-permute-start(f32[2,24,320]{2,1,0:T(8,128)} %get-tuple-element.111), channel_id=1, source_target_pairs={{0,4},{4,8},{8,12},{1,5},{5,9},{9,13},{2,6},{6,10},{10,14},{3,7},{... | collective-permute-start | bytes 184328 | tf_op jit(solution)/shard_map/ppermute | solution.py:966
  20.3 8.2 %collective-permute-start.1 = (f32[2,24,320]{2,1,0:T(8,128)}, f32[2,24,320]{2,1,0:T(8,128)S(1)}, u32[]{:S(2)}, u32[]{:S(2)}) collective-permute-start(f32[2,24,320]{2,1,0:T(8,128)} %get-tuple-element.112), channel_id=1, source_target_pairs={{4,0},{8,4},{12,8},{5,1},{9,5},{13,9},{6,2},{10,6},{14,10},{7,3},{... | collective-permute-start | bytes 184328 | tf_op jit(solution)/shard_map/ppermute | solution.py:967
  21.6 6.9 %collective-permute-start.2 = (f32[2,16,320]{2,1,0:T(8,128)}, f32[2,16,320]{2,1,0:T(8,128)S(1)}, u32[]{:S(2)}, u32[]{:S(2)}) collective-permute-start(f32[2,16,320]{2,1,0:T(8,128)} %get-tuple-element.113), channel_id=1, source_target_pairs={{0,1},{1,2},{2,3},{4,5},{5,6},{6,7},{8,9},{9,10},{10,11},{12,13},{... | collective-permute-start | bytes 122888 | tf_op jit(solution)/shard_map/ppermute | solution.py:968
  23.1 5.4 %collective-permute-start.3 = (f32[2,16,320]{2,1,0:T(8,128)}, f32[2,16,320]{2,1,0:T(8,128)S(1)}, u32[]{:S(2)}, u32[]{:S(2)}) collective-permute-start(f32[2,16,320]{2,1,0:T(8,128)} %get-tuple-element.114), channel_id=1, source_target_pairs={{1,0},{2,1},{3,2},{5,4},{6,5},{7,6},{9,8},{10,9},{11,10},{13,12},{... | collective-permute-start | bytes 122888 | tf_op jit(solution)/shard_map/ppermute | solution.py:969
  35.8 12.6 %collective-permute-start.7 = (f32[1,192,384]{2,1,0:T(8,128)S(1)}, f32[1,192,384]{2,1,0:T(8,128)S(1)}, u32[]{:S(2)}, u32[]{:S(2)}) collective-permute-start(f32[1,192,384]{2,1,0:T(8,128)S(1)} %get-tuple-element.123.refs_1_), channel_id=1, source_target_pairs={{16,0},{20,16},{4,20},{8,4},{24,8},{28,24},{12,28},{17,1},{21,17},... | collective-permute-start | bytes 884744 | tf_op jit(solution)/shard_map/ppermute | solution.py:1004
  37.1 11.3 %collective-permute-start.6 = (f32[1,192,384]{2,1,0:T(8,128)S(1)}, f32[1,192,384]{2,1,0:T(8,128)S(1)}, u32[]{:S(2)}, u32[]{:S(2)}) collective-permute-start(f32[1,192,384]{2,1,0:T(8,128)S(1)} %get-tuple-element.124.refs_2_), channel_id=1, source_target_pairs={{0,16},{16,20},{20,4},{4,8},{8,24},{24,28},{28,12},{1,17},{17,21},... | collective-permute-start | bytes 884744 | tf_op jit(solution)/shard_map/ppermute | solution.py:1003
  48.5 8.0 %collective-permute-start.9 = (f32[10,8,384]{2,1,0:T(8,128)S(1)}, f32[10,8,384]{2,1,0:T(8,128)S(1)}, u32[]{:S(2)}, u32[]{:S(2)}) collective-permute-start(f32[10,8,384]{2,1,0:T(8,128)S(1)} %get-tuple-element.136), channel_id=1, source_target_pairs={{0,1},{1,2},{2,3},{4,5},{5,6},{6,7},{8,9},{9,10},{10,11},{12,13},{... | collective-permute-start | bytes 368648 | tf_op jit(solution)/shard_map/ppermute | solution.py:1021
  49.8 6.7 %collective-permute-start.10 = (f32[10,8,384]{2,1,0:T(8,128)S(1)}, f32[10,8,384]{2,1,0:T(8,128)S(1)}, u32[]{:S(2)}, u32[]{:S(2)}) collective-permute-start(f32[10,8,384]{2,1,0:T(8,128)S(1)} %get-tuple-element.137), channel_id=1, source_target_pairs={{1,0},{2,1},{3,2},{5,4},{6,5},{7,6},{9,8},{10,9},{11,10},{13,12},{... | collective-permute-start | bytes 368648 | tf_op jit(solution)/shard_map/ppermute | solution.py:1021
  51.2 5.2 %collective-permute-start.8 = (f32[2,8,128]{2,1,0:T(8,128)S(1)}, f32[2,8,128]{2,1,0:T(8,128)S(1)}, u32[]{:S(2)}, u32[]{:S(2)}) collective-permute-start(f32[2,8,128]{2,1,0:T(8,128)S(1)} %get-tuple-element.131), channel_id=1, source_target_pairs={{0,1},{1,0},{2,3},{3,2},{4,5},{5,4},{6,7},{7,6},{8,9},{9,8},{10,11... | collective-permute-start | bytes 24584 | tf_op jit(solution)/shard_map/ppermute | solution.py:32
  82.4 6.4 %collective-permute-start.17 = (f32[8,128]{1,0:T(8,128)S(1)}, f32[8,128]{1,0:T(8,128)S(1)}, u32[]{:S(2)}, u32[]{:S(2)}) collective-permute-start(f32[8,128]{1,0:T(8,128)S(1)} %add.259), channel_id=1, source_target_pairs={{0,2},{1,3},{2,0},{3,1},{4,6},{5,7},{6,4},{7,5},{8,10},{9,11},{10,... | collective-permute-start | bytes 12296 | tf_op jit(solution)/shard_map/ppermute | solution.py:32
  88.9 14.5 %collective-permute-start.20 = (f16[1,4,4,24,320]{4,3,2,1,0:T(8,128)(2,1)S(1)}, f16[1,4,4,24,320]{4,3,2,1,0:T(8,128)(2,1)S(1)}, u32[]{:S(2)}, u32[]{:S(2)}) collective-permute-start(f16[1,4,4,24,320]{4,3,2,1,0:T(8,128)(2,1)S(1)} %convert_element_type.87), channel_id=1, source_target_pairs={{0,16},{16,0},{1,17},{17,1},{2,18},{18,2},{3,19},{19,3},{4,20},{20... | collective-permute-start | bytes 737288 | tf_op jit(solution)/shard_map/ppermute | solution.py:961
  107.6 8.9 %collective-permute-start.22 = (f16[2,1,6,2,2,40,128]{6,5,4,3,2,1,0:T(8,128)(2,1)S(1)}, f16[2,1,6,2,2,40,128]{6,5,4,3,2,1,0:T(8,128)(2,1)S(1)}, u32[]{:S(2)}, u32[]{:S(2)}) collective-permute-start(f16[2,1,6,2,2,40,128]{6,5,4,3,2,1,0:T(8,128)(2,1)S(1)} %add_convert_fusion), channel_id=1, source_target_pairs={{0,2},{1,5},{2,0},{3,7},{4,6},{5,1},{6,4},{7,3},{8,10},{9,13},{10,... | collective-permute-start | bytes 1474568 | tf_op jit(solution)/shard_map/ppermute | solution.py:857
  116.7 6.3 %collective-permute-start.23 = (f16[2,1,6,1,2,40,128]{6,5,4,3,2,1,0:T(8,128)(2,1)S(1)}, f16[2,1,6,1,2,40,128]{6,5,4,3,2,1,0:T(8,128)(2,1)S(1)}, u32[]{:S(2)}, u32[]{:S(2)}) collective-permute-start(f16[2,1,6,1,2,40,128]{6,5,4,3,2,1,0:T(8,128)(2,1)S(1)} %dynamic-slice_convert_fusion), channel_id=1, source_target_pairs={{0,4},{1,3},{2,6},{3,1},{4,0},{5,7},{6,2},{7,5},{8,12},{9,11},{10,... | collective-permute-start | bytes 737288 | tf_op jit(solution)/shard_map/ppermute | solution.py:857
  123.0 4.8 %collective-permute-start.24 = (f16[1,1,6,1,1,40,128]{6,5,4,3,2,1,0:T(8,128)(2,1)S(1)}, f16[1,1,6,1,1,40,128]{6,5,4,3,2,1,0:T(8,128)(2,1)S(1)}, u32[]{:S(2)}, u32[]{:S(2)}) collective-permute-start(f16[1,1,6,1,1,40,128]{6,5,4,3,2,1,0:T(8,128)(2,1)S(1)} %get-tuple-element.210), channel_id=1, source_target_pairs={{0,16},{4,20},{8,24},{12,28},{16,0},{20,4},{24,8},{28,12},{1,17},{... | collective-permute-start | bytes 184328 | tf_op jit(solution)/shard_map/ppermute | solution.py:864
  123.9 7.3 %collective-permute-start.26 = (f16[1,1,6,1,1,40,128]{6,5,4,3,2,1,0:T(8,128)(2,1)S(1)}, f16[1,1,6,1,1,40,128]{6,5,4,3,2,1,0:T(8,128)(2,1)S(1)}, u32[]{:S(2)}, u32[]{:S(2)}) collective-permute-start(f16[1,1,6,1,1,40,128]{6,5,4,3,2,1,0:T(8,128)(2,1)S(1)} %get-tuple-element.211), channel_id=1, source_target_pairs={{0,24},{4,28},{8,16},{12,20},{16,8},{20,12},{24,0},{28,4},{1,25},{... | collective-permute-start | bytes 184328 | tf_op jit(solution)/shard_map/ppermute | solution.py:864
  127.0 5.1 %collective-permute-start.25 = (f16[1,1,6,1,1,40,128]{6,5,4,3,2,1,0:T(8,128)(2,1)S(1)}, f16[1,1,6,1,1,40,128]{6,5,4,3,2,1,0:T(8,128)(2,1)S(1)}, u32[]{:S(2)}, u32[]{:S(2)}) collective-permute-start(f16[1,1,6,1,1,40,128]{6,5,4,3,2,1,0:T(8,128)(2,1)S(1)} %get-tuple-element.212), channel_id=1, source_target_pairs={{0,8},{4,12},{8,0},{12,4},{16,24},{20,28},{24,16},{28,20},{1,9},{5... | collective-permute-start | bytes 184328 | tf_op jit(solution)/shard_map/ppermute | solution.py:864
  132.1 5.7 %collective-permute-start.27 = (f16[1,1,6,1,1,40,128]{6,5,4,3,2,1,0:T(8,128)(2,1)S(1)}, f16[1,1,6,1,1,40,128]{6,5,4,3,2,1,0:T(8,128)(2,1)S(1)}, u32[]{:S(2)}, u32[]{:S(2)}) collective-permute-start(f16[1,1,6,1,1,40,128]{6,5,4,3,2,1,0:T(8,128)(2,1)S(1)} %add_convert_fusion.1), channel_id=1, source_target_pairs={{0,8},{1,9},{2,10},{3,11},{4,12},{5,13},{6,14},{7,15},{8,0},{9,1},... | collective-permute-start | bytes 184328 | tf_op jit(solution)/shard_map/ppermute | solution.py:857
  132.9 5.5 %collective-permute-start.28 = (f16[1,1,6,1,1,40,128]{6,5,4,3,2,1,0:T(8,128)(2,1)S(1)}, f16[1,1,6,1,1,40,128]{6,5,4,3,2,1,0:T(8,128)(2,1)S(1)}, u32[]{:S(2)}, u32[]{:S(2)}) collective-permute-start(f16[1,1,6,1,1,40,128]{6,5,4,3,2,1,0:T(8,128)(2,1)S(1)} %add_convert_fusion.1), channel_id=1, source_target_pairs={{0,4},{1,3},{2,6},{3,1},{4,0},{5,7},{6,2},{7,5},{8,12},{9,11},{10,... | collective-permute-start | bytes 184328 | tf_op jit(solution)/shard_map/ppermute | solution.py:857
  136.3 6.7 %collective-permute-start.29 = (f16[1,1,6,1,1,40,128]{6,5,4,3,2,1,0:T(8,128)(2,1)S(1)}, f16[1,1,6,1,1,40,128]{6,5,4,3,2,1,0:T(8,128)(2,1)S(1)}, u32[]{:S(2)}, u32[]{:S(2)}) collective-permute-start(f16[1,1,6,1,1,40,128]{6,5,4,3,2,1,0:T(8,128)(2,1)S(1)} %add_convert_fusion.1), channel_id=1, source_target_pairs={{0,12},{1,11},{2,14},{3,9},{4,8},{5,15},{6,10},{7,13},{8,4},{9,3},... | collective-permute-start | bytes 184328 | tf_op jit(solution)/shard_map/ppermute | solution.py:857
  143.2 6.3 %collective-permute-start.30 = (f16[1,1,6,2,2,40,128]{6,5,4,3,2,1,0:T(8,128)(2,1)S(1)}, f16[1,1,6,2,2,40,128]{6,5,4,3,2,1,0:T(8,128)(2,1)S(1)}, u32[]{:S(2)}, u32[]{:S(2)}) collective-permute-start(f16[1,1,6,2,2,40,128]{6,5,4,3,2,1,0:T(8,128)(2,1)S(1)} %pad_maximum_fusion.1), channel_id=1, source_target_pairs={{0,2},{1,5},{2,0},{3,7},{4,6},{5,1},{6,4},{7,3},{8,10},{9,13},{10,... | collective-permute-start | bytes 737288 | tf_op jit(solution)/shard_map/ppermute | solution.py:857
  143.8 6.8 %collective-permute-start.31 = (f16[1,4,4,24,320]{4,3,2,1,0:T(8,128)(2,1)S(1)}, f16[1,4,4,24,320]{4,3,2,1,0:T(8,128)(2,1)S(1)}, u32[]{:S(2)}, u32[]{:S(2)}) collective-permute-start(f16[1,4,4,24,320]{4,3,2,1,0:T(8,128)(2,1)S(1)} %convert_element_type.100), channel_id=1, source_target_pairs={{0,16},{16,0},{1,17},{17,1},{2,18},{18,2},{3,19},{19,3},{4,20},{20... | collective-permute-start | bytes 737288 | tf_op jit(solution)/shard_map/ppermute | solution.py:961
  (16 other events, 124.1 us)

commit v6 on v5

--- a/solution.py
+++ b/solution.py
@@ -184,7 +184,8 @@
         ],
         sem,
     )
-    ready()
+    loads = ready.args[0]
+    wait_copies(loads[:2])
     tall, wide, channels = lat_ref.shape
     lanes = table_ref.shape[2]
     corners = []
@@ -199,6 +200,14 @@
             for ref in (lat_ref, reward_ref):
                 cell = widen(ref[row, col : col + 1], lanes)
                 corners += [cell[:, at : at + LANES] for at in range(0, lanes, LANES)]
+    x = lat_ref[...].reshape(tall * wide, channels)
+    sums = jnp.broadcast_to(jnp.sum(x, axis=0, keepdims=True), (8, channels))
+    mean = gather_groups(sums, group, 0) * (1.0 / (tall * wide * group))
+    gap = x - spread_groups(mean, channels, group)[0:1]
+    square = jnp.broadcast_to(jnp.sum(gap * gap, axis=0, keepdims=True), (8, channels))
+    part = jnp.concatenate([mean + gather_groups(square, group, 1)] + corners, axis=0)
+    part_ref[...] = jnp.broadcast_to(part[None], part_ref.shape)
+    wait_copies(loads[2:])
     entries = time_ref.shape[1]
     which = lax.broadcasted_iota(jnp.int32, (entries, LANES), 0)
     line = lax.broadcasted_iota(jnp.int32, (entries, LANES), 1)
@@ -211,13 +220,6 @@
     for k in range(steps):
         for i, ref in enumerate((state_ref, drift_ref, noise_coef_ref)):
             table_ref[i + 1, k : k + 1] = jnp.full((1, lanes), ref[k], F32)
-    x = lat_ref[...].reshape(tall * wide, channels)
-    sums = jnp.broadcast_to(jnp.sum(x, axis=0, keepdims=True), (8, channels))
-    mean = gather_groups(sums, group, 0) * (1.0 / (tall * wide * group))
-    gap = x - spread_groups(mean, channels, group)[0:1]
-    square = jnp.broadcast_to(jnp.sum(gap * gap, axis=0, keepdims=True), (8, channels))
-    part = jnp.concatenate([mean + gather_groups(square, group, 1)] + corners, axis=0)
-    part_ref[...] = jnp.broadcast_to(part[None], part_ref.shape)
     wait_copies(copies)
 
 

time: 155 us -> 155 us (level)
  no operation moved by 1% of the time
where the time goes in v6:
time: 155 us
  starting transfers between devices  57.3 us (37%)
  Pallas kernels  56.2 us (36%)
  waiting for transfers between devices  35.3 us (23%)
  local copies, waits for them, and re-layouts  3.08 us (2%)
    pallas_call x20, Pallas kernels, call(): pl.pallas_call(body, out_shape=shapes, in_specs=specs, out_specs=out_spec...  56.2 us
    ppermute x6, waiting for transfers between devices, send_tile(): return lambda value: lax.ppermute(value, ('sy', 'sx'), pairs)  17.9 us
    ppermute x12, starting transfers between devices, swap(): return lax.ppermute(value, axis, pairs)  17.6 us
    ppermute x12, waiting for transfers between devices, swap(): return lax.ppermute(value, axis, pairs)  8.51 us
    ppermute x6, starting transfers between devices, send_tile(): return lambda value: lax.ppermute(value, ('sy', 'sx'), pairs)  7.12 us
    all_to_all x1, starting transfers between devices, share(): return lax.all_to_all(copies, axes, 0, 0)  5.94 us
    ppermute x4, starting transfers between devices, to_slabs(): return lax.ppermute(pieces, 'tm', shifted(1))  5.75 us
    ppermute x3, waiting for transfers between devices, send_slab(): return lambda value: lax.ppermute(value, ('tm', 'sy'), pairs)  4.58 us
  transfers between devices with their start and end apart: 34, of which 17 were waited for; matrix products, arithmetic and copies ran while one was open for 0% of the time, Pallas kernels for 27%

profile of v6, /device:TPU:0, one launch (start us, length us, event | category | flops | bytes accessed | tf_op | source)
XLA Modules:
  0.0 154.6 jit_solution(396620740028519406)
XLA Ops:
  1.5 5.3 %shard_map.113 = (f32[16,32,128]{2,1,0:T(8,128)}, f32[4,4,384]{2,1,0:T(4,128)}, f32[2,24,320]{2,1,0:T(8,128)}, f32[2,24,320]{2,1,0:T(8,128)}, f32[2,16,320]{2,1,...) custom-call(s32[4]{0:T(128)} %refs_0_.1, s32[10]{0:T(128)} %stack.88.refs_1_.refs_0_, f32[4]{0:T(128)} %refs_2_.1, ...), custom_call_target="tpu_custom_call" | custom-call | flops 1000000 | bytes 4230504 | tf_op jit(solution)/shard_map/pallas_call | solution.py:766
  6.8 3.0 %collective-permute-start.4 = (f32[1,4,4,384]{3,2,1,0:T(4,128)}, f32[1,4,4,384]{3,2,1,0:T(4,128)S(1)}, u32[]{:S(2)}, u32[]{:S(2)}) collective-permute-start(f32[1,4,4,384]{3,2,1,0:T(4,128)} %bitcast.28), channel_id=1, source_target_pairs={{0,16},{16,0},{1,17},{17,1},{2,18},{18,2},{3,19},{19,3},{4,20},{20... | collective-permute-start | bytes 73736 | tf_op jit(solution)/shard_map/ppermute | solution.py:963
  9.8 5.9 %all-to-all-start = ((f32[16,32,128]{2,1,0:T(8,128)}), f32[16,32,128]{2,1,0:T(8,128)S(1)}, u32[]{:S(2)}, u32[]{:S(2)}) async-start(f32[16,32,128]{2,1,0:T(8,128)} %get-tuple-element.115), calls=%async_computation | async-start | bytes 524288 | tf_op jit(solution)/shard_map/all_to_all | solution.py:41
  16.4 3.8 %collective-permute-start = (f32[2,24,320]{2,1,0:T(8,128)}, f32[2,24,320]{2,1,0:T(8,128)S(1)}, u32[]{:S(2)}, u32[]{:S(2)}) collective-permute-start(f32[2,24,320]{2,1,0:T(8,128)} %get-tuple-element.111), channel_id=1, source_target_pairs={{0,4},{4,8},{8,12},{1,5},{5,9},{9,13},{2,6},{6,10},{10,14},{3,7},{... | collective-permute-start | bytes 184328 | tf_op jit(solution)/shard_map/ppermute | solution.py:968
  28.4 3.3 %collective-permute-done.5.refs_9_.refs_7_.refs_4_ = bf16[1,4,8,24,320]{4,3,2,1,0:T(8,128)(2,1)S(1)} collective-permute-done((bf16[1,4,8,24,320]{4,3,2,1,0:T(8,128)(2,1)}, bf16[1,4,8,24,320]{4,3,2,1,0:T(8,128)(2,1)S(1)}, u32[]{:S(2)}, u32[]{:S(2)}) %collective-permute-start.5) | collective-permute-done | bytes 491552 | tf_op jit(solution)/shard_map/ppermute | solution.py:963
  31.7 4.0 %shard_map.116 = (bf16[10,208,384]{2,1,0:T(8,128)(2,1)S(1)}, bf16[10,192,384]{2,1,0:T(8,128)(2,1)S(1)}, f32[2,2,18,384]{3,2,1,0:T(8,128)S(1)}, f32[1,192,384]{2,1,0:T(8,128)S(1)}, f32[1,192,384]{2,1,0:T(8,128)S(1)}) custom-call(f32[8]{0:T(128)S(1)} %convert_element_type.78.refs_0_, s32[10]{0:T(128)S(1)} %copy-done.4, ...), custom_call_target="tpu_custom_call" | custom-call | flops 707788800 | bytes 8515656 | tf_op jit(solution)/shard_map/pallas_call | solution.py:766
  37.1 4.6 %collective-permute-start.6 = (f32[1,192,384]{2,1,0:T(8,128)S(1)}, f32[1,192,384]{2,1,0:T(8,128)S(1)}, u32[]{:S(2)}, u32[]{:S(2)}) collective-permute-start(f32[1,192,384]{2,1,0:T(8,128)S(1)} %get-tuple-element.124.refs_2_), channel_id=1, source_target_pairs={{0,16},{16,20},{20,4},{4,8},{8,24},{24,28},{28,12},{1,17},{17,21},... | collective-permute-start | bytes 884744 | tf_op jit(solution)/shard_map/ppermute | solution.py:1005
  41.6 6.7 %shard_map.117 = (f32[8,192,384]{2,1,0:T(8,128)S(1)}, f32[2,8,128]{2,1,0:T(8,128)S(1)}, f32[8,8,384]{2,1,0:T(8,128)S(1)}, f32[8,8,384]{2,1,0:T(8,128)S(1)}) custom-call(s32[10]{0:T(128)S(1)} %copy-done.4, f32[1,192,384]{2,1,0:T(8,128)S(1)} %get-tuple-element.123.refs_1_, f32[1,192,384]{2,1,0:T(8,128)S(1)} %get-tuple-element.124.refs_2_, ...), custom_call_target="tpu_custom_call" | custom-call | flops 2831155200 | bytes 10502184 | tf_op jit(solution)/shard_map/pallas_call | solution.py:766
  51.2 3.1 %collective-permute-start.8 = (f32[2,8,128]{2,1,0:T(8,128)S(1)}, f32[2,8,128]{2,1,0:T(8,128)S(1)}, u32[]{:S(2)}, u32[]{:S(2)}) collective-permute-start(f32[2,8,128]{2,1,0:T(8,128)S(1)} %get-tuple-element.131), channel_id=1, source_target_pairs={{0,1},{1,0},{2,3},{3,2},{4,5},{5,4},{6,7},{7,6},{8,9},{9,8},{10,11... | collective-permute-start | bytes 24584 | tf_op jit(solution)/shard_map/ppermute | solution.py:32
  64.4 2.4 %collective-permute-start.13 = (f32[2,8,128]{2,1,0:T(8,128)S(1)}, f32[2,8,128]{2,1,0:T(8,128)S(1)}, u32[]{:S(2)}, u32[]{:S(2)}) collective-permute-start(f32[2,8,128]{2,1,0:T(8,128)S(1)} %pad_maximum_fusion.6), channel_id=1, source_target_pairs={{0,8},{4,12},{8,0},{12,4},{1,9},{5,13},{9,1},{13,5},{2,10},{6,14},... | collective-permute-start | bytes 24584 | tf_op jit(solution)/shard_map/ppermute | solution.py:32
  72.8 3.4 %shard_map.123 = (bf16[10,208,384]{2,1,0:T(8,128)(2,1)S(1)}, bf16[10,192,384]{2,1,0:T(8,128)(2,1)S(1)}, f32[8,192,384]{2,1,0:T(8,128)S(1)}, f32[8,128]{1,0:T(8,128)S(1)}, f32[2,8,384]{2,1,0:T(8,128)S(1)}) custom-call(f32[8]{0:T(128)S(1)} %convert_element_type.78.refs_0_, s32[10]{0:T(128)S(1)} %copy-done.4, f32[2,8,128]{2,1,0:T(8,128)S(1)} %pad_maximum_fusion.8.refs_2_, ...), custom_call_target="tpu_custom_call" | custom-call | flops 23592960 | bytes 11563080 | tf_op jit(solution)/shard_map/pallas_call | solution.py:766
  77.6 2.3 %shard_map.124.refs_9_.refs_6_ = f32[12,320,128]{2,1,0:T(8,128)S(1)} custom-call(s32[10]{0:T(128)S(1)} %copy-done.4, f32[16,24,320]{2,1,0:T(8,128)S(1)} %copy-done, f32[4,8,384]{2,1,0:T(8,128)S(1)} %shard_map.114.refs_7_.refs_5_.refs_2_.refs_1_.refs_4_, bf16[10,208,384]{2,1,0:T(8,128)(2,1)S(1)} %get-tuple-element.161.refs_3_.refs_6_, ...), custom_call_target="tpu_custom_call" | custom-call | flops 1415577600 | bytes 5578792 | tf_op jit(solution)/shard_map/pallas_call | solution.py:766
  80.0 2.3 %shard_map.125.refs_10_.refs_7_ = f32[12,320,128]{2,1,0:T(8,128)S(1)} custom-call(s32[10]{0:T(128)S(1)} %copy-done.4, f32[16,24,320]{2,1,0:T(8,128)S(1)} %copy-done, f32[4,8,384]{2,1,0:T(8,128)S(1)} %shard_map.114.refs_7_.refs_5_.refs_2_.refs_1_.refs_4_, bf16[10,208,384]{2,1,0:T(8,128)(2,1)S(1)} %get-tuple-element.161.refs_3_.refs_6_, ...), custom_call_target="tpu_custom_call" | custom-call | flops 1415577600 | bytes 5578792 | tf_op jit(solution)/shard_map/pallas_call | solution.py:766
  83.9 4.8 %shard_map.126 = (f32[4,16,24,320]{3,2,1,0:T(8,128)}, f32[1,4,4,24,320]{4,3,2,1,0:T(8,128)S(1)}) custom-call(s32[10]{0:T(128)S(1)} %copy-done.4, f32[4,8,384]{2,1,0:T(8,128)S(1)} %shard_map.114.refs_7_.refs_5_.refs_2_.refs_1_.refs_4_, f32[16,24,320]{2,1,0:T(8,128)S(1)} %copy-done.1, f32[8,192,384]{2,1,0:T(8,128)S(1)} %get-tuple-element.127.refs_9_.refs_3_.refs_1_, ...), custom_call_target="tpu_custom_call" | custom-call | flops 1415577600 | bytes 12165160 | tf_op jit(solution)/shard_map/pallas_call | solution.py:766
  93.7 2.4 %collective-permute-start.19 = (f32[8,128]{1,0:T(8,128)S(1)}, f32[8,128]{1,0:T(8,128)S(1)}, u32[]{:S(2)}, u32[]{:S(2)}) collective-permute-start(f32[8,128]{1,0:T(8,128)S(1)} %add.261), channel_id=1, source_target_pairs={{0,8},{4,12},{8,0},{12,4},{1,9},{5,13},{9,1},{13,5},{2,10},{6,14},... | collective-permute-start | bytes 12296 | tf_op jit(solution)/shard_map/ppermute | solution.py:32
  98.2 5.1 %shard_map.127 = (f32[2,12,160,128]{3,2,1,0:T(8,128)S(1)}, f32[16,128]{1,0:T(8,128)S(1)}, bf16[320,1536]{1,0:T(8,128)(2,1)S(1)}) custom-call(s32[10]{0:T(128)S(1)} %copy-done.4, f32[8,192,384]{2,1,0:T(8,128)S(1)} %get-tuple-element.127.refs_9_.refs_3_.refs_1_, f32[2,8,384]{2,1,0:T(8,128)S(1)} %get-tuple-element.157.refs_2_, f32[8,128]{1,0:T(8,128)S(1)} %add.262.refs_3_, ...), custom_call_target="tpu_custom_call" | custom-call | flops 1415577600 | bytes 1000000 | tf_op jit(solution)/shard_map/pallas_call | solution.py:766
  108.1 4.8 %shard_map.129 = (f32[4,16,24,320]{3,2,1,0:T(8,128)}, f32[1,4,4,24,320]{4,3,2,1,0:T(8,128)S(1)}) custom-call(s32[10]{0:T(128)S(1)} %copy-done.4, f32[4,8,384]{2,1,0:T(8,128)S(1)} %shard_map.114.refs_7_.refs_5_.refs_2_.refs_1_.refs_4_, f32[16,24,320]{2,1,0:T(8,128)S(1)} %copy-done.1, ...), custom_call_target="tpu_custom_call", output_to_operand_aliasing={{0}: (9, {})} | custom-call | flops 1415577600 | bytes 14131240 | tf_op jit(solution)/shard_map/pallas_call | solution.py:766
  113.0 3.4 %collective-permute-done.22 = f16[2,1,6,2,2,40,128]{6,5,4,3,2,1,0:T(8,128)(2,1)S(1)} collective-permute-done((f16[2,1,6,2,2,40,128]{6,5,4,3,2,1,0:T(8,128)(2,1)S(1)}, f16[2,1,6,2,2,40,128]{6,5,4,3,2,1,0:T(8,128)(2,1)S(1)}, u32[]{:S(2)}, u32[]{:S(2)}) %collective-permute-start.22) | collective-permute-done | bytes 491552 | tf_op jit(solution)/shard_map/ppermute | solution.py:859
  119.7 3.2 %collective-permute-done.23 = f16[2,1,6,1,2,40,128]{6,5,4,3,2,1,0:T(8,128)(2,1)S(1)} collective-permute-done((f16[2,1,6,1,2,40,128]{6,5,4,3,2,1,0:T(8,128)(2,1)S(1)}, f16[2,1,6,1,2,40,128]{6,5,4,3,2,1,0:T(8,128)(2,1)S(1)}, u32[]{:S(2)}, u32[]{:S(2)}) %collective-permute-start.23) | collective-permute-done | bytes 245792 | tf_op jit(solution)/shard_map/ppermute | solution.py:859
  123.9 3.0 %collective-permute-start.26 = (f16[1,1,6,1,1,40,128]{6,5,4,3,2,1,0:T(8,128)(2,1)S(1)}, f16[1,1,6,1,1,40,128]{6,5,4,3,2,1,0:T(8,128)(2,1)S(1)}, u32[]{:S(2)}, u32[]{:S(2)}) collective-permute-start(f16[1,1,6,1,1,40,128]{6,5,4,3,2,1,0:T(8,128)(2,1)S(1)} %get-tuple-element.211), channel_id=1, source_target_pairs={{0,24},{4,28},{8,16},{12,20},{16,8},{20,12},{24,0},{28,4},{1,25},{... | collective-permute-start | bytes 184328 | tf_op jit(solution)/shard_map/ppermute | solution.py:866
  127.7 3.5 %collective-permute-done.26 = f16[1,1,6,1,1,40,128]{6,5,4,3,2,1,0:T(8,128)(2,1)S(1)} collective-permute-done((f16[1,1,6,1,1,40,128]{6,5,4,3,2,1,0:T(8,128)(2,1)S(1)}, f16[1,1,6,1,1,40,128]{6,5,4,3,2,1,0:T(8,128)(2,1)S(1)}, u32[]{:S(2)}, u32[]{:S(2)}) %collective-permute-start.26) | collective-permute-done | bytes 61472 | tf_op jit(solution)/shard_map/ppermute | solution.py:866
  132.9 3.3 %collective-permute-start.28 = (f16[1,1,6,1,1,40,128]{6,5,4,3,2,1,0:T(8,128)(2,1)S(1)}, f16[1,1,6,1,1,40,128]{6,5,4,3,2,1,0:T(8,128)(2,1)S(1)}, u32[]{:S(2)}, u32[]{:S(2)}) collective-permute-start(f16[1,1,6,1,1,40,128]{6,5,4,3,2,1,0:T(8,128)(2,1)S(1)} %add_convert_fusion.1), channel_id=1, source_target_pairs={{0,4},{1,3},{2,6},{3,1},{4,0},{5,7},{6,2},{7,5},{8,12},{9,11},{10,... | collective-permute-start | bytes 184328 | tf_op jit(solution)/shard_map/ppermute | solution.py:859
  138.4 4.5 %collective-permute-done.29 = f16[1,1,6,1,1,40,128]{6,5,4,3,2,1,0:T(8,128)(2,1)S(1)} collective-permute-done((f16[1,1,6,1,1,40,128]{6,5,4,3,2,1,0:T(8,128)(2,1)S(1)}, f16[1,1,6,1,1,40,128]{6,5,4,3,2,1,0:T(8,128)(2,1)S(1)}, u32[]{:S(2)}, u32[]{:S(2)}) %collective-permute-start.29) | collective-permute-done | bytes 61472 | tf_op jit(solution)/shard_map/ppermute | solution.py:859
  144.6 4.8 %collective-permute-done.30 = f16[1,1,6,2,2,40,128]{6,5,4,3,2,1,0:T(8,128)(2,1)S(1)} collective-permute-done((f16[1,1,6,2,2,40,128]{6,5,4,3,2,1,0:T(8,128)(2,1)S(1)}, f16[1,1,6,2,2,40,128]{6,5,4,3,2,1,0:T(8,128)(2,1)S(1)}, u32[]{:S(2)}, u32[]{:S(2)}) %collective-permute-start.30) | collective-permute-done | bytes 245792 | tf_op jit(solution)/shard_map/ppermute | solution.py:859
  (112 shorter events, 60.0 us)
Async XLA Ops:
  6.8 9.0 %collective-permute-start.4 = (f32[1,4,4,384]{3,2,1,0:T(4,128)}, f32[1,4,4,384]{3,2,1,0:T(4,128)S(1)}, u32[]{:S(2)}, u32[]{:S(2)}) collective-permute-start(f32[1,4,4,384]{3,2,1,0:T(4,128)} %bitcast.28), channel_id=1, source_target_pairs={{0,16},{16,0},{1,17},{17,1},{2,18},{18,2},{3,19},{19,3},{4,20},{20... | collective-permute-start | bytes 73736 | tf_op jit(solution)/shard_map/ppermute | solution.py:963
  9.8 16.0 %all-to-all-start = ((f32[16,32,128]{2,1,0:T(8,128)}), f32[16,32,128]{2,1,0:T(8,128)S(1)}, u32[]{:S(2)}, u32[]{:S(2)}) async-start(f32[16,32,128]{2,1,0:T(8,128)} %get-tuple-element.115), calls=%async_computation | async-start | bytes 524288 | tf_op jit(solution)/shard_map/all_to_all | solution.py:41
  15.8 15.9 %collective-permute-start.5 = (bf16[1,4,8,24,320]{4,3,2,1,0:T(8,128)(2,1)}, bf16[1,4,8,24,320]{4,3,2,1,0:T(8,128)(2,1)S(1)}, u32[]{:S(2)}, u32[]{:S(2)}) collective-permute-start(bf16[1,4,8,24,320]{4,3,2,1,0:T(8,128)(2,1)} %get-tuple-element.120), channel_id=1, source_target_pairs={{0,16},{16,0},{1,17},{17,1},{2,18},{18,2},{3,19},{19,3},{4,20},{20... | collective-permute-start | bytes 1474568 | tf_op jit(solution)/shard_map/ppermute | solution.py:963
  16.4 12.0 %collective-permute-start = (f32[2,24,320]{2,1,0:T(8,128)}, f32[2,24,320]{2,1,0:T(8,128)S(1)}, u32[]{:S(2)}, u32[]{:S(2)}) collective-permute-start(f32[2,24,320]{2,1,0:T(8,128)} %get-tuple-element.111), channel_id=1, source_target_pairs={{0,4},{4,8},{8,12},{1,5},{5,9},{9,13},{2,6},{6,10},{10,14},{3,7},{... | collective-permute-start | bytes 184328 | tf_op jit(solution)/shard_map/ppermute | solution.py:968
  20.2 8.2 %collective-permute-start.1 = (f32[2,24,320]{2,1,0:T(8,128)}, f32[2,24,320]{2,1,0:T(8,128)S(1)}, u32[]{:S(2)}, u32[]{:S(2)}) collective-permute-start(f32[2,24,320]{2,1,0:T(8,128)} %get-tuple-element.112), channel_id=1, source_target_pairs={{4,0},{8,4},{12,8},{5,1},{9,5},{13,9},{6,2},{10,6},{14,10},{7,3},{... | collective-permute-start | bytes 184328 | tf_op jit(solution)/shard_map/ppermute | solution.py:969
  21.5 6.9 %collective-permute-start.2 = (f32[2,16,320]{2,1,0:T(8,128)}, f32[2,16,320]{2,1,0:T(8,128)S(1)}, u32[]{:S(2)}, u32[]{:S(2)}) collective-permute-start(f32[2,16,320]{2,1,0:T(8,128)} %get-tuple-element.113), channel_id=1, source_target_pairs={{0,1},{1,2},{2,3},{4,5},{5,6},{6,7},{8,9},{9,10},{10,11},{12,13},{... | collective-permute-start | bytes 122888 | tf_op jit(solution)/shard_map/ppermute | solution.py:970
  23.0 5.4 %collective-permute-start.3 = (f32[2,16,320]{2,1,0:T(8,128)}, f32[2,16,320]{2,1,0:T(8,128)S(1)}, u32[]{:S(2)}, u32[]{:S(2)}) collective-permute-start(f32[2,16,320]{2,1,0:T(8,128)} %get-tuple-element.114), channel_id=1, source_target_pairs={{1,0},{2,1},{3,2},{5,4},{6,5},{7,6},{9,8},{10,9},{11,10},{13,12},{... | collective-permute-start | bytes 122888 | tf_op jit(solution)/shard_map/ppermute | solution.py:971
  35.8 12.6 %collective-permute-start.7 = (f32[1,192,384]{2,1,0:T(8,128)S(1)}, f32[1,192,384]{2,1,0:T(8,128)S(1)}, u32[]{:S(2)}, u32[]{:S(2)}) collective-permute-start(f32[1,192,384]{2,1,0:T(8,128)S(1)} %get-tuple-element.123.refs_1_), channel_id=1, source_target_pairs={{16,0},{20,16},{4,20},{8,4},{24,8},{28,24},{12,28},{17,1},{21,17},... | collective-permute-start | bytes 884744 | tf_op jit(solution)/shard_map/ppermute | solution.py:1006
  37.1 11.3 %collective-permute-start.6 = (f32[1,192,384]{2,1,0:T(8,128)S(1)}, f32[1,192,384]{2,1,0:T(8,128)S(1)}, u32[]{:S(2)}, u32[]{:S(2)}) collective-permute-start(f32[1,192,384]{2,1,0:T(8,128)S(1)} %get-tuple-element.124.refs_2_), channel_id=1, source_target_pairs={{0,16},{16,20},{20,4},{4,8},{8,24},{24,28},{28,12},{1,17},{17,21},... | collective-permute-start | bytes 884744 | tf_op jit(solution)/shard_map/ppermute | solution.py:1005
  48.4 8.0 %collective-permute-start.9 = (f32[10,8,384]{2,1,0:T(8,128)S(1)}, f32[10,8,384]{2,1,0:T(8,128)S(1)}, u32[]{:S(2)}, u32[]{:S(2)}) collective-permute-start(f32[10,8,384]{2,1,0:T(8,128)S(1)} %get-tuple-element.136), channel_id=1, source_target_pairs={{0,1},{1,2},{2,3},{4,5},{5,6},{6,7},{8,9},{9,10},{10,11},{12,13},{... | collective-permute-start | bytes 368648 | tf_op jit(solution)/shard_map/ppermute | solution.py:1023
  49.7 6.7 %collective-permute-start.10 = (f32[10,8,384]{2,1,0:T(8,128)S(1)}, f32[10,8,384]{2,1,0:T(8,128)S(1)}, u32[]{:S(2)}, u32[]{:S(2)}) collective-permute-start(f32[10,8,384]{2,1,0:T(8,128)S(1)} %get-tuple-element.137), channel_id=1, source_target_pairs={{1,0},{2,1},{3,2},{5,4},{6,5},{7,6},{9,8},{10,9},{11,10},{13,12},{... | collective-permute-start | bytes 368648 | tf_op jit(solution)/shard_map/ppermute | solution.py:1023
  51.2 5.2 %collective-permute-start.8 = (f32[2,8,128]{2,1,0:T(8,128)S(1)}, f32[2,8,128]{2,1,0:T(8,128)S(1)}, u32[]{:S(2)}, u32[]{:S(2)}) collective-permute-start(f32[2,8,128]{2,1,0:T(8,128)S(1)} %get-tuple-element.131), channel_id=1, source_target_pairs={{0,1},{1,0},{2,3},{3,2},{4,5},{5,4},{6,7},{7,6},{8,9},{9,8},{10,11... | collective-permute-start | bytes 24584 | tf_op jit(solution)/shard_map/ppermute | solution.py:32
  82.4 6.4 %collective-permute-start.17 = (f32[8,128]{1,0:T(8,128)S(1)}, f32[8,128]{1,0:T(8,128)S(1)}, u32[]{:S(2)}, u32[]{:S(2)}) collective-permute-start(f32[8,128]{1,0:T(8,128)S(1)} %add.259), channel_id=1, source_target_pairs={{0,2},{1,3},{2,0},{3,1},{4,6},{5,7},{6,4},{7,5},{8,10},{9,11},{10,... | collective-permute-start | bytes 12296 | tf_op jit(solution)/shard_map/ppermute | solution.py:32
  88.8 14.5 %collective-permute-start.20 = (f16[1,4,4,24,320]{4,3,2,1,0:T(8,128)(2,1)S(1)}, f16[1,4,4,24,320]{4,3,2,1,0:T(8,128)(2,1)S(1)}, u32[]{:S(2)}, u32[]{:S(2)}) collective-permute-start(f16[1,4,4,24,320]{4,3,2,1,0:T(8,128)(2,1)S(1)} %convert_element_type.87), channel_id=1, source_target_pairs={{0,16},{16,0},{1,17},{17,1},{2,18},{18,2},{3,19},{19,3},{4,20},{20... | collective-permute-start | bytes 737288 | tf_op jit(solution)/shard_map/ppermute | solution.py:963
  107.5 8.9 %collective-permute-start.22 = (f16[2,1,6,2,2,40,128]{6,5,4,3,2,1,0:T(8,128)(2,1)S(1)}, f16[2,1,6,2,2,40,128]{6,5,4,3,2,1,0:T(8,128)(2,1)S(1)}, u32[]{:S(2)}, u32[]{:S(2)}) collective-permute-start(f16[2,1,6,2,2,40,128]{6,5,4,3,2,1,0:T(8,128)(2,1)S(1)} %add_convert_fusion), channel_id=1, source_target_pairs={{0,2},{1,5},{2,0},{3,7},{4,6},{5,1},{6,4},{7,3},{8,10},{9,13},{10,... | collective-permute-start | bytes 1474568 | tf_op jit(solution)/shard_map/ppermute | solution.py:859
  116.6 6.3 %collective-permute-start.23 = (f16[2,1,6,1,2,40,128]{6,5,4,3,2,1,0:T(8,128)(2,1)S(1)}, f16[2,1,6,1,2,40,128]{6,5,4,3,2,1,0:T(8,128)(2,1)S(1)}, u32[]{:S(2)}, u32[]{:S(2)}) collective-permute-start(f16[2,1,6,1,2,40,128]{6,5,4,3,2,1,0:T(8,128)(2,1)S(1)} %dynamic-slice_convert_fusion), channel_id=1, source_target_pairs={{0,4},{1,3},{2,6},{3,1},{4,0},{5,7},{6,2},{7,5},{8,12},{9,11},{10,... | collective-permute-start | bytes 737288 | tf_op jit(solution)/shard_map/ppermute | solution.py:859
  123.0 4.7 %collective-permute-start.24 = (f16[1,1,6,1,1,40,128]{6,5,4,3,2,1,0:T(8,128)(2,1)S(1)}, f16[1,1,6,1,1,40,128]{6,5,4,3,2,1,0:T(8,128)(2,1)S(1)}, u32[]{:S(2)}, u32[]{:S(2)}) collective-permute-start(f16[1,1,6,1,1,40,128]{6,5,4,3,2,1,0:T(8,128)(2,1)S(1)} %get-tuple-element.210), channel_id=1, source_target_pairs={{0,16},{4,20},{8,24},{12,28},{16,0},{20,4},{24,8},{28,12},{1,17},{... | collective-permute-start | bytes 184328 | tf_op jit(solution)/shard_map/ppermute | solution.py:866
  123.9 7.3 %collective-permute-start.26 = (f16[1,1,6,1,1,40,128]{6,5,4,3,2,1,0:T(8,128)(2,1)S(1)}, f16[1,1,6,1,1,40,128]{6,5,4,3,2,1,0:T(8,128)(2,1)S(1)}, u32[]{:S(2)}, u32[]{:S(2)}) collective-permute-start(f16[1,1,6,1,1,40,128]{6,5,4,3,2,1,0:T(8,128)(2,1)S(1)} %get-tuple-element.211), channel_id=1, source_target_pairs={{0,24},{4,28},{8,16},{12,20},{16,8},{20,12},{24,0},{28,4},{1,25},{... | collective-permute-start | bytes 184328 | tf_op jit(solution)/shard_map/ppermute | solution.py:866
  126.9 5.1 %collective-permute-start.25 = (f16[1,1,6,1,1,40,128]{6,5,4,3,2,1,0:T(8,128)(2,1)S(1)}, f16[1,1,6,1,1,40,128]{6,5,4,3,2,1,0:T(8,128)(2,1)S(1)}, u32[]{:S(2)}, u32[]{:S(2)}) collective-permute-start(f16[1,1,6,1,1,40,128]{6,5,4,3,2,1,0:T(8,128)(2,1)S(1)} %get-tuple-element.212), channel_id=1, source_target_pairs={{0,8},{4,12},{8,0},{12,4},{16,24},{20,28},{24,16},{28,20},{1,9},{5... | collective-permute-start | bytes 184328 | tf_op jit(solution)/shard_map/ppermute | solution.py:866
  132.1 5.7 %collective-permute-start.27 = (f16[1,1,6,1,1,40,128]{6,5,4,3,2,1,0:T(8,128)(2,1)S(1)}, f16[1,1,6,1,1,40,128]{6,5,4,3,2,1,0:T(8,128)(2,1)S(1)}, u32[]{:S(2)}, u32[]{:S(2)}) collective-permute-start(f16[1,1,6,1,1,40,128]{6,5,4,3,2,1,0:T(8,128)(2,1)S(1)} %add_convert_fusion.1), channel_id=1, source_target_pairs={{0,8},{1,9},{2,10},{3,11},{4,12},{5,13},{6,14},{7,15},{8,0},{9,1},... | collective-permute-start | bytes 184328 | tf_op jit(solution)/shard_map/ppermute | solution.py:859
  132.9 5.5 %collective-permute-start.28 = (f16[1,1,6,1,1,40,128]{6,5,4,3,2,1,0:T(8,128)(2,1)S(1)}, f16[1,1,6,1,1,40,128]{6,5,4,3,2,1,0:T(8,128)(2,1)S(1)}, u32[]{:S(2)}, u32[]{:S(2)}) collective-permute-start(f16[1,1,6,1,1,40,128]{6,5,4,3,2,1,0:T(8,128)(2,1)S(1)} %add_convert_fusion.1), channel_id=1, source_target_pairs={{0,4},{1,3},{2,6},{3,1},{4,0},{5,7},{6,2},{7,5},{8,12},{9,11},{10,... | collective-permute-start | bytes 184328 | tf_op jit(solution)/shard_map/ppermute | solution.py:859
  136.2 6.7 %collective-permute-start.29 = (f16[1,1,6,1,1,40,128]{6,5,4,3,2,1,0:T(8,128)(2,1)S(1)}, f16[1,1,6,1,1,40,128]{6,5,4,3,2,1,0:T(8,128)(2,1)S(1)}, u32[]{:S(2)}, u32[]{:S(2)}) collective-permute-start(f16[1,1,6,1,1,40,128]{6,5,4,3,2,1,0:T(8,128)(2,1)S(1)} %add_convert_fusion.1), channel_id=1, source_target_pairs={{0,12},{1,11},{2,14},{3,9},{4,8},{5,15},{6,10},{7,13},{8,4},{9,3},... | collective-permute-start | bytes 184328 | tf_op jit(solution)/shard_map/ppermute | solution.py:859
  143.2 6.3 %collective-permute-start.30 = (f16[1,1,6,2,2,40,128]{6,5,4,3,2,1,0:T(8,128)(2,1)S(1)}, f16[1,1,6,2,2,40,128]{6,5,4,3,2,1,0:T(8,128)(2,1)S(1)}, u32[]{:S(2)}, u32[]{:S(2)}) collective-permute-start(f16[1,1,6,2,2,40,128]{6,5,4,3,2,1,0:T(8,128)(2,1)S(1)} %pad_maximum_fusion.1), channel_id=1, source_target_pairs={{0,2},{1,5},{2,0},{3,7},{4,6},{5,1},{6,4},{7,3},{8,10},{9,13},{10,... | collective-permute-start | bytes 737288 | tf_op jit(solution)/shard_map/ppermute | solution.py:859
  143.7 6.8 %collective-permute-start.31 = (f16[1,4,4,24,320]{4,3,2,1,0:T(8,128)(2,1)S(1)}, f16[1,4,4,24,320]{4,3,2,1,0:T(8,128)(2,1)S(1)}, u32[]{:S(2)}, u32[]{:S(2)}) collective-permute-start(f16[1,4,4,24,320]{4,3,2,1,0:T(8,128)(2,1)S(1)} %convert_element_type.100), channel_id=1, source_target_pairs={{0,16},{16,0},{1,17},{17,1},{2,18},{18,2},{3,19},{19,3},{4,20},{20... | collective-permute-start | bytes 737288 | tf_op jit(solution)/shard_map/ppermute | solution.py:963
  (16 other events, 124.0 us)

commit v7 on v5

--- a/solution.py
+++ b/solution.py
@@ -933,7 +933,7 @@
     for _, bit in axis_bits(("tm",))[::-1]:
         held //= 2
         halves.append(side(bit_of("tm", bit), held))
-    cut = rows // 2
+    cut = max(1, rows // 4)
     place, flags, halves, latent_init = lax.optimization_barrier((place, flags, halves, latent_init))
 
     def shifted(offset):

time: 155 us -> 154 us (level)
  waiting for transfers between devices: 35.3 us -> 33.4 us
    ppermute x6, waiting for transfers between devices: 17.9 us -> 15.8 us  [send_tile(): return lambda value: lax.ppermute(value, ('sy', 'sx'), pairs)]
    ppermute x4, waiting for transfers between devices: 4.1 us -> 5.7 us  [to_slabs(): return lax.ppermute(pieces, 'tm', shifted(1))]
where the time goes in v7:
time: 154 us; the launch traced here: 153 us
  starting transfers between devices  57.7 us (37%)
  Pallas kernels  56.3 us (37%)
  waiting for transfers between devices  33.4 us (22%)
  local copies, waits for them, and re-layouts  3.14 us (2%)
    pallas_call x20, Pallas kernels, call(): pl.pallas_call(body, out_shape=shapes, in_specs=specs, out_specs=out_spec...  56.3 us
    ppermute x12, starting transfers between devices, swap(): return lax.ppermute(value, axis, pairs)  17.6 us
    ppermute x6, waiting for transfers between devices, send_tile(): return lambda value: lax.ppermute(value, ('sy', 'sx'), pairs)  15.8 us
    ppermute x6, starting transfers between devices, send_tile(): return lambda value: lax.ppermute(value, ('sy', 'sx'), pairs)  7.1 us
    ppermute x12, waiting for transfers between devices, swap(): return lax.ppermute(value, axis, pairs)  7.08 us
    ppermute x4, starting transfers between devices, to_slabs(): return lax.ppermute(pieces, 'tm', shifted(1))  6.11 us
    all_to_all x1, starting transfers between devices, share(): return lax.all_to_all(copies, axes, 0, 0)  5.94 us
    ppermute x4, waiting for transfers between devices, to_slabs(): return lax.ppermute(pieces, 'tm', shifted(1))  5.7 us
  transfers between devices with their start and end apart: 34, of which 17 were waited for; matrix products, arithmetic and copies ran while one was open for 0% of the time, Pallas kernels for 27%

profile of v7, /device:TPU:0, one launch (start us, length us, event | category | flops | bytes accessed | tf_op | source)
XLA Modules:
  0.0 153.4 jit_solution(7286983524807907329)
XLA Ops:
  1.5 5.3 %shard_map.113 = (f32[16,32,128]{2,1,0:T(8,128)}, f32[4,4,384]{2,1,0:T(4,128)}, f32[2,24,320]{2,1,0:T(8,128)}, f32[2,24,320]{2,1,0:T(8,128)}, f32[2,16,320]{2,1,...) custom-call(s32[4]{0:T(128)} %refs_0_.1, s32[10]{0:T(128)} %stack.88.refs_1_.refs_0_, f32[4]{0:T(128)} %refs_2_.1, ...), custom_call_target="tpu_custom_call" | custom-call | flops 1000000 | bytes 4230504 | tf_op jit(solution)/shard_map/pallas_call | solution.py:764
  6.9 3.0 %collective-permute-start.4 = (f32[1,4,4,384]{3,2,1,0:T(4,128)}, f32[1,4,4,384]{3,2,1,0:T(4,128)S(1)}, u32[]{:S(2)}, u32[]{:S(2)}) collective-permute-start(f32[1,4,4,384]{3,2,1,0:T(4,128)} %bitcast.28), channel_id=1, source_target_pairs={{0,16},{16,0},{1,17},{17,1},{2,18},{18,2},{3,19},{19,3},{4,20},{20... | collective-permute-start | bytes 73736 | tf_op jit(solution)/shard_map/ppermute | solution.py:961
  9.9 5.9 %all-to-all-start = ((f32[16,32,128]{2,1,0:T(8,128)}), f32[16,32,128]{2,1,0:T(8,128)S(1)}, u32[]{:S(2)}, u32[]{:S(2)}) async-start(f32[16,32,128]{2,1,0:T(8,128)} %get-tuple-element.115), calls=%async_computation | async-start | bytes 524288 | tf_op jit(solution)/shard_map/all_to_all | solution.py:41
  16.5 3.8 %collective-permute-start = (f32[2,24,320]{2,1,0:T(8,128)}, f32[2,24,320]{2,1,0:T(8,128)S(1)}, u32[]{:S(2)}, u32[]{:S(2)}) collective-permute-start(f32[2,24,320]{2,1,0:T(8,128)} %get-tuple-element.111), channel_id=1, source_target_pairs={{0,4},{4,8},{8,12},{1,5},{5,9},{9,13},{2,6},{6,10},{10,14},{3,7},{... | collective-permute-start | bytes 184328 | tf_op jit(solution)/shard_map/ppermute | solution.py:966
  28.5 3.3 %collective-permute-done.5.refs_9_.refs_7_.refs_4_ = bf16[1,4,8,24,320]{4,3,2,1,0:T(8,128)(2,1)S(1)} collective-permute-done((bf16[1,4,8,24,320]{4,3,2,1,0:T(8,128)(2,1)}, bf16[1,4,8,24,320]{4,3,2,1,0:T(8,128)(2,1)S(1)}, u32[]{:S(2)}, u32[]{:S(2)}) %collective-permute-start.5) | collective-permute-done | bytes 491552 | tf_op jit(solution)/shard_map/ppermute | solution.py:961
  31.8 4.0 %shard_map.116 = (bf16[10,208,384]{2,1,0:T(8,128)(2,1)S(1)}, bf16[10,192,384]{2,1,0:T(8,128)(2,1)S(1)}, f32[2,2,18,384]{3,2,1,0:T(8,128)S(1)}, f32[1,192,384]{2,1,0:T(8,128)S(1)}, f32[1,192,384]{2,1,0:T(8,128)S(1)}) custom-call(f32[8]{0:T(128)S(1)} %convert_element_type.78.refs_0_, s32[10]{0:T(128)S(1)} %copy-done.4, ...), custom_call_target="tpu_custom_call" | custom-call | flops 707788800 | bytes 8515656 | tf_op jit(solution)/shard_map/pallas_call | solution.py:764
  37.2 4.6 %collective-permute-start.6 = (f32[1,192,384]{2,1,0:T(8,128)S(1)}, f32[1,192,384]{2,1,0:T(8,128)S(1)}, u32[]{:S(2)}, u32[]{:S(2)}) collective-permute-start(f32[1,192,384]{2,1,0:T(8,128)S(1)} %get-tuple-element.124.refs_2_), channel_id=1, source_target_pairs={{0,16},{16,20},{20,4},{4,8},{8,24},{24,28},{28,12},{1,17},{17,21},... | collective-permute-start | bytes 884744 | tf_op jit(solution)/shard_map/ppermute | solution.py:1003
  41.7 6.7 %shard_map.117 = (f32[8,192,384]{2,1,0:T(8,128)S(1)}, f32[2,8,128]{2,1,0:T(8,128)S(1)}, f32[8,8,384]{2,1,0:T(8,128)S(1)}, f32[8,8,384]{2,1,0:T(8,128)S(1)}) custom-call(s32[10]{0:T(128)S(1)} %copy-done.4, f32[1,192,384]{2,1,0:T(8,128)S(1)} %get-tuple-element.123.refs_1_, f32[1,192,384]{2,1,0:T(8,128)S(1)} %get-tuple-element.124.refs_2_, ...), custom_call_target="tpu_custom_call" | custom-call | flops 2831155200 | bytes 10502184 | tf_op jit(solution)/shard_map/pallas_call | solution.py:764
  51.3 3.1 %collective-permute-start.8 = (f32[2,8,128]{2,1,0:T(8,128)S(1)}, f32[2,8,128]{2,1,0:T(8,128)S(1)}, u32[]{:S(2)}, u32[]{:S(2)}) collective-permute-start(f32[2,8,128]{2,1,0:T(8,128)S(1)} %get-tuple-element.131), channel_id=1, source_target_pairs={{0,1},{1,0},{2,3},{3,2},{4,5},{5,4},{6,7},{7,6},{8,9},{9,8},{10,11... | collective-permute-start | bytes 24584 | tf_op jit(solution)/shard_map/ppermute | solution.py:32
  64.5 2.4 %collective-permute-start.13 = (f32[2,8,128]{2,1,0:T(8,128)S(1)}, f32[2,8,128]{2,1,0:T(8,128)S(1)}, u32[]{:S(2)}, u32[]{:S(2)}) collective-permute-start(f32[2,8,128]{2,1,0:T(8,128)S(1)} %pad_maximum_fusion.6), channel_id=1, source_target_pairs={{0,8},{4,12},{8,0},{12,4},{1,9},{5,13},{9,1},{13,5},{2,10},{6,14},... | collective-permute-start | bytes 24584 | tf_op jit(solution)/shard_map/ppermute | solution.py:32
  72.9 3.4 %shard_map.123 = (bf16[10,208,384]{2,1,0:T(8,128)(2,1)S(1)}, bf16[10,192,384]{2,1,0:T(8,128)(2,1)S(1)}, f32[8,192,384]{2,1,0:T(8,128)S(1)}, f32[8,128]{1,0:T(8,128)S(1)}, f32[2,8,384]{2,1,0:T(8,128)S(1)}) custom-call(f32[8]{0:T(128)S(1)} %convert_element_type.78.refs_0_, s32[10]{0:T(128)S(1)} %copy-done.4, f32[2,8,128]{2,1,0:T(8,128)S(1)} %pad_maximum_fusion.8.refs_2_, ...), custom_call_target="tpu_custom_call" | custom-call | flops 23592960 | bytes 11563080 | tf_op jit(solution)/shard_map/pallas_call | solution.py:764
  77.7 2.3 %shard_map.124.refs_9_.refs_6_ = f32[12,320,128]{2,1,0:T(8,128)S(1)} custom-call(s32[10]{0:T(128)S(1)} %copy-done.4, f32[16,24,320]{2,1,0:T(8,128)S(1)} %copy-done, f32[4,8,384]{2,1,0:T(8,128)S(1)} %shard_map.114.refs_7_.refs_5_.refs_2_.refs_1_.refs_4_, bf16[10,208,384]{2,1,0:T(8,128)(2,1)S(1)} %get-tuple-element.161.refs_3_.refs_6_, ...), custom_call_target="tpu_custom_call" | custom-call | flops 1415577600 | bytes 5578792 | tf_op jit(solution)/shard_map/pallas_call | solution.py:764
  80.1 2.3 %shard_map.125.refs_10_.refs_7_ = f32[12,320,128]{2,1,0:T(8,128)S(1)} custom-call(s32[10]{0:T(128)S(1)} %copy-done.4, f32[16,24,320]{2,1,0:T(8,128)S(1)} %copy-done, f32[4,8,384]{2,1,0:T(8,128)S(1)} %shard_map.114.refs_7_.refs_5_.refs_2_.refs_1_.refs_4_, bf16[10,208,384]{2,1,0:T(8,128)(2,1)S(1)} %get-tuple-element.161.refs_3_.refs_6_, ...), custom_call_target="tpu_custom_call" | custom-call | flops 1415577600 | bytes 5578792 | tf_op jit(solution)/shard_map/pallas_call | solution.py:764
  84.0 3.1 %shard_map.126 = (f32[4,16,24,320]{3,2,1,0:T(8,128)}, f32[1,4,2,24,320]{4,3,2,1,0:T(8,128)S(1)}) custom-call(s32[10]{0:T(128)S(1)} %copy-done.4, f32[4,8,384]{2,1,0:T(8,128)S(1)} %shard_map.114.refs_7_.refs_5_.refs_2_.refs_1_.refs_4_, f32[16,24,320]{2,1,0:T(8,128)S(1)} %copy-done.1, f32[8,192,384]{2,1,0:T(8,128)S(1)} %get-tuple-element.127.refs_9_.refs_3_.refs_1_, ...), custom_call_target="tpu_custom_call" | custom-call | flops 1415577600 | bytes 11919400 | tf_op jit(solution)/shard_map/pallas_call | solution.py:764
  90.8 2.4 %collective-permute-start.19 = (f32[8,128]{1,0:T(8,128)S(1)}, f32[8,128]{1,0:T(8,128)S(1)}, u32[]{:S(2)}, u32[]{:S(2)}) collective-permute-start(f32[8,128]{1,0:T(8,128)S(1)} %add.261), channel_id=1, source_target_pairs={{0,8},{4,12},{8,0},{12,4},{1,9},{5,13},{9,1},{13,5},{2,10},{6,14},... | collective-permute-start | bytes 12296 | tf_op jit(solution)/shard_map/ppermute | solution.py:32
  95.3 5.1 %shard_map.127 = (f32[2,12,160,128]{3,2,1,0:T(8,128)S(1)}, f32[16,128]{1,0:T(8,128)S(1)}, bf16[320,1536]{1,0:T(8,128)(2,1)S(1)}) custom-call(s32[10]{0:T(128)S(1)} %copy-done.4, f32[8,192,384]{2,1,0:T(8,128)S(1)} %get-tuple-element.127.refs_9_.refs_3_.refs_1_, f32[2,8,384]{2,1,0:T(8,128)S(1)} %get-tuple-element.157.refs_2_, f32[8,128]{1,0:T(8,128)S(1)} %add.262.refs_3_, ...), custom_call_target="tpu_custom_call" | custom-call | flops 1415577600 | bytes 1000000 | tf_op jit(solution)/shard_map/pallas_call | solution.py:764
  105.2 6.7 %shard_map.129 = (f32[4,16,24,320]{3,2,1,0:T(8,128)}, f32[1,4,6,24,320]{4,3,2,1,0:T(8,128)S(1)}) custom-call(s32[10]{0:T(128)S(1)} %copy-done.4, f32[4,8,384]{2,1,0:T(8,128)S(1)} %shard_map.114.refs_7_.refs_5_.refs_2_.refs_1_.refs_4_, f32[16,24,320]{2,1,0:T(8,128)S(1)} %copy-done.1, ...), custom_call_target="tpu_custom_call", output_to_operand_aliasing={{0}: (9, {})} | custom-call | flops 1415577600 | bytes 14377000 | tf_op jit(solution)/shard_map/pallas_call | solution.py:764
  116.6 3.4 %collective-permute-done.23 = f16[2,1,6,1,2,40,128]{6,5,4,3,2,1,0:T(8,128)(2,1)S(1)} collective-permute-done((f16[2,1,6,1,2,40,128]{6,5,4,3,2,1,0:T(8,128)(2,1)S(1)}, f16[2,1,6,1,2,40,128]{6,5,4,3,2,1,0:T(8,128)(2,1)S(1)}, u32[]{:S(2)}, u32[]{:S(2)}) %collective-permute-start.23) | collective-permute-done | bytes 245792 | tf_op jit(solution)/shard_map/ppermute | solution.py:857
  121.4 2.7 %collective-permute-start.26 = (f16[1,1,6,1,1,40,128]{6,5,4,3,2,1,0:T(8,128)(2,1)S(1)}, f16[1,1,6,1,1,40,128]{6,5,4,3,2,1,0:T(8,128)(2,1)S(1)}, u32[]{:S(2)}, u32[]{:S(2)}) collective-permute-start(f16[1,1,6,1,1,40,128]{6,5,4,3,2,1,0:T(8,128)(2,1)S(1)} %get-tuple-element.211), channel_id=1, source_target_pairs={{0,24},{4,28},{8,16},{12,20},{16,8},{20,12},{24,0},{28,4},{1,25},{... | collective-permute-start | bytes 184328 | tf_op jit(solution)/shard_map/ppermute | solution.py:864
  125.1 3.6 %collective-permute-done.26 = f16[1,1,6,1,1,40,128]{6,5,4,3,2,1,0:T(8,128)(2,1)S(1)} collective-permute-done((f16[1,1,6,1,1,40,128]{6,5,4,3,2,1,0:T(8,128)(2,1)S(1)}, f16[1,1,6,1,1,40,128]{6,5,4,3,2,1,0:T(8,128)(2,1)S(1)}, u32[]{:S(2)}, u32[]{:S(2)}) %collective-permute-start.26) | collective-permute-done | bytes 61472 | tf_op jit(solution)/shard_map/ppermute | solution.py:864
  130.0 3.3 %collective-permute-start.28 = (f16[1,1,6,1,1,40,128]{6,5,4,3,2,1,0:T(8,128)(2,1)S(1)}, f16[1,1,6,1,1,40,128]{6,5,4,3,2,1,0:T(8,128)(2,1)S(1)}, u32[]{:S(2)}, u32[]{:S(2)}) collective-permute-start(f16[1,1,6,1,1,40,128]{6,5,4,3,2,1,0:T(8,128)(2,1)S(1)} %add_convert_fusion.1), channel_id=1, source_target_pairs={{0,4},{1,3},{2,6},{3,1},{4,0},{5,7},{6,2},{7,5},{8,12},{9,11},{10,... | collective-permute-start | bytes 184328 | tf_op jit(solution)/shard_map/ppermute | solution.py:857
  135.6 4.5 %collective-permute-done.29 = f16[1,1,6,1,1,40,128]{6,5,4,3,2,1,0:T(8,128)(2,1)S(1)} collective-permute-done((f16[1,1,6,1,1,40,128]{6,5,4,3,2,1,0:T(8,128)(2,1)S(1)}, f16[1,1,6,1,1,40,128]{6,5,4,3,2,1,0:T(8,128)(2,1)S(1)}, u32[]{:S(2)}, u32[]{:S(2)}) %collective-permute-start.29) | collective-permute-done | bytes 61472 | tf_op jit(solution)/shard_map/ppermute | solution.py:857
  142.1 4.4 %collective-permute-done.30 = f16[1,1,6,2,2,40,128]{6,5,4,3,2,1,0:T(8,128)(2,1)S(1)} collective-permute-done((f16[1,1,6,2,2,40,128]{6,5,4,3,2,1,0:T(8,128)(2,1)S(1)}, f16[1,1,6,2,2,40,128]{6,5,4,3,2,1,0:T(8,128)(2,1)S(1)}, u32[]{:S(2)}, u32[]{:S(2)}) %collective-permute-start.30) | collective-permute-done | bytes 245792 | tf_op jit(solution)/shard_map/ppermute | solution.py:857
  146.9 2.4 %collective-permute-done.31 = f16[1,4,6,24,320]{4,3,2,1,0:T(8,128)(2,1)S(1)} collective-permute-done((f16[1,4,6,24,320]{4,3,2,1,0:T(8,128)(2,1)S(1)}, f16[1,4,6,24,320]{4,3,2,1,0:T(8,128)(2,1)S(1)}, u32[]{:S(2)}, u32[]{:S(2)}) %collective-permute-start.31) | collective-permute-done | bytes 368672 | tf_op jit(solution)/shard_map/ppermute | solution.py:961
  (116 shorter events, 60.1 us)
Async XLA Ops:
  6.9 9.0 %collective-permute-start.4 = (f32[1,4,4,384]{3,2,1,0:T(4,128)}, f32[1,4,4,384]{3,2,1,0:T(4,128)S(1)}, u32[]{:S(2)}, u32[]{:S(2)}) collective-permute-start(f32[1,4,4,384]{3,2,1,0:T(4,128)} %bitcast.28), channel_id=1, source_target_pairs={{0,16},{16,0},{1,17},{17,1},{2,18},{18,2},{3,19},{19,3},{4,20},{20... | collective-permute-start | bytes 73736 | tf_op jit(solution)/shard_map/ppermute | solution.py:961
  9.9 16.0 %all-to-all-start = ((f32[16,32,128]{2,1,0:T(8,128)}), f32[16,32,128]{2,1,0:T(8,128)S(1)}, u32[]{:S(2)}, u32[]{:S(2)}) async-start(f32[16,32,128]{2,1,0:T(8,128)} %get-tuple-element.115), calls=%async_computation | async-start | bytes 524288 | tf_op jit(solution)/shard_map/all_to_all | solution.py:41
  15.9 15.9 %collective-permute-start.5 = (bf16[1,4,8,24,320]{4,3,2,1,0:T(8,128)(2,1)}, bf16[1,4,8,24,320]{4,3,2,1,0:T(8,128)(2,1)S(1)}, u32[]{:S(2)}, u32[]{:S(2)}) collective-permute-start(bf16[1,4,8,24,320]{4,3,2,1,0:T(8,128)(2,1)} %get-tuple-element.120), channel_id=1, source_target_pairs={{0,16},{16,0},{1,17},{17,1},{2,18},{18,2},{3,19},{19,3},{4,20},{20... | collective-permute-start | bytes 1474568 | tf_op jit(solution)/shard_map/ppermute | solution.py:961
  16.5 12.0 %collective-permute-start = (f32[2,24,320]{2,1,0:T(8,128)}, f32[2,24,320]{2,1,0:T(8,128)S(1)}, u32[]{:S(2)}, u32[]{:S(2)}) collective-permute-start(f32[2,24,320]{2,1,0:T(8,128)} %get-tuple-element.111), channel_id=1, source_target_pairs={{0,4},{4,8},{8,12},{1,5},{5,9},{9,13},{2,6},{6,10},{10,14},{3,7},{... | collective-permute-start | bytes 184328 | tf_op jit(solution)/shard_map/ppermute | solution.py:966
  20.3 8.2 %collective-permute-start.1 = (f32[2,24,320]{2,1,0:T(8,128)}, f32[2,24,320]{2,1,0:T(8,128)S(1)}, u32[]{:S(2)}, u32[]{:S(2)}) collective-permute-start(f32[2,24,320]{2,1,0:T(8,128)} %get-tuple-element.112), channel_id=1, source_target_pairs={{4,0},{8,4},{12,8},{5,1},{9,5},{13,9},{6,2},{10,6},{14,10},{7,3},{... | collective-permute-start | bytes 184328 | tf_op jit(solution)/shard_map/ppermute | solution.py:967
  21.6 6.9 %collective-permute-start.2 = (f32[2,16,320]{2,1,0:T(8,128)}, f32[2,16,320]{2,1,0:T(8,128)S(1)}, u32[]{:S(2)}, u32[]{:S(2)}) collective-permute-start(f32[2,16,320]{2,1,0:T(8,128)} %get-tuple-element.113), channel_id=1, source_target_pairs={{0,1},{1,2},{2,3},{4,5},{5,6},{6,7},{8,9},{9,10},{10,11},{12,13},{... | collective-permute-start | bytes 122888 | tf_op jit(solution)/shard_map/ppermute | solution.py:968
  23.1 5.4 %collective-permute-start.3 = (f32[2,16,320]{2,1,0:T(8,128)}, f32[2,16,320]{2,1,0:T(8,128)S(1)}, u32[]{:S(2)}, u32[]{:S(2)}) collective-permute-start(f32[2,16,320]{2,1,0:T(8,128)} %get-tuple-element.114), channel_id=1, source_target_pairs={{1,0},{2,1},{3,2},{5,4},{6,5},{7,6},{9,8},{10,9},{11,10},{13,12},{... | collective-permute-start | bytes 122888 | tf_op jit(solution)/shard_map/ppermute | solution.py:969
  35.9 12.6 %collective-permute-start.7 = (f32[1,192,384]{2,1,0:T(8,128)S(1)}, f32[1,192,384]{2,1,0:T(8,128)S(1)}, u32[]{:S(2)}, u32[]{:S(2)}) collective-permute-start(f32[1,192,384]{2,1,0:T(8,128)S(1)} %get-tuple-element.123.refs_1_), channel_id=1, source_target_pairs={{16,0},{20,16},{4,20},{8,4},{24,8},{28,24},{12,28},{17,1},{21,17},... | collective-permute-start | bytes 884744 | tf_op jit(solution)/shard_map/ppermute | solution.py:1004
  37.2 11.3 %collective-permute-start.6 = (f32[1,192,384]{2,1,0:T(8,128)S(1)}, f32[1,192,384]{2,1,0:T(8,128)S(1)}, u32[]{:S(2)}, u32[]{:S(2)}) collective-permute-start(f32[1,192,384]{2,1,0:T(8,128)S(1)} %get-tuple-element.124.refs_2_), channel_id=1, source_target_pairs={{0,16},{16,20},{20,4},{4,8},{8,24},{24,28},{28,12},{1,17},{17,21},... | collective-permute-start | bytes 884744 | tf_op jit(solution)/shard_map/ppermute | solution.py:1003
  48.5 8.0 %collective-permute-start.9 = (f32[10,8,384]{2,1,0:T(8,128)S(1)}, f32[10,8,384]{2,1,0:T(8,128)S(1)}, u32[]{:S(2)}, u32[]{:S(2)}) collective-permute-start(f32[10,8,384]{2,1,0:T(8,128)S(1)} %get-tuple-element.136), channel_id=1, source_target_pairs={{0,1},{1,2},{2,3},{4,5},{5,6},{6,7},{8,9},{9,10},{10,11},{12,13},{... | collective-permute-start | bytes 368648 | tf_op jit(solution)/shard_map/ppermute | solution.py:1021
  49.8 6.7 %collective-permute-start.10 = (f32[10,8,384]{2,1,0:T(8,128)S(1)}, f32[10,8,384]{2,1,0:T(8,128)S(1)}, u32[]{:S(2)}, u32[]{:S(2)}) collective-permute-start(f32[10,8,384]{2,1,0:T(8,128)S(1)} %get-tuple-element.137), channel_id=1, source_target_pairs={{1,0},{2,1},{3,2},{5,4},{6,5},{7,6},{9,8},{10,9},{11,10},{13,12},{... | collective-permute-start | bytes 368648 | tf_op jit(solution)/shard_map/ppermute | solution.py:1021
  51.3 5.2 %collective-permute-start.8 = (f32[2,8,128]{2,1,0:T(8,128)S(1)}, f32[2,8,128]{2,1,0:T(8,128)S(1)}, u32[]{:S(2)}, u32[]{:S(2)}) collective-permute-start(f32[2,8,128]{2,1,0:T(8,128)S(1)} %get-tuple-element.131), channel_id=1, source_target_pairs={{0,1},{1,0},{2,3},{3,2},{4,5},{5,4},{6,7},{7,6},{8,9},{9,8},{10,11... | collective-permute-start | bytes 24584 | tf_op jit(solution)/shard_map/ppermute | solution.py:32
  82.5 4.6 %collective-permute-start.17 = (f32[8,128]{1,0:T(8,128)S(1)}, f32[8,128]{1,0:T(8,128)S(1)}, u32[]{:S(2)}, u32[]{:S(2)}) collective-permute-start(f32[8,128]{1,0:T(8,128)S(1)} %add.259), channel_id=1, source_target_pairs={{0,2},{1,3},{2,0},{3,1},{4,6},{5,7},{6,4},{7,5},{8,10},{9,11},{10,... | collective-permute-start | bytes 12296 | tf_op jit(solution)/shard_map/ppermute | solution.py:32
  93.2 7.2 %collective-permute-start.20 = (f16[1,4,2,24,320]{4,3,2,1,0:T(8,128)(2,1)S(1)}, f16[1,4,2,24,320]{4,3,2,1,0:T(8,128)(2,1)S(1)}, u32[]{:S(2)}, u32[]{:S(2)}) collective-permute-start(f16[1,4,2,24,320]{4,3,2,1,0:T(8,128)(2,1)S(1)} %convert_element_type.87), channel_id=1, source_target_pairs={{0,16},{16,0},{1,17},{17,1},{2,18},{18,2},{3,19},{19,3},{4,20},{20... | collective-permute-start | bytes 368648 | tf_op jit(solution)/shard_map/ppermute | solution.py:961
  104.6 8.9 %collective-permute-start.22 = (f16[2,1,6,2,2,40,128]{6,5,4,3,2,1,0:T(8,128)(2,1)S(1)}, f16[2,1,6,2,2,40,128]{6,5,4,3,2,1,0:T(8,128)(2,1)S(1)}, u32[]{:S(2)}, u32[]{:S(2)}) collective-permute-start(f16[2,1,6,2,2,40,128]{6,5,4,3,2,1,0:T(8,128)(2,1)S(1)} %add_convert_fusion), channel_id=1, source_target_pairs={{0,2},{1,5},{2,0},{3,7},{4,6},{5,1},{6,4},{7,3},{8,10},{9,13},{10,... | collective-permute-start | bytes 1474568 | tf_op jit(solution)/shard_map/ppermute | solution.py:857
  113.7 6.3 %collective-permute-start.23 = (f16[2,1,6,1,2,40,128]{6,5,4,3,2,1,0:T(8,128)(2,1)S(1)}, f16[2,1,6,1,2,40,128]{6,5,4,3,2,1,0:T(8,128)(2,1)S(1)}, u32[]{:S(2)}, u32[]{:S(2)}) collective-permute-start(f16[2,1,6,1,2,40,128]{6,5,4,3,2,1,0:T(8,128)(2,1)S(1)} %dynamic-slice_convert_fusion), channel_id=1, source_target_pairs={{0,4},{1,3},{2,6},{3,1},{4,0},{5,7},{6,2},{7,5},{8,12},{9,11},{10,... | collective-permute-start | bytes 737288 | tf_op jit(solution)/shard_map/ppermute | solution.py:857
  120.1 4.9 %collective-permute-start.24 = (f16[1,1,6,1,1,40,128]{6,5,4,3,2,1,0:T(8,128)(2,1)S(1)}, f16[1,1,6,1,1,40,128]{6,5,4,3,2,1,0:T(8,128)(2,1)S(1)}, u32[]{:S(2)}, u32[]{:S(2)}) collective-permute-start(f16[1,1,6,1,1,40,128]{6,5,4,3,2,1,0:T(8,128)(2,1)S(1)} %get-tuple-element.210), channel_id=1, source_target_pairs={{0,16},{4,20},{8,24},{12,28},{16,0},{20,4},{24,8},{28,12},{1,17},{... | collective-permute-start | bytes 184328 | tf_op jit(solution)/shard_map/ppermute | solution.py:864
  121.4 7.3 %collective-permute-start.26 = (f16[1,1,6,1,1,40,128]{6,5,4,3,2,1,0:T(8,128)(2,1)S(1)}, f16[1,1,6,1,1,40,128]{6,5,4,3,2,1,0:T(8,128)(2,1)S(1)}, u32[]{:S(2)}, u32[]{:S(2)}) collective-permute-start(f16[1,1,6,1,1,40,128]{6,5,4,3,2,1,0:T(8,128)(2,1)S(1)} %get-tuple-element.211), channel_id=1, source_target_pairs={{0,24},{4,28},{8,16},{12,20},{16,8},{20,12},{24,0},{28,4},{1,25},{... | collective-permute-start | bytes 184328 | tf_op jit(solution)/shard_map/ppermute | solution.py:864
  124.0 5.1 %collective-permute-start.25 = (f16[1,1,6,1,1,40,128]{6,5,4,3,2,1,0:T(8,128)(2,1)S(1)}, f16[1,1,6,1,1,40,128]{6,5,4,3,2,1,0:T(8,128)(2,1)S(1)}, u32[]{:S(2)}, u32[]{:S(2)}) collective-permute-start(f16[1,1,6,1,1,40,128]{6,5,4,3,2,1,0:T(8,128)(2,1)S(1)} %get-tuple-element.212), channel_id=1, source_target_pairs={{0,8},{4,12},{8,0},{12,4},{16,24},{20,28},{24,16},{28,20},{1,9},{5... | collective-permute-start | bytes 184328 | tf_op jit(solution)/shard_map/ppermute | solution.py:864
  129.2 5.7 %collective-permute-start.27 = (f16[1,1,6,1,1,40,128]{6,5,4,3,2,1,0:T(8,128)(2,1)S(1)}, f16[1,1,6,1,1,40,128]{6,5,4,3,2,1,0:T(8,128)(2,1)S(1)}, u32[]{:S(2)}, u32[]{:S(2)}) collective-permute-start(f16[1,1,6,1,1,40,128]{6,5,4,3,2,1,0:T(8,128)(2,1)S(1)} %add_convert_fusion.1), channel_id=1, source_target_pairs={{0,8},{1,9},{2,10},{3,11},{4,12},{5,13},{6,14},{7,15},{8,0},{9,1},... | collective-permute-start | bytes 184328 | tf_op jit(solution)/shard_map/ppermute | solution.py:857
  130.0 5.5 %collective-permute-start.28 = (f16[1,1,6,1,1,40,128]{6,5,4,3,2,1,0:T(8,128)(2,1)S(1)}, f16[1,1,6,1,1,40,128]{6,5,4,3,2,1,0:T(8,128)(2,1)S(1)}, u32[]{:S(2)}, u32[]{:S(2)}) collective-permute-start(f16[1,1,6,1,1,40,128]{6,5,4,3,2,1,0:T(8,128)(2,1)S(1)} %add_convert_fusion.1), channel_id=1, source_target_pairs={{0,4},{1,3},{2,6},{3,1},{4,0},{5,7},{6,2},{7,5},{8,12},{9,11},{10,... | collective-permute-start | bytes 184328 | tf_op jit(solution)/shard_map/ppermute | solution.py:857
  133.4 6.7 %collective-permute-start.29 = (f16[1,1,6,1,1,40,128]{6,5,4,3,2,1,0:T(8,128)(2,1)S(1)}, f16[1,1,6,1,1,40,128]{6,5,4,3,2,1,0:T(8,128)(2,1)S(1)}, u32[]{:S(2)}, u32[]{:S(2)}) collective-permute-start(f16[1,1,6,1,1,40,128]{6,5,4,3,2,1,0:T(8,128)(2,1)S(1)} %add_convert_fusion.1), channel_id=1, source_target_pairs={{0,12},{1,11},{2,14},{3,9},{4,8},{5,15},{6,10},{7,13},{8,4},{9,3},... | collective-permute-start | bytes 184328 | tf_op jit(solution)/shard_map/ppermute | solution.py:857
  140.3 6.3 %collective-permute-start.30 = (f16[1,1,6,2,2,40,128]{6,5,4,3,2,1,0:T(8,128)(2,1)S(1)}, f16[1,1,6,2,2,40,128]{6,5,4,3,2,1,0:T(8,128)(2,1)S(1)}, u32[]{:S(2)}, u32[]{:S(2)}) collective-permute-start(f16[1,1,6,2,2,40,128]{6,5,4,3,2,1,0:T(8,128)(2,1)S(1)} %pad_maximum_fusion.1), channel_id=1, source_target_pairs={{0,2},{1,5},{2,0},{3,7},{4,6},{5,1},{6,4},{7,3},{8,10},{9,13},{10,... | collective-permute-start | bytes 737288 | tf_op jit(solution)/shard_map/ppermute | solution.py:857
  140.9 8.4 %collective-permute-start.31 = (f16[1,4,6,24,320]{4,3,2,1,0:T(8,128)(2,1)S(1)}, f16[1,4,6,24,320]{4,3,2,1,0:T(8,128)(2,1)S(1)}, u32[]{:S(2)}, u32[]{:S(2)}) collective-permute-start(f16[1,4,6,24,320]{4,3,2,1,0:T(8,128)(2,1)S(1)} %convert_element_type.100), channel_id=1, source_target_pairs={{0,16},{16,0},{1,17},{17,1},{2,18},{18,2},{3,19},{19,3},{4,20},{20... | collective-permute-start | bytes 1105928 | tf_op jit(solution)/shard_map/ppermute | solution.py:961
  (18 other events, 128.3 us)
